TPU v7x, 32 devices: a whole 2x2x4 slice. The times are simulated.
32 devices in a mesh: seq: 8 (over z, y), tp: 4 (over x, core).
Axes of the slice: x: 2, y: 2, z: 4, core: 2. Of those that a mesh axis runs over, the one named last changes fastest.
Arguments:
- stream_in: bfloat16 [1024, 2880], P('seq'), may hold values from -40 to 40
- attn_gain: float32 [2880], replicated, may hold values from 0.1 to 1.9
- w_qkv: bfloat16 [2880, 8, 640], P(None, 'tp'), may hold values from -2 to 2
- key_value_cache: bfloat16 [128, 8, 128], P(None, 'tp'), may hold values from -6 to 6
- w_out: bfloat16 [4096, 2880], P('tp'), may hold values from -0.09375 to 0.09375
- mlp_gain: float32 [2880], replicated, may hold values from 0.1 to 1.9
- expert_index: int32 [1024, 4], P(('seq', 'tp')), may hold values from 0 to 31, all different within a row; in each aligned block of 32 rows (0 to 31, 32 to 63, ...) at most 8 rows name the same one
- gate_weight: float32 [1024, 4], P(('seq', 'tp')), may hold values from 0.05 to 0.5
- w_gateup: bfloat16 [32, 2880, 2, 2880], P('seq', None, None, 'tp'), may hold values from -0.109375 to 0.109375
- w_down: bfloat16 [32, 2880, 2880], P('seq', 'tp'), may hold values from -0.109375 to 0.109375
Outputs:
- stream_out: bfloat16 [1024, 2880], P(('seq', 'tp'))
Inputs may be any that keep to these rules, and one draw needn't show every extreme that they name: `expert_index`: in the rows of one device (aligned blocks of 32 rows) no expert is named by more than 8 rows, a bound that some block reaches; a row names 4 different experts.
All inputs are finite; a program needn't handle non-finite values.
Results may differ from a plain program's by a relative error of at most 0.01.
Values may be sent and summed in bfloat16 or wider, within the bound.
No kernel may reach another device: no remote copies, remote signals or barrier semaphores. Data moves between devices by JAX's collectives and lax.ppermute only.
A program may use at most 128 MiB of HBM per device.

v0:
```python
import functools

import jax
import jax.numpy as jnp
from jax import lax
from jax.experimental import pallas as pl
from jax.experimental.pallas import tpu as pltpu
from jax.sharding import PartitionSpec as P

MODEL_WIDTH = 2880
QUERY_HEADS = 64
KEY_VALUE_HEADS = 8
HEAD_SIZE = 64
WINDOW_KEYS = 128
EXPERTS = 32
TOPK = 4


EPS = 1e-05


def from_behind(value, axis, steps):
    count = lax.axis_size(axis)
    first, last = (max(0, -steps), min(count, count - steps))
    return lax.ppermute(value, axis, [(source, source + steps) for source in range(first, last)])


def axis_plan(seq_count, tp_count):
    across = tp_count // 2
    slow = min(4, seq_count)
    quick = seq_count // slow
    x_step, quick_step, slow_step = 2, 2 * across, 2 * across * quick
    along = [(slow, slow_step, slow_step)]
    if across == quick:
        along.append((across, x_step, quick_step))
        along.append((across, quick_step, x_step))
    else:
        along.append((across, x_step, x_step))
        along.append((quick, quick_step, quick_step))
    return along


def swap(value, even_mask, odd_mask):
    count = lax.axis_size("seq") * lax.axis_size("tp")
    pairs = [
        (device, device ^ (odd_mask if device % 2 else even_mask)) for device in range(count)
    ]
    return lax.ppermute(value, ("seq", "tp"), pairs)


def spread(piece, steps):
    pieces = [piece]
    for size, even, odd in steps:
        pieces = pieces + [
            swap(held, other * even, other * odd) for other in range(1, size) for held in pieces
        ]
    return pieces


ROUTING = 64


def join_kernel(*refs):
    parts, out_ref = refs[:-1], refs[-1]
    rows = parts[0].shape[0]
    for place, part in enumerate(parts):
        out_ref[place * rows : (place + 1) * rows, :] = part[...]


def join(parts):
    rows, width = parts[0].shape
    return pl.pallas_call(
        join_kernel,
        out_shape=jax.ShapeDtypeStruct((len(parts) * rows, width), parts[0].dtype),
        cost_estimate=pl.CostEstimate(
            flops=0, bytes_accessed=4 * len(parts) * rows * width, transcendentals=0
        ),
    )(*parts)


def fold_kernel(count, *refs):
    terms, outs = refs[:count], refs[count:]
    rows = outs[0].shape[0]
    for place, out_ref in enumerate(outs):
        cut = slice(place * rows, (place + 1) * rows)
        total = terms[0][cut, :].astype(jnp.float32)
        for term in terms[1:]:
            total = total + term[cut, :].astype(jnp.float32)
        out_ref[...] = total.astype(out_ref.dtype)


def fold(terms, parts):
    rows, width = terms[0].shape
    rows = rows // parts
    kinds = [jnp.float32] + [jnp.bfloat16] * (parts - 1)
    return pl.pallas_call(
        functools.partial(fold_kernel, len(terms)),
        out_shape=[jax.ShapeDtypeStruct((rows, width), kind) for kind in kinds],
        cost_estimate=pl.CostEstimate(
            flops=len(terms) * rows * parts * width,
            bytes_accessed=4 * len(terms) * rows * parts * width,
            transcendentals=0,
        ),
    )(*terms)


def collect(kept, arrived, steps):
    terms = [kept, arrived]
    for size, even, odd in reversed(steps):
        parts = fold(terms, size)
        terms = [parts[0]] + [
            swap(parts[other], other * even, other * odd) for other in range(1, size)
        ]
    return fold(terms, 1)[0]


def expert_kernel(sizes, first_ref, *refs):
    groups, per_group, block_rows, capacity = sizes
    halves = refs[: 2 * groups]
    gate_up_ref, down_ref = refs[2 * groups : 2 * groups + 2]
    outs = refs[2 * groups + 2 : 4 * groups + 2]
    tokens_ref, gate_up_buf, down_buf, packed_ref, gate_ref, placer_ref = refs[4 * groups + 2 : -4]
    token_sem, gate_up_sem, down_sem, out_sem = refs[-4:]
    experts, _, units, width = gate_up_ref.shape
    tokens_n = per_group * block_rows
    half = tokens_n // 2
    span = per_group * capacity
    slots_n = experts * span

    def token_copy(group, side):
        return pltpu.make_async_copy(
            halves[2 * group + side],
            tokens_ref.at[group, pl.ds(side * half, half)],
            token_sem.at[group, side],
        )

    def out_copy(group, side):
        return pltpu.make_async_copy(
            tokens_ref.at[group, pl.ds(side * half, half)],
            outs[2 * group + side],
            out_sem.at[group, side],
        )

    def gate_up_copy(expert):
        return pltpu.make_async_copy(
            gate_up_ref.at[expert], gate_up_buf.at[expert % 2], gate_up_sem.at[expert % 2]
        )

    def down_copy(expert):
        return pltpu.make_async_copy(
            down_ref.at[expert], down_buf.at[expert % 2], down_sem.at[expert % 2]
        )

    for group in range(groups):
        for side in range(2):
            token_copy(group, side).start()
    gate_up_copy(0).start()
    down_copy(0).start()

    slot = lax.broadcasted_iota(jnp.int32, (slots_n, tokens_n), 0)
    token = lax.broadcasted_iota(jnp.int32, (slots_n, tokens_n), 1)
    expert_of = (slot // span + first_ref[0]).astype(jnp.float32)
    place_of = (slot % capacity).astype(jnp.float32)
    own_block = (slot // capacity) % per_group == token // block_rows
    before = lax.broadcasted_iota(jnp.int32, (tokens_n, tokens_n), 0)
    after = lax.broadcasted_iota(jnp.int32, (tokens_n, tokens_n), 1)
    earlier = (before // block_rows == after // block_rows) & (before < after)
    earlier = jnp.where(earlier, 1.0, 0.0).astype(jnp.bfloat16)
    start = width + ROUTING - 128
    for group in range(groups):
        for side in range(2):
            token_copy(group, side).wait()
        tail = tokens_ref[group, :, start : start + 128].astype(jnp.float32)
        tail = jnp.transpose(tail)[128 - ROUTING :]
        member = jnp.zeros((slots_n, tokens_n), jnp.float32)
        gate = jnp.zeros((slots_n, tokens_n), jnp.float32)
        for choice in range(TOPK):
            hit = tail[choice : choice + 1] == expert_of
            weight = (
                tail[TOPK + choice : TOPK + choice + 1]
                + tail[2 * TOPK + choice : 2 * TOPK + choice + 1]
                + tail[3 * TOPK + choice : 3 * TOPK + choice + 1]
            )
            member = member + jnp.where(hit, 1.0, 0.0)
            gate = gate + jnp.where(hit, weight, 0.0)
        rank = jnp.dot(member.astype(jnp.bfloat16), earlier, preferred_element_type=jnp.float32)
        chosen = own_block & (rank == place_of) & (member > 0.5)
        hot = jnp.where(chosen, 1.0, 0.0)
        gate = jnp.sum(jnp.where(chosen, gate, 0.0), axis=1, keepdims=True)
        placer_ref[group] = jnp.transpose(hot).astype(jnp.bfloat16)
        rows = tokens_ref[group, :, :width]
        packed = jnp.dot(hot.astype(jnp.bfloat16), rows, preferred_element_type=jnp.float32)
        packed = packed.astype(jnp.bfloat16)
        for expert in range(experts):
            place = slice(group * span, (group + 1) * span)
            packed_ref[expert, place] = packed[expert * span : (expert + 1) * span]
            gate_ref[expert, place] = jnp.broadcast_to(
                gate[expert * span : (expert + 1) * span], (span, 128)
            )

    for expert in range(experts):
        if expert + 1 < experts:
            gate_up_copy(expert + 1).start()
            down_copy(expert + 1).start()
        gate_up_copy(expert).wait()
        both = lax.dot_general(
            gate_up_buf[expert % 2].reshape(2 * units, width),
            packed_ref[expert],
            (((1,), (1,)), ((), ())),
            preferred_element_type=jnp.float32,
        )
        gate, up = both[:units], both[units:]
        scale = jnp.transpose(gate_ref[expert])[0:1]
        act = gate / (1.0 + jnp.exp(-gate)) * up * scale
        act = jnp.transpose(act).astype(jnp.bfloat16)
        down_copy(expert).wait()
        result = jnp.dot(act, down_buf[expert % 2], preferred_element_type=jnp.float32)
        packed_ref[expert] = result.astype(jnp.bfloat16)

    for group in range(groups):
        place = slice(group * span, (group + 1) * span)
        rows = jnp.concatenate([packed_ref[expert, place] for expert in range(experts)], axis=0)
        summed = jnp.dot(placer_ref[group], rows, preferred_element_type=jnp.float32)
        tokens_ref[group, :, :width] = summed.astype(jnp.bfloat16)
        for side in range(2):
            out_copy(group, side).start()
    for group in range(groups):
        for side in range(2):
            out_copy(group, side).wait()


def run_experts(first, halves, gate_up, down, block_rows, capacity):
    groups = len(halves) // 2
    half, wide = halves[0].shape
    experts, _, units, width = gate_up.shape
    per_group = 2 * half // block_rows
    slots_n = experts * per_group * capacity
    anywhere = pl.BlockSpec(memory_space=pl.ANY)
    out = jax.ShapeDtypeStruct((half, wide), jnp.bfloat16)
    return pl.pallas_call(
        functools.partial(expert_kernel, (groups, per_group, block_rows, capacity)),
        in_specs=[pl.BlockSpec(memory_space=pltpu.SMEM)] + [anywhere] * (2 * groups + 2),
        out_specs=[anywhere] * (2 * groups),
        out_shape=[out] * (2 * groups),
        scratch_shapes=[
            pltpu.VMEM((groups, 2 * half, wide), jnp.bfloat16),
            pltpu.VMEM((2, 2, units, width), jnp.bfloat16),
            pltpu.VMEM((2, units, width), jnp.bfloat16),
            pltpu.VMEM((experts, groups * per_group * capacity, width), jnp.bfloat16),
            pltpu.VMEM((experts, groups * per_group * capacity, 128), jnp.float32),
            pltpu.VMEM((groups, 2 * half, slots_n), jnp.bfloat16),
            pltpu.SemaphoreType.DMA((groups, 2)),
            pltpu.SemaphoreType.DMA((2,)),
            pltpu.SemaphoreType.DMA((2,)),
            pltpu.SemaphoreType.DMA((groups, 2)),
        ],
        compiler_params=pltpu.CompilerParams(vmem_limit_bytes=54 << 20),
        cost_estimate=pl.CostEstimate(
            flops=6 * slots_n * groups * width * units,
            bytes_accessed=6 * experts * width * units,
            transcendentals=0,
        ),
    )(first, *halves, gate_up, down)


def rms_scale(values, gain_vec):
    mean_sq = jnp.mean(values * values, axis=-1, keepdims=True)
    return values * lax.rsqrt(mean_sq + EPS) * gain_vec


def window_block(queries, key_rows, value_rows):
    scores = jnp.einsum(
        "qhgc,khc->hgqk", queries, key_rows, preferred_element_type=jnp.float32
    ) * HEAD_SIZE ** (-0.5)
    key_offset = jnp.arange(key_rows.shape[0])[None, :] - jnp.arange(queries.shape[0])[:, None]
    in_window = (key_offset >= 1) & (key_offset <= WINDOW_KEYS)
    scores = jnp.where(in_window, scores, -1e30)
    row_max = jnp.max(scores, axis=-1, keepdims=True)
    exponent = jnp.exp(scores - row_max)
    layer_weights = (exponent / jnp.sum(exponent, axis=-1, keepdims=True)).astype(jnp.bfloat16)
    attended = jnp.einsum(
        "hgqk,khc->qhgc", layer_weights, value_rows, preferred_element_type=jnp.float32
    )
    return attended.astype(jnp.bfloat16)


def local(
    stream_in,
    attn_gain,
    w_qkv,
    key_value_cache,
    w_out,
    mlp_gain,
    expert_index,
    gate_weight,
    w_gateup,
    w_down,
):
    seq_count = lax.axis_size("seq")
    tp_count = lax.axis_size("tp")
    length_local = stream_in.shape[0]
    heads_local = w_qkv.shape[1]
    query_group_width = QUERY_HEADS // KEY_VALUE_HEADS
    normed = rms_scale(stream_in.astype(jnp.float32), attn_gain).astype(jnp.bfloat16)
    projected_rows = jnp.einsum(
        "td,dhc->thc", normed, w_qkv, preferred_element_type=jnp.float32
    ).astype(jnp.bfloat16)
    projected_rows = projected_rows.reshape(
        length_local, heads_local, query_group_width + 2, HEAD_SIZE
    )
    queries = projected_rows[:, :, :query_group_width]
    kv_tail_rows = jnp.concatenate(
        [
            projected_rows[length_local - WINDOW_KEYS :, :, query_group_width],
            projected_rows[length_local - WINDOW_KEYS :, :, query_group_width + 1],
        ],
        axis=-1,
    )
    earlier = from_behind(kv_tail_rows, "seq", 1)
    at_start = lax.axis_index("seq") == 0
    earlier = jnp.where(at_start, key_value_cache, earlier)
    key_rows = jnp.concatenate(
        [earlier[:, :, :HEAD_SIZE], projected_rows[:, :, query_group_width]], axis=0
    )
    value_rows = jnp.concatenate(
        [earlier[:, :, HEAD_SIZE:], projected_rows[:, :, query_group_width + 1]], axis=0
    )
    attended = window_block(queries, key_rows, value_rows).reshape(
        length_local, heads_local * query_group_width * HEAD_SIZE
    )
    block_rows = length_local // tp_count
    plan = axis_plan(seq_count, tp_count)
    across = tp_count // 2

    terms = jnp.dot(attended, w_out, preferred_element_type=jnp.float32)
    terms = terms.reshape(across, 2, block_rows, MODEL_WIDTH)
    core = lax.axis_index("tp") % 2
    kept = lax.dynamic_index_in_dim(terms, core, 1, False)
    handed = lax.dynamic_index_in_dim(terms, 1 - core, 1, False).astype(jnp.bfloat16)
    kept = kept + swap(handed, 1, 1).astype(jnp.float32)
    place = lax.axis_index("tp") // 2
    attn_out = lax.dynamic_index_in_dim(kept, place, 0, False)
    for other in range(1, across):
        part = lax.dynamic_index_in_dim(kept, place ^ other, 0, False).astype(jnp.bfloat16)
        attn_out = attn_out + swap(part, 2 * other, 2 * other).astype(jnp.float32)
    own_start = lax.axis_index("tp") * block_rows
    residual = (
        lax.dynamic_slice_in_dim(stream_in, own_start, block_rows, 0).astype(jnp.float32) + attn_out
    )
    hidden_in = rms_scale(residual, mlp_gain).astype(jnp.bfloat16)

    experts_dev = w_gateup.shape[0]
    capacity = 2 * length_local * TOPK // (tp_count * EXPERTS)
    high = lax.reduce_precision(gate_weight, 8, 7)
    middle = lax.reduce_precision(gate_weight - high, 8, 7)
    low = lax.reduce_precision(gate_weight - high - middle, 8, 7)
    routing = jnp.concatenate([expert_index.astype(jnp.float32), high, middle, low], axis=1)
    routing = jnp.pad(routing, ((0, 0), (0, ROUTING - 4 * TOPK))).astype(jnp.bfloat16)
    rows = jnp.concatenate([hidden_in, routing], axis=1)

    (slow, slow_step, _), inner = plan[0], plan[1:]
    held = [rows] + [swap(rows, other * slow_step, other * slow_step) for other in range(1, slow)]
    mine = [join(spread(piece, inner)) for piece in held]
    halves = []
    for joined in mine:
        halves += [joined, swap(joined, 1, 1)]

    first = (lax.axis_index("seq") * experts_dev).astype(jnp.int32).reshape(1)
    weights = jnp.transpose(w_gateup, (0, 2, 3, 1))
    sums = run_experts(first, halves, weights, w_down, block_rows, capacity)

    total = residual
    for group in list(range(1, slow)) + [0]:
        kept, handed = sums[2 * group : 2 * group + 2]
        part = collect(kept, swap(handed, 1, 1), inner)
        if group:
            part = swap(part.astype(jnp.bfloat16), group * slow_step, group * slow_step)
        total = total + part[:, :MODEL_WIDTH].astype(jnp.float32)
    return total.astype(jnp.bfloat16)


def solution(mesh):
    in_specs = (
        P("seq", None),
        P(),
        P(None, "tp", None),
        P(None, "tp", None),
        P("tp", None),
        P(),
        P(("seq", "tp"), None),
        P(("seq", "tp"), None),
        P("seq", None, None, "tp"),
        P("seq", "tp", None),
    )
    out_specs = P(("seq", "tp"), None)
    return jax.shard_map(local, mesh=mesh, in_specs=in_specs, out_specs=out_specs, check_vma=False)
```

profile of v0, /device:TPU:0, one launch (start us, length us, event | category | flops | bytes accessed | tf_op | source)
XLA Modules:
  0.0 179.2 jit_solution(12707260143798052558)
XLA Ops:
  1.5 4.8 %fusion.9 = bf16[128,2,640]{2,0,1:T(8,128)(2,1)S(1)} fusion(bf16[2880,2,640]{2,1,0:T(2,128)(2,1)} %param.12, bf16[128,2880]{0,1:T(8,128)(2,1)} %param.10, f32[2880]{0:T(1024)} %param.11, f32[128]{0:T(128)S(1)} %add_rsqrt_fusion.1), kind=kOutput, calls=%fused_computation.14 | convolution fusion | flops 945356800 | bytes 8449792 | tf_op jit(solution)/shard_map/td,dhc->thc/dot_general | solution.py:305
  6.6 4.9 %collective-permute-start = (bf16[128,2,128]{0,2,1:T(8,128)(2,1)S(1)}, bf16[128,2,128]{0,2,1:T(8,128)(2,1)S(1)}, u32[]{:S(2)}, u32[]{:S(2)}) collective-permute-start(bf16[128,2,128]{0,2,1:T(8,128)(2,1)S(1)} %pad_maximum_fusion.1), channel_id=1, source_target_pairs={{0,4},{4,8},{8,12},{12,16},{16,20},{20,24},{24,28},{1,5},{5,9},{9,... | collective-permute-start | bytes 196616 | tf_op jit(solution)/shard_map/ppermute | solution.py:25
  13.4 2.1 %fusion.54 = (f32[2,8,128]{2,1,0:T(8,128)S(1)}, f32[2,8,128,256]{2,3,1,0:T(8,128)}) fusion(pred[128,256]{0,1:T(8,128)(4,1)S(1)} %fusion.32, bf16[128,2,10,64]{0,3,2,1:T(8,128)(2,1)S(1)} %bitcast.64, bf16[128,2,64]{0,2,1:T(8,128)(2,1)S(1)} %get-tuple-element.56, bf16[128,2,64]{0,2,1:T(8,128)(2,1)S(1)} %get-tuple-element.58), kind=kOutput, calls=%fused_computation.71 | convolution fusion | flops 69337344 | bytes 2465792 | tf_op jit(solution)/shard_map/sub | solution.py:279
  18.2 4.8 %fusion.3 = f32[2,2,32,2880]{3,2,1,0:T(8,128)S(1)} fusion(bf16[2,2,32,1024]{3,2,1,0:T(8,128)(2,1)S(1)} %dot_general.17, bf16[1024,2880]{0,1:T(8,128)(2,1)} %param.14), kind=kOutput, calls=%fused_computation.3 | convolution fusion | flops 754974720 | bytes 7634944 | tf_op jit(solution)/shard_map/dot_general | solution.py:335
  27.8 4.8 %collective-permute-done.2 = bf16[32,2880]{1,0:T(8,128)(2,1)S(1)} collective-permute-done((bf16[32,2880]{1,0:T(8,128)(2,1)S(1)}, bf16[32,2880]{1,0:T(8,128)(2,1)S(1)}, u32[]{:S(2)}, u32[]{:S(2)}) %collective-permute-start.2) | collective-permute-done | bytes 184352 | tf_op jit(solution)/shard_map/ppermute | solution.py:48
  33.0 3.3 %collective-permute-start.7 = (bf16[32,2944]{1,0:T(8,128)(2,1)S(1)}, bf16[32,2944]{1,0:T(8,128)(2,1)S(1)}, u32[]{:S(2)}, u32[]{:S(2)}) collective-permute-start(bf16[32,2944]{1,0:T(8,128)(2,1)S(1)} %pad_maximum_fusion.refs_0_), channel_id=1, source_target_pairs={{0,8},{1,9},{2,10},{3,11},{4,12},{5,13},{6,14},{7,15},{8,0},{9,1},... | collective-permute-start | bytes 565256 | tf_op jit(solution)/shard_map/ppermute | solution.py:48
  36.4 2.5 %collective-permute-start.17 = (bf16[32,2944]{1,0:T(8,128)(2,1)S(1)}, bf16[32,2944]{1,0:T(8,128)(2,1)S(1)}, u32[]{:S(2)}, u32[]{:S(2)}) collective-permute-start(bf16[32,2944]{1,0:T(8,128)(2,1)S(1)} %pad_maximum_fusion.refs_0_), channel_id=1, source_target_pairs={{0,24},{1,25},{2,26},{3,27},{4,28},{5,29},{6,30},{7,31},{8,16},{9,... | collective-permute-start | bytes 565256 | tf_op jit(solution)/shard_map/ppermute | solution.py:48
  43.0 5.6 %collective-permute-done.17.refs_0_ = bf16[32,2944]{1,0:T(8,128)(2,1)S(1)} collective-permute-done((bf16[32,2944]{1,0:T(8,128)(2,1)S(1)}, bf16[32,2944]{1,0:T(8,128)(2,1)S(1)}, u32[]{:S(2)}, u32[]{:S(2)}) %collective-permute-start.17) | collective-permute-done | bytes 188448 | tf_op jit(solution)/shard_map/ppermute | solution.py:48
  50.1 4.9 %collective-permute-done.12.refs_0_ = bf16[32,2944]{1,0:T(8,128)(2,1)S(1)} collective-permute-done((bf16[32,2944]{1,0:T(8,128)(2,1)S(1)}, bf16[32,2944]{1,0:T(8,128)(2,1)S(1)}, u32[]{:S(2)}, u32[]{:S(2)}) %collective-permute-start.12) | collective-permute-done | bytes 188448 | tf_op jit(solution)/shard_map/ppermute | solution.py:48
  60.6 2.1 %collective-permute-done.13.refs_1_ = bf16[32,2944]{1,0:T(8,128)(2,1)S(1)} collective-permute-done((bf16[32,2944]{1,0:T(8,128)(2,1)S(1)}, bf16[32,2944]{1,0:T(8,128)(2,1)S(1)}, u32[]{:S(2)}, u32[]{:S(2)}) %collective-permute-start.13) | collective-permute-done | bytes 188448 | tf_op jit(solution)/shard_map/ppermute | solution.py:48
  65.4 2.1 %shard_map.100.refs_0_ = bf16[128,2944]{1,0:T(8,128)(2,1)} custom-call(bf16[32,2944]{1,0:T(8,128)(2,1)} %copy-done.9, bf16[32,2944]{1,0:T(8,128)(2,1)} %copy-done.25, bf16[32,2944]{1,0:T(8,128)(2,1)} %copy-done.24, bf16[32,2944]{1,0:T(8,128)(2,1)} %copy-done.30), custom_call_target="tpu_custom_call" | custom-call | bytes 1507328 | tf_op jit(solution)/shard_map/pallas_call | solution.py:72
  68.2 2.1 %shard_map.101.refs_2_ = bf16[128,2944]{1,0:T(8,128)(2,1)} custom-call(bf16[32,2944]{1,0:T(8,128)(2,1)} %copy-done.21, bf16[32,2944]{1,0:T(8,128)(2,1)} %copy-done.23, bf16[32,2944]{1,0:T(8,128)(2,1)} %copy-done.26, bf16[32,2944]{1,0:T(8,128)(2,1)} %copy-done.29), custom_call_target="tpu_custom_call" | custom-call | bytes 1507328 | tf_op jit(solution)/shard_map/pallas_call | solution.py:72
  71.0 2.1 %shard_map.102.refs_4_ = bf16[128,2944]{1,0:T(8,128)(2,1)} custom-call(bf16[32,2944]{1,0:T(8,128)(2,1)} %copy-done.19, bf16[32,2944]{1,0:T(8,128)(2,1)} %copy-done.22, bf16[32,2944]{1,0:T(8,128)(2,1)} %copy-done.28, bf16[32,2944]{1,0:T(8,128)(2,1)} %collective-permute-done.15.refs_3_), custom_call_target="tpu_custom_call" | custom-call | bytes 1507328 | tf_op jit(solution)/shard_map/pallas_call | solution.py:72
  74.3 2.2 %shard_map.103.refs_6_ = bf16[128,2944]{1,0:T(8,128)(2,1)} custom-call(bf16[32,2944]{1,0:T(8,128)(2,1)} %copy-done.18, bf16[32,2944]{1,0:T(8,128)(2,1)} %copy-done.20, bf16[32,2944]{1,0:T(8,128)(2,1)} %copy-done.27, bf16[32,2944]{1,0:T(8,128)(2,1)} %collective-permute-done.20.refs_3_), custom_call_target="tpu_custom_call" | custom-call | bytes 1507328 | tf_op jit(solution)/shard_map/pallas_call | solution.py:72
  76.6 2.4 %collective-permute-done.21.refs_7_ = bf16[128,2944]{1,0:T(8,128)(2,1)S(1)} collective-permute-done((bf16[128,2944]{1,0:T(8,128)(2,1)}, bf16[128,2944]{1,0:T(8,128)(2,1)S(1)}, u32[]{:S(2)}, u32[]{:S(2)}) %collective-permute-start.21) | collective-permute-done | bytes 753696 | tf_op jit(solution)/shard_map/ppermute | solution.py:48
  79.8 38.6 %shard_map.104 = (bf16[128,2944]{1,0:T(8,128)(2,1)}, bf16[128,2944]{1,0:T(8,128)(2,1)}, bf16[128,2944]{1,0:T(8,128)(2,1)}, bf16[128,2944]{1,0:T(8,128)(2,1)}, bf...) custom-call(s32[1]{0:T(128)} %bitcast.16.first_ref, ...), custom_call_target="tpu_custom_call" | custom-call | flops 12740198400 | bytes 49766400 | tf_op jit(solution)/shard_map/pallas_call | solution.py:240
  121.8 2.5 %shard_map.105 = (f32[64,2944]{1,0:T(8,128)}, bf16[64,2944]{1,0:T(8,128)(2,1)}) custom-call(bf16[128,2944]{1,0:T(8,128)(2,1)} %get-tuple-element.29.refs_0_, bf16[128,2944]{1,0:T(8,128)(2,1)} %copy-done.8), custom_call_target="tpu_custom_call" | custom-call | flops 753664 | bytes 3014656 | tf_op jit(solution)/shard_map/pallas_call | solution.py:96
  126.2 2.4 %shard_map.108 = (f32[64,2944]{1,0:T(8,128)}, bf16[64,2944]{1,0:T(8,128)(2,1)}) custom-call(bf16[128,2944]{1,0:T(8,128)(2,1)} %get-tuple-element.35.refs_0_, bf16[128,2944]{1,0:T(8,128)(2,1)} %copy-done.7), custom_call_target="tpu_custom_call" | custom-call | flops 753664 | bytes 3014656 | tf_op jit(solution)/shard_map/pallas_call | solution.py:96
  130.5 2.4 %shard_map.111 = (f32[64,2944]{1,0:T(8,128)}, bf16[64,2944]{1,0:T(8,128)(2,1)}) custom-call(bf16[128,2944]{1,0:T(8,128)(2,1)} %get-tuple-element.41.refs_0_, bf16[128,2944]{1,0:T(8,128)(2,1)} %copy-done.6), custom_call_target="tpu_custom_call" | custom-call | flops 753664 | bytes 3014656 | tf_op jit(solution)/shard_map/pallas_call | solution.py:96
  134.9 2.4 %shard_map.114 = (f32[64,2944]{1,0:T(8,128)}, bf16[64,2944]{1,0:T(8,128)(2,1)}) custom-call(bf16[128,2944]{1,0:T(8,128)(2,1)} %get-tuple-element.47.refs_0_, bf16[128,2944]{1,0:T(8,128)(2,1)} %copy-done.5), custom_call_target="tpu_custom_call" | custom-call | flops 753664 | bytes 3014656 | tf_op jit(solution)/shard_map/pallas_call | solution.py:96
  139.0 2.1 %shard_map.106 = (f32[32,2944]{1,0:T(8,128)}, bf16[32,2944]{1,0:T(8,128)(2,1)}) custom-call(f32[64,2944]{1,0:T(8,128)} %get-tuple-element.31.refs_0_, bf16[64,2944]{1,0:T(8,128)(2,1)} %copy-done.13), custom_call_target="tpu_custom_call" | custom-call | flops 376832 | bytes 1507328 | tf_op jit(solution)/shard_map/pallas_call | solution.py:96
  143.1 2.1 %shard_map.109 = (f32[32,2944]{1,0:T(8,128)}, bf16[32,2944]{1,0:T(8,128)(2,1)}) custom-call(f32[64,2944]{1,0:T(8,128)} %get-tuple-element.37.refs_0_, bf16[64,2944]{1,0:T(8,128)(2,1)} %copy-done.12), custom_call_target="tpu_custom_call" | custom-call | flops 376832 | bytes 1507328 | tf_op jit(solution)/shard_map/pallas_call | solution.py:96
  146.8 2.1 %shard_map.112 = (f32[32,2944]{1,0:T(8,128)}, bf16[32,2944]{1,0:T(8,128)(2,1)}) custom-call(f32[64,2944]{1,0:T(8,128)} %get-tuple-element.43.refs_0_, bf16[64,2944]{1,0:T(8,128)(2,1)} %copy-done.10), custom_call_target="tpu_custom_call" | custom-call | flops 376832 | bytes 1507328 | tf_op jit(solution)/shard_map/pallas_call | solution.py:96
  171.2 6.1 %collective-permute-done.29 = bf16[32,2944]{1,0:T(8,128)(2,1)S(1)} collective-permute-done((bf16[32,2944]{1,0:T(8,128)(2,1)S(1)}, bf16[32,2944]{1,0:T(8,128)(2,1)S(1)}, u32[]{:S(2)}, u32[]{:S(2)}) %collective-permute-start.29) | collective-permute-done | bytes 188448 | tf_op jit(solution)/shard_map/ppermute | solution.py:48
  (172 shorter events, 67.3 us)
Async XLA Ops:
  36.4 12.3 %collective-permute-start.17 = (bf16[32,2944]{1,0:T(8,128)(2,1)S(1)}, bf16[32,2944]{1,0:T(8,128)(2,1)S(1)}, u32[]{:S(2)}, u32[]{:S(2)}) collective-permute-start(bf16[32,2944]{1,0:T(8,128)(2,1)S(1)} %pad_maximum_fusion.refs_0_), channel_id=1, source_target_pairs={{0,24},{1,25},{2,26},{3,27},{4,28},{5,29},{6,30},{7,31},{8,16},{9,... | collective-permute-start | bytes 565256 | tf_op jit(solution)/shard_map/ppermute | solution.py:48
  38.8 16.1 %collective-permute-start.12 = (bf16[32,2944]{1,0:T(8,128)(2,1)S(1)}, bf16[32,2944]{1,0:T(8,128)(2,1)S(1)}, u32[]{:S(2)}, u32[]{:S(2)}) collective-permute-start(bf16[32,2944]{1,0:T(8,128)(2,1)S(1)} %pad_maximum_fusion.refs_0_), channel_id=1, source_target_pairs={{0,16},{1,17},{2,18},{3,19},{4,20},{5,21},{6,22},{7,23},{8,24},{9,... | collective-permute-start | bytes 565256 | tf_op jit(solution)/shard_map/ppermute | solution.py:48
  39.0 17.5 %collective-permute-start.4 = (bf16[32,2944]{1,0:T(8,128)(2,1)S(1)}, bf16[32,2944]{1,0:T(8,128)(2,1)S(1)}, u32[]{:S(2)}, u32[]{:S(2)}) collective-permute-start(bf16[32,2944]{1,0:T(8,128)(2,1)S(1)} %pad_maximum_fusion.refs_0_), channel_id=1, source_target_pairs={{0,4},{1,3},{2,6},{3,1},{4,0},{5,7},{6,2},{7,5},{8,12},{9,11},{10,... | collective-permute-start | bytes 565256 | tf_op jit(solution)/shard_map/ppermute | solution.py:48
  39.6 17.5 %collective-permute-start.3 = (bf16[32,2944]{1,0:T(8,128)(2,1)S(1)}, bf16[32,2944]{1,0:T(8,128)(2,1)S(1)}, u32[]{:S(2)}, u32[]{:S(2)}) collective-permute-start(bf16[32,2944]{1,0:T(8,128)(2,1)S(1)} %pad_maximum_fusion.refs_0_), channel_id=1, source_target_pairs={{0,2},{1,5},{2,0},{3,7},{4,6},{5,1},{6,4},{7,3},{8,10},{9,13},{10,... | collective-permute-start | bytes 565256 | tf_op jit(solution)/shard_map/ppermute | solution.py:48
  41.5 17.0 %collective-permute-start.8 = (bf16[32,2944]{1,0:T(8,128)(2,1)S(1)}, bf16[32,2944]{1,0:T(8,128)(2,1)S(1)}, u32[]{:S(2)}, u32[]{:S(2)}) collective-permute-start(bf16[32,2944]{1,0:T(8,128)(2,1)S(1)} %collective-permute-done.7.refs_0_), channel_id=1, source_target_pairs={{0,2},{1,5},{2,0},{3,7},{4,6},{5,1},{6,4},{7,3},{8,10},{9,13},{10,... | collective-permute-start | bytes 565256 | tf_op jit(solution)/shard_map/ppermute | solution.py:48
  48.6 10.5 %collective-permute-start.18 = (bf16[32,2944]{1,0:T(8,128)(2,1)S(1)}, bf16[32,2944]{1,0:T(8,128)(2,1)S(1)}, u32[]{:S(2)}, u32[]{:S(2)}) collective-permute-start(bf16[32,2944]{1,0:T(8,128)(2,1)S(1)} %collective-permute-done.17.refs_0_), channel_id=1, source_target_pairs={{0,2},{1,5},{2,0},{3,7},{4,6},{5,1},{6,4},{7,3},{8,10},{9,13},{10,... | collective-permute-start | bytes 565256 | tf_op jit(solution)/shard_map/ppermute | solution.py:48
  58.5 9.0 %collective-permute-start.10 = (bf16[32,2944]{1,0:T(8,128)(2,1)S(1)}, bf16[32,2944]{1,0:T(8,128)(2,1)S(1)}, u32[]{:S(2)}, u32[]{:S(2)}) collective-permute-start(bf16[32,2944]{1,0:T(8,128)(2,1)S(1)} %collective-permute-done.8.refs_1_), channel_id=1, source_target_pairs={{0,4},{1,3},{2,6},{3,1},{4,0},{5,7},{6,2},{7,5},{8,12},{9,11},{10,... | collective-permute-start | bytes 565256 | tf_op jit(solution)/shard_map/ppermute | solution.py:48
  59.2 11.2 %collective-permute-start.14 = (bf16[32,2944]{1,0:T(8,128)(2,1)S(1)}, bf16[32,2944]{1,0:T(8,128)(2,1)S(1)}, u32[]{:S(2)}, u32[]{:S(2)}) collective-permute-start(bf16[32,2944]{1,0:T(8,128)(2,1)S(1)} %collective-permute-done.12.refs_0_), channel_id=1, source_target_pairs={{0,4},{1,3},{2,6},{3,1},{4,0},{5,7},{6,2},{7,5},{8,12},{9,11},{10,... | collective-permute-start | bytes 565256 | tf_op jit(solution)/shard_map/ppermute | solution.py:48
  63.3 9.9 %collective-permute-start.19 = (bf16[32,2944]{1,0:T(8,128)(2,1)S(1)}, bf16[32,2944]{1,0:T(8,128)(2,1)S(1)}, u32[]{:S(2)}, u32[]{:S(2)}) collective-permute-start(bf16[32,2944]{1,0:T(8,128)(2,1)S(1)} %collective-permute-done.17.refs_0_), channel_id=1, source_target_pairs={{0,4},{1,3},{2,6},{3,1},{4,0},{5,7},{6,2},{7,5},{8,12},{9,11},{10,... | collective-permute-start | bytes 565256 | tf_op jit(solution)/shard_map/ppermute | solution.py:48
  64.7 9.6 %collective-permute-start.20 = (bf16[32,2944]{1,0:T(8,128)(2,1)S(1)}, bf16[32,2944]{1,0:T(8,128)(2,1)}, u32[]{:S(2)}, u32[]{:S(2)}) collective-permute-start(bf16[32,2944]{1,0:T(8,128)(2,1)S(1)} %collective-permute-done.18.refs_1_), channel_id=1, source_target_pairs={{0,4},{1,3},{2,6},{3,1},{4,0},{5,7},{6,2},{7,5},{8,12},{9,11},{10,... | collective-permute-start | bytes 565256 | tf_op jit(solution)/shard_map/ppermute | solution.py:48
  67.5 9.0 %collective-permute-start.6 = (bf16[128,2944]{1,0:T(8,128)(2,1)}, bf16[128,2944]{1,0:T(8,128)(2,1)S(1)}, u32[]{:S(2)}, u32[]{:S(2)}) collective-permute-start(bf16[128,2944]{1,0:T(8,128)(2,1)} %shard_map.100.refs_0_), channel_id=1, source_target_pairs={{0,1},{1,0},{2,3},{3,2},{4,5},{5,4},{6,7},{7,6},{8,9},{9,8},{10,11... | collective-permute-start | bytes 2261000 | tf_op jit(solution)/shard_map/ppermute | solution.py:48
  119.0 10.6 %collective-permute-start.30 = (bf16[128,2944]{1,0:T(8,128)(2,1)}, bf16[128,2944]{1,0:T(8,128)(2,1)S(1)}, u32[]{:S(2)}, u32[]{:S(2)}) collective-permute-start(bf16[128,2944]{1,0:T(8,128)(2,1)} %get-tuple-element.42), channel_id=1, source_target_pairs={{0,1},{1,0},{2,3},{3,2},{4,5},{5,4},{6,7},{7,6},{8,9},{9,8},{10,11... | collective-permute-start | bytes 2261000 | tf_op jit(solution)/shard_map/ppermute | solution.py:48
  119.2 14.8 %collective-permute-start.34 = (bf16[128,2944]{1,0:T(8,128)(2,1)}, bf16[128,2944]{1,0:T(8,128)(2,1)S(1)}, u32[]{:S(2)}, u32[]{:S(2)}) collective-permute-start(bf16[128,2944]{1,0:T(8,128)(2,1)} %get-tuple-element.48), channel_id=1, source_target_pairs={{0,1},{1,0},{2,3},{3,2},{4,5},{5,4},{6,7},{7,6},{8,9},{9,8},{10,11... | collective-permute-start | bytes 2261000 | tf_op jit(solution)/shard_map/ppermute | solution.py:48
  124.3 14.0 %collective-permute-start.23 = (bf16[64,2944]{1,0:T(8,128)(2,1)}, bf16[64,2944]{1,0:T(8,128)(2,1)S(1)}, u32[]{:S(2)}, u32[]{:S(2)}) collective-permute-start(bf16[64,2944]{1,0:T(8,128)(2,1)} %get-tuple-element.32), channel_id=1, source_target_pairs={{0,4},{1,3},{2,6},{3,1},{4,0},{5,7},{6,2},{7,5},{8,12},{9,11},{10,... | collective-permute-start | bytes 1130504 | tf_op jit(solution)/shard_map/ppermute | solution.py:48
  128.7 13.7 %collective-permute-start.27 = (bf16[64,2944]{1,0:T(8,128)(2,1)}, bf16[64,2944]{1,0:T(8,128)(2,1)S(1)}, u32[]{:S(2)}, u32[]{:S(2)}) collective-permute-start(bf16[64,2944]{1,0:T(8,128)(2,1)} %get-tuple-element.38), channel_id=1, source_target_pairs={{0,4},{1,3},{2,6},{3,1},{4,0},{5,7},{6,2},{7,5},{8,12},{9,11},{10,... | collective-permute-start | bytes 1130504 | tf_op jit(solution)/shard_map/ppermute | solution.py:48
  132.9 13.1 %collective-permute-start.31 = (bf16[64,2944]{1,0:T(8,128)(2,1)}, bf16[64,2944]{1,0:T(8,128)(2,1)S(1)}, u32[]{:S(2)}, u32[]{:S(2)}) collective-permute-start(bf16[64,2944]{1,0:T(8,128)(2,1)} %get-tuple-element.44), channel_id=1, source_target_pairs={{0,4},{1,3},{2,6},{3,1},{4,0},{5,7},{6,2},{7,5},{8,12},{9,11},{10,... | collective-permute-start | bytes 1130504 | tf_op jit(solution)/shard_map/ppermute | solution.py:48
  137.3 12.7 %collective-permute-start.35 = (bf16[64,2944]{1,0:T(8,128)(2,1)}, bf16[64,2944]{1,0:T(8,128)(2,1)S(1)}, u32[]{:S(2)}, u32[]{:S(2)}) collective-permute-start(bf16[64,2944]{1,0:T(8,128)(2,1)} %get-tuple-element.50), channel_id=1, source_target_pairs={{0,4},{1,3},{2,6},{3,1},{4,0},{5,7},{6,2},{7,5},{8,12},{9,11},{10,... | collective-permute-start | bytes 1130504 | tf_op jit(solution)/shard_map/ppermute | solution.py:48
  141.2 12.5 %collective-permute-start.24 = (bf16[32,2944]{1,0:T(8,128)(2,1)}, bf16[32,2944]{1,0:T(8,128)(2,1)S(1)}, u32[]{:S(2)}, u32[]{:S(2)}) collective-permute-start(bf16[32,2944]{1,0:T(8,128)(2,1)} %get-tuple-element.34), channel_id=1, source_target_pairs={{0,2},{1,5},{2,0},{3,7},{4,6},{5,1},{6,4},{7,3},{8,10},{9,13},{10,... | collective-permute-start | bytes 565256 | tf_op jit(solution)/shard_map/ppermute | solution.py:48
  145.1 13.9 %collective-permute-start.28 = (bf16[32,2944]{1,0:T(8,128)(2,1)}, bf16[32,2944]{1,0:T(8,128)(2,1)S(1)}, u32[]{:S(2)}, u32[]{:S(2)}) collective-permute-start(bf16[32,2944]{1,0:T(8,128)(2,1)} %get-tuple-element.40), channel_id=1, source_target_pairs={{0,2},{1,5},{2,0},{3,7},{4,6},{5,1},{6,4},{7,3},{8,10},{9,13},{10,... | collective-permute-start | bytes 565256 | tf_op jit(solution)/shard_map/ppermute | solution.py:48
  148.8 15.2 %collective-permute-start.32 = (bf16[32,2944]{1,0:T(8,128)(2,1)}, bf16[32,2944]{1,0:T(8,128)(2,1)S(1)}, u32[]{:S(2)}, u32[]{:S(2)}) collective-permute-start(bf16[32,2944]{1,0:T(8,128)(2,1)} %get-tuple-element.46), channel_id=1, source_target_pairs={{0,2},{1,5},{2,0},{3,7},{4,6},{5,1},{6,4},{7,3},{8,10},{9,13},{10,... | collective-permute-start | bytes 565256 | tf_op jit(solution)/shard_map/ppermute | solution.py:48
  152.8 16.0 %collective-permute-start.36 = (bf16[32,2944]{1,0:T(8,128)(2,1)}, bf16[32,2944]{1,0:T(8,128)(2,1)S(1)}, u32[]{:S(2)}, u32[]{:S(2)}) collective-permute-start(bf16[32,2944]{1,0:T(8,128)(2,1)} %get-tuple-element.52), channel_id=1, source_target_pairs={{0,2},{1,5},{2,0},{3,7},{4,6},{5,1},{6,4},{7,3},{8,10},{9,13},{10,... | collective-permute-start | bytes 565256 | tf_op jit(solution)/shard_map/ppermute | solution.py:48
  157.2 14.1 %collective-permute-start.25 = (bf16[32,2944]{1,0:T(8,128)(2,1)S(1)}, bf16[32,2944]{1,0:T(8,128)(2,1)S(1)}, u32[]{:S(2)}, u32[]{:S(2)}) collective-permute-start(bf16[32,2944]{1,0:T(8,128)(2,1)S(1)} %convert_element_type.84), channel_id=1, source_target_pairs={{0,8},{1,9},{2,10},{3,11},{4,12},{5,13},{6,14},{7,15},{8,0},{9,1},... | collective-permute-start | bytes 565256 | tf_op jit(solution)/shard_map/ppermute | solution.py:48
  162.5 14.9 %collective-permute-start.29 = (bf16[32,2944]{1,0:T(8,128)(2,1)S(1)}, bf16[32,2944]{1,0:T(8,128)(2,1)S(1)}, u32[]{:S(2)}, u32[]{:S(2)}) collective-permute-start(bf16[32,2944]{1,0:T(8,128)(2,1)S(1)} %convert_element_type.86), channel_id=1, source_target_pairs={{0,16},{1,17},{2,18},{3,19},{4,20},{5,21},{6,22},{7,23},{8,24},{9,... | collective-permute-start | bytes 565256 | tf_op jit(solution)/shard_map/ppermute | solution.py:48
  167.5 9.9 %collective-permute-start.33 = (bf16[32,2944]{1,0:T(8,128)(2,1)S(1)}, bf16[32,2944]{1,0:T(8,128)(2,1)S(1)}, u32[]{:S(2)}, u32[]{:S(2)}) collective-permute-start(bf16[32,2944]{1,0:T(8,128)(2,1)S(1)} %convert_element_type.88), channel_id=1, source_target_pairs={{0,24},{1,25},{2,26},{3,27},{4,28},{5,29},{6,30},{7,31},{8,16},{9,... | collective-permute-start | bytes 565256 | tf_op jit(solution)/shard_map/ppermute | solution.py:48
  (48 other events, 283.6 us)
where the time goes:
time: 180 us; the launch traced here: 179 us
  Pallas kernels  72.6 us (40%)
  starting transfers between devices  39.4 us (22%)
  waiting for transfers between devices  32 us (18%)
  local copies, waits for them, and re-layouts  14.2 us (8%)
  matrix products  13.6 us (8%)
  other arithmetic  6.92 us (4%)
    pallas_call x1, Pallas kernels, run_experts(): pl.pallas_call(functools.partial(expert_kernel, (groups, per_group, block...  38.6 us
    ppermute x36, starting transfers between devices, swap(): return lax.ppermute(value, ('seq', 'tp'), pairs)  34.6 us
    ppermute x36, waiting for transfers between devices, swap(): return lax.ppermute(value, ('seq', 'tp'), pairs)  30.5 us
    pallas_call x12, Pallas kernels, fold(): pl.pallas_call(functools.partial(fold_kernel, len(terms)), out_shape=[jax...  25.3 us
    unnamed x73, local copies, waits for them, and re-layouts  11.9 us
    pallas_call x4, Pallas kernels, join(): pl.pallas_call(join_kernel, out_shape=jax.ShapeDtypeStruct((len(parts) *...  8.61 us
    ppermute x1, starting transfers between devices, from_behind(): lax.ppermute(value, axis, [(source, source + steps) for source in range(f...  4.87 us
    dot_general x1, matrix products, local(): jnp.einsum('td,dhc->thc', normed, w_qkv, preferred_element_type=jnp.float32)  4.8 us
  transfers between devices with their start and end apart: 37, of which 11 were waited for; matrix products, arithmetic and copies ran while one was open for 2% of the time, Pallas kernels for 19%

commit v1 on v0

--- a/solution.py
+++ b/solution.py
@@ -58,6 +58,7 @@
 
 
 ROUTING = 64
+SMALL_KERNEL = 8 << 20
 
 
 def join_kernel(*refs):
@@ -72,6 +73,7 @@
     return pl.pallas_call(
         join_kernel,
         out_shape=jax.ShapeDtypeStruct((len(parts) * rows, width), parts[0].dtype),
+        compiler_params=pltpu.CompilerParams(vmem_limit_bytes=SMALL_KERNEL),
         cost_estimate=pl.CostEstimate(
             flops=0, bytes_accessed=4 * len(parts) * rows * width, transcendentals=0
         ),
@@ -89,13 +91,14 @@
         out_ref[...] = total.astype(out_ref.dtype)
 
 
-def fold(terms, parts):
+def fold(terms, parts, first=jnp.float32):
     rows, width = terms[0].shape
     rows = rows // parts
-    kinds = [jnp.float32] + [jnp.bfloat16] * (parts - 1)
+    kinds = [first] + [jnp.bfloat16] * (parts - 1)
     return pl.pallas_call(
         functools.partial(fold_kernel, len(terms)),
         out_shape=[jax.ShapeDtypeStruct((rows, width), kind) for kind in kinds],
+        compiler_params=pltpu.CompilerParams(vmem_limit_bytes=SMALL_KERNEL),
         cost_estimate=pl.CostEstimate(
             flops=len(terms) * rows * parts * width,
             bytes_accessed=4 * len(terms) * rows * parts * width,
@@ -104,42 +107,34 @@
     )(*terms)
 
 
-def collect(kept, arrived, steps):
+def collect(kept, arrived, steps, last, first):
     terms = [kept, arrived]
     for size, even, odd in reversed(steps):
         parts = fold(terms, size)
         terms = [parts[0]] + [
             swap(parts[other], other * even, other * odd) for other in range(1, size)
         ]
-    return fold(terms, 1)[0]
+    return fold(terms, last, first)
 
 
 def expert_kernel(sizes, first_ref, *refs):
-    groups, per_group, block_rows, capacity = sizes
-    halves = refs[: 2 * groups]
-    gate_up_ref, down_ref = refs[2 * groups : 2 * groups + 2]
-    outs = refs[2 * groups + 2 : 4 * groups + 2]
-    tokens_ref, gate_up_buf, down_buf, packed_ref, gate_ref, placer_ref = refs[4 * groups + 2 : -4]
+    groups, block_rows, capacity = sizes
+    ins = refs[:groups]
+    gate_up_ref, down_ref = refs[groups : groups + 2]
+    outs = refs[groups + 2 : 2 * groups + 2]
+    tokens_ref, gate_up_buf, down_buf, packed_ref, gate_ref, placer_ref = refs[2 * groups + 2 : -4]
     token_sem, gate_up_sem, down_sem, out_sem = refs[-4:]
     experts, _, units, width = gate_up_ref.shape
-    tokens_n = per_group * block_rows
-    half = tokens_n // 2
+    tokens_n = ins[0].shape[0]
+    per_group = tokens_n // block_rows
     span = per_group * capacity
     slots_n = experts * span
 
-    def token_copy(group, side):
-        return pltpu.make_async_copy(
-            halves[2 * group + side],
-            tokens_ref.at[group, pl.ds(side * half, half)],
-            token_sem.at[group, side],
-        )
-
-    def out_copy(group, side):
-        return pltpu.make_async_copy(
-            tokens_ref.at[group, pl.ds(side * half, half)],
-            outs[2 * group + side],
-            out_sem.at[group, side],
-        )
+    def token_copy(group):
+        return pltpu.make_async_copy(ins[group], tokens_ref.at[group], token_sem.at[group])
+
+    def out_copy(group):
+        return pltpu.make_async_copy(tokens_ref.at[group], outs[group], out_sem.at[group])
 
     def gate_up_copy(expert):
         return pltpu.make_async_copy(
@@ -152,8 +147,7 @@
         )
 
     for group in range(groups):
-        for side in range(2):
-            token_copy(group, side).start()
+        token_copy(group).start()
     gate_up_copy(0).start()
     down_copy(0).start()
 
@@ -168,8 +162,7 @@
     earlier = jnp.where(earlier, 1.0, 0.0).astype(jnp.bfloat16)
     start = width + ROUTING - 128
     for group in range(groups):
-        for side in range(2):
-            token_copy(group, side).wait()
+        token_copy(group).wait()
         tail = tokens_ref[group, :, start : start + 128].astype(jnp.float32)
         tail = jnp.transpose(tail)[128 - ROUTING :]
         member = jnp.zeros((slots_n, tokens_n), jnp.float32)
@@ -198,23 +191,24 @@
                 gate[expert * span : (expert + 1) * span], (span, 128)
             )
 
+    contract = (((1,), (1,)), ((), ()))
     for expert in range(experts):
+        held = expert % 2
         if expert + 1 < experts:
             gate_up_copy(expert + 1).start()
             down_copy(expert + 1).start()
         gate_up_copy(expert).wait()
-        both = lax.dot_general(
-            gate_up_buf[expert % 2].reshape(2 * units, width),
-            packed_ref[expert],
-            (((1,), (1,)), ((), ())),
-            preferred_element_type=jnp.float32,
+        rows = packed_ref[expert]
+        gate = lax.dot_general(
+            rows, gate_up_buf[held, 0], contract, preferred_element_type=jnp.float32
         )
-        gate, up = both[:units], both[units:]
-        scale = jnp.transpose(gate_ref[expert])[0:1]
-        act = gate / (1.0 + jnp.exp(-gate)) * up * scale
-        act = jnp.transpose(act).astype(jnp.bfloat16)
+        up = lax.dot_general(
+            rows, gate_up_buf[held, 1], contract, preferred_element_type=jnp.float32
+        )
+        act = gate / (1.0 + jnp.exp(-gate)) * up * gate_ref[expert][:, :1]
+        act = act.astype(jnp.bfloat16)
         down_copy(expert).wait()
-        result = jnp.dot(act, down_buf[expert % 2], preferred_element_type=jnp.float32)
+        result = jnp.dot(act, down_buf[held], preferred_element_type=jnp.float32)
         packed_ref[expert] = result.astype(jnp.bfloat16)
 
     for group in range(groups):
@@ -222,45 +216,42 @@
         rows = jnp.concatenate([packed_ref[expert, place] for expert in range(experts)], axis=0)
         summed = jnp.dot(placer_ref[group], rows, preferred_element_type=jnp.float32)
         tokens_ref[group, :, :width] = summed.astype(jnp.bfloat16)
-        for side in range(2):
-            out_copy(group, side).start()
+        out_copy(group).start()
     for group in range(groups):
-        for side in range(2):
-            out_copy(group, side).wait()
-
-
-def run_experts(first, halves, gate_up, down, block_rows, capacity):
-    groups = len(halves) // 2
-    half, wide = halves[0].shape
+        out_copy(group).wait()
+
+
+def run_experts(first, tokens, gate_up, down, block_rows, capacity):
+    groups = len(tokens)
+    tokens_n, wide = tokens[0].shape
     experts, _, units, width = gate_up.shape
-    per_group = 2 * half // block_rows
-    slots_n = experts * per_group * capacity
+    span = tokens_n // block_rows * capacity
+    slots_n = experts * span
     anywhere = pl.BlockSpec(memory_space=pl.ANY)
-    out = jax.ShapeDtypeStruct((half, wide), jnp.bfloat16)
     return pl.pallas_call(
-        functools.partial(expert_kernel, (groups, per_group, block_rows, capacity)),
-        in_specs=[pl.BlockSpec(memory_space=pltpu.SMEM)] + [anywhere] * (2 * groups + 2),
-        out_specs=[anywhere] * (2 * groups),
-        out_shape=[out] * (2 * groups),
+        functools.partial(expert_kernel, (groups, block_rows, capacity)),
+        in_specs=[pl.BlockSpec(memory_space=pltpu.SMEM)] + [anywhere] * (groups + 2),
+        out_specs=[anywhere] * groups,
+        out_shape=[jax.ShapeDtypeStruct((tokens_n, wide), jnp.bfloat16)] * groups,
         scratch_shapes=[
-            pltpu.VMEM((groups, 2 * half, wide), jnp.bfloat16),
+            pltpu.VMEM((groups, tokens_n, wide), jnp.bfloat16),
             pltpu.VMEM((2, 2, units, width), jnp.bfloat16),
             pltpu.VMEM((2, units, width), jnp.bfloat16),
-            pltpu.VMEM((experts, groups * per_group * capacity, width), jnp.bfloat16),
-            pltpu.VMEM((experts, groups * per_group * capacity, 128), jnp.float32),
-            pltpu.VMEM((groups, 2 * half, slots_n), jnp.bfloat16),
-            pltpu.SemaphoreType.DMA((groups, 2)),
+            pltpu.VMEM((experts, groups * span, width), jnp.bfloat16),
+            pltpu.VMEM((experts, groups * span, 128), jnp.float32),
+            pltpu.VMEM((groups, tokens_n, slots_n), jnp.bfloat16),
+            pltpu.SemaphoreType.DMA((groups,)),
             pltpu.SemaphoreType.DMA((2,)),
             pltpu.SemaphoreType.DMA((2,)),
-            pltpu.SemaphoreType.DMA((groups, 2)),
+            pltpu.SemaphoreType.DMA((groups,)),
         ],
-        compiler_params=pltpu.CompilerParams(vmem_limit_bytes=54 << 20),
+        compiler_params=pltpu.CompilerParams(vmem_limit_bytes=52 << 20),
         cost_estimate=pl.CostEstimate(
             flops=6 * slots_n * groups * width * units,
             bytes_accessed=6 * experts * width * units,
             transcendentals=0,
         ),
-    )(first, *halves, gate_up, down)
+    )(first, *tokens, gate_up, down)
 
 
 def rms_scale(values, gain_vec):
@@ -360,21 +351,21 @@
 
     (slow, slow_step, _), inner = plan[0], plan[1:]
     held = [rows] + [swap(rows, other * slow_step, other * slow_step) for other in range(1, slow)]
-    mine = [join(spread(piece, inner)) for piece in held]
-    halves = []
-    for joined in mine:
-        halves += [joined, swap(joined, 1, 1)]
+    near, far = held[: slow // 2], held[slow // 2 :]
+    near, far = [join(spread(join(pieces), inner)) for pieces in (near, far)]
+    tokens = [near, swap(near, 1, 1), far, swap(far, 1, 1)]
 
     first = (lax.axis_index("seq") * experts_dev).astype(jnp.int32).reshape(1)
     weights = jnp.transpose(w_gateup, (0, 2, 3, 1))
-    sums = run_experts(first, halves, weights, w_down, block_rows, capacity)
-
-    total = residual
-    for group in list(range(1, slow)) + [0]:
-        kept, handed = sums[2 * group : 2 * group + 2]
-        part = collect(kept, swap(handed, 1, 1), inner)
-        if group:
-            part = swap(part.astype(jnp.bfloat16), group * slow_step, group * slow_step)
+    near, near_handed, far, far_handed = run_experts(
+        first, tokens, weights, w_down, block_rows, capacity
+    )
+
+    far = collect(far, swap(far_handed, 1, 1), inner, slow // 2, jnp.bfloat16)
+    near = collect(near, swap(near_handed, 1, 1), inner, slow // 2, jnp.float32)
+    total = residual + near[0][:, :MODEL_WIDTH]
+    for other, part in enumerate(near[1:] + far, 1):
+        part = swap(part, other * slow_step, other * slow_step)
         total = total + part[:, :MODEL_WIDTH].astype(jnp.float32)
     return total.astype(jnp.bfloat16)
 

time: 180 us -> 162 us (0.900)
  waiting for transfers between devices: 32 us -> 87.9 us
  Pallas kernels: 72.6 us -> 26.4 us
  starting transfers between devices: 39.4 us -> 25.9 us
  local copies, waits for them, and re-layouts: 14.2 us -> 2.81 us
  other arithmetic: 6.92 us -> 2.91 us
    ppermute x36 -> x22, waiting for transfers between devices: 30.5 us -> 86.4 us  [swap(): return lax.ppermute(value, ('seq', 'tp'), pairs)]
    pallas_call x12 -> x6, Pallas kernels: 25.3 us -> 1.05 us  [fold(): pl.pallas_call(functools.partial(fold_kernel, len(terms)), out_shape=[jax...]
    ppermute x36 -> x22, starting transfers between devices: 34.6 us -> 21 us  [swap(): return lax.ppermute(value, ('seq', 'tp'), pairs)]
    pallas_call x1, Pallas kernels: 38.6 us -> 25.1 us  [run_experts(): pl.pallas_call(functools.partial(expert_kernel, (groups, block_rows, capa...]
    unnamed x73 -> x19, local copies, waits for them, and re-layouts: 11.9 us -> 0.52 us
    pallas_call x4, Pallas kernels: 8.61 us -> 0.26 us  [join(): pl.pallas_call(join_kernel, out_shape=jax.ShapeDtypeStruct((len(parts) *...]
    convert_element_type x3 -> x0, other arithmetic: 3.03 us -> none  [local(): part = swap(part.astype(jnp.bfloat16), group * slow_step, group * slow_step)]
  transfers between devices with their start and end apart: 37 -> 23, of which waited for: 11 -> 16; matrix products, arithmetic and copies ran while one was open for 2% -> 1% of each run, Pallas kernels for 19% -> 1%
where the time goes in v1:
time: 162 us; the launch traced here: 160 us
  waiting for transfers between devices  87.9 us (54%)
  Pallas kernels  26.4 us (16%)
  starting transfers between devices  25.9 us (16%)
  matrix products  13.6 us (8%)
  other arithmetic  2.91 us (2%)
  local copies, waits for them, and re-layouts  2.81 us (2%)
    ppermute x22, waiting for transfers between devices, swap(): return lax.ppermute(value, ('seq', 'tp'), pairs)  86.4 us
    pallas_call x1, Pallas kernels, run_experts(): pl.pallas_call(functools.partial(expert_kernel, (groups, block_rows, capa...  25.1 us
    ppermute x22, starting transfers between devices, swap(): return lax.ppermute(value, ('seq', 'tp'), pairs)  21 us
    ppermute x1, starting transfers between devices, from_behind(): lax.ppermute(value, axis, [(source, source + steps) for source in range(f...  4.87 us
    dot_general x1, matrix products, local(): jnp.einsum('td,dhc->thc', normed, w_qkv, preferred_element_type=jnp.float32)  4.79 us
    dot_general x1, matrix products, local(): terms = jnp.dot(attended, w_out, preferred_element_type=jnp.float32)  4.78 us
  transfers between devices with their start and end apart: 23, of which 16 were waited for; matrix products, arithmetic and copies ran while one was open for 1% of the time, Pallas kernels for 1%

profile of v1, /device:TPU:0, one launch (start us, length us, event | category | flops | bytes accessed | tf_op | source)
XLA Modules:
  0.0 159.8 jit_solution(5289772648699866050)
XLA Ops:
  1.5 4.8 %fusion.9 = bf16[128,2,640]{2,0,1:T(8,128)(2,1)S(1)} fusion(bf16[2880,2,640]{2,1,0:T(2,128)(2,1)} %param.12, bf16[128,2880]{0,1:T(8,128)(2,1)} %param.10, f32[2880]{0:T(1024)} %param.11, f32[128]{0:T(128)S(1)} %add_rsqrt_fusion.1), kind=kOutput, calls=%fused_computation.14 | convolution fusion | flops 945356800 | bytes 8449792 | tf_op jit(solution)/shard_map/td,dhc->thc/dot_general | solution.py:296
  6.6 4.9 %collective-permute-start = (bf16[128,2,128]{0,2,1:T(8,128)(2,1)S(1)}, bf16[128,2,128]{0,2,1:T(8,128)(2,1)S(1)}, u32[]{:S(2)}, u32[]{:S(2)}) collective-permute-start(bf16[128,2,128]{0,2,1:T(8,128)(2,1)S(1)} %pad_maximum_fusion.1), channel_id=1, source_target_pairs={{0,4},{4,8},{8,12},{12,16},{16,20},{20,24},{24,28},{1,5},{5,9},{9,... | collective-permute-start | bytes 196616 | tf_op jit(solution)/shard_map/ppermute | solution.py:25
  13.4 2.1 %fusion.53 = (f32[2,8,128]{2,1,0:T(8,128)S(1)}, f32[2,8,128,256]{2,3,1,0:T(8,128)}) fusion(pred[128,256]{0,1:T(8,128)(4,1)S(1)} %fusion.31, bf16[128,2,10,64]{0,3,2,1:T(8,128)(2,1)S(1)} %bitcast.64, bf16[128,2,64]{0,2,1:T(8,128)(2,1)S(1)} %get-tuple-element.40, bf16[128,2,64]{0,2,1:T(8,128)(2,1)S(1)} %get-tuple-element.42), kind=kOutput, calls=%fused_computation.70 | convolution fusion | flops 69337344 | bytes 2465792 | tf_op jit(solution)/shard_map/sub | solution.py:270
  15.5 1.9 %fusion.12 = bf16[128,2,8,64]{0,3,2,1:T(8,128)(2,1)S(1)} fusion(f32[2,8,128,256]{2,3,1,0:T(8,128)} %get-tuple-element.47, f32[2,8,128]{2,1,0:T(8,128)S(1)} %get-tuple-element.46, bf16[128,2,64]{0,2,1:T(8,128)(2,1)S(1)} %get-tuple-element.39, bf16[128,2,64]{0,2,1:T(8,128)(2,1)S(1)} %get-tuple-element.41), kind=kOutput, calls=%fused_computation.16 | convolution fusion | flops 68419584 | bytes 2433024 | tf_op jit(solution)/shard_map/hgqk,khc->qhgc/dot_general | solution.py:272
  18.2 4.8 %fusion.3 = f32[2,2,32,2880]{3,2,1,0:T(8,128)S(1)} fusion(bf16[2,2,32,1024]{3,2,1,0:T(8,128)(2,1)S(1)} %dot_general.17, bf16[1024,2880]{0,1:T(8,128)(2,1)} %param.14), kind=kOutput, calls=%fused_computation.3 | convolution fusion | flops 754974720 | bytes 7634944 | tf_op jit(solution)/shard_map/dot_general | solution.py:326
  24.1 1.6 collective-permute-done.1
  25.8 1.6 collective-permute-start.2
  27.8 4.8 %collective-permute-done.2 = bf16[32,2880]{1,0:T(8,128)(2,1)S(1)} collective-permute-done((bf16[32,2880]{1,0:T(8,128)(2,1)S(1)}, bf16[32,2880]{1,0:T(8,128)(2,1)S(1)}, u32[]{:S(2)}, u32[]{:S(2)}) %collective-permute-start.2) | collective-permute-done | bytes 184352 | tf_op jit(solution)/shard_map/ppermute | solution.py:48
  33.0 5.4 %collective-permute-start.9 = (bf16[32,2944]{1,0:T(8,128)(2,1)S(1)}, bf16[32,2944]{1,0:T(8,128)(2,1)S(1)}, u32[]{:S(2)}, u32[]{:S(2)}) collective-permute-start(bf16[32,2944]{1,0:T(8,128)(2,1)S(1)} %pad_maximum_fusion.refs_0_), channel_id=1, source_target_pairs={{0,24},{1,25},{2,26},{3,27},{4,28},{5,29},{6,30},{7,31},{8,16},{9,... | collective-permute-start | bytes 565256 | tf_op jit(solution)/shard_map/ppermute | solution.py:48
  39.0 5.0 %collective-permute-done.9.refs_1_ = bf16[32,2944]{1,0:T(8,128)(2,1)S(1)} collective-permute-done((bf16[32,2944]{1,0:T(8,128)(2,1)S(1)}, bf16[32,2944]{1,0:T(8,128)(2,1)S(1)}, u32[]{:S(2)}, u32[]{:S(2)}) %collective-permute-start.9) | collective-permute-done | bytes 188448 | tf_op jit(solution)/shard_map/ppermute | solution.py:48
  44.1 9.8 %collective-permute-done.8.refs_0_ = bf16[32,2944]{1,0:T(8,128)(2,1)S(1)} collective-permute-done((bf16[32,2944]{1,0:T(8,128)(2,1)S(1)}, bf16[32,2944]{1,0:T(8,128)(2,1)S(1)}, u32[]{:S(2)}, u32[]{:S(2)}) %collective-permute-start.8) | collective-permute-done | bytes 188448 | tf_op jit(solution)/shard_map/ppermute | solution.py:48
  53.9 1.6 collective-permute-start.10
  56.7 8.9 %collective-permute-done.10.refs_1_ = bf16[64,2944]{1,0:T(8,128)(2,1)S(1)} collective-permute-done((bf16[64,2944]{1,0:T(8,128)(2,1)S(1)}, bf16[64,2944]{1,0:T(8,128)(2,1)S(1)}, u32[]{:S(2)}, u32[]{:S(2)}) %collective-permute-start.10) | collective-permute-done | bytes 376864 | tf_op jit(solution)/shard_map/ppermute | solution.py:48
  67.6 6.0 %collective-permute-done.4.refs_1_ = bf16[64,2944]{1,0:T(8,128)(2,1)S(1)} collective-permute-done((bf16[64,2944]{1,0:T(8,128)(2,1)S(1)}, bf16[64,2944]{1,0:T(8,128)(2,1)S(1)}, u32[]{:S(2)}, u32[]{:S(2)}) %collective-permute-start.4) | collective-permute-done | bytes 376864 | tf_op jit(solution)/shard_map/ppermute | solution.py:48
  74.5 2.7 %collective-permute-done.5.refs_2_ = bf16[64,2944]{1,0:T(8,128)(2,1)S(1)} collective-permute-done((bf16[64,2944]{1,0:T(8,128)(2,1)S(1)}, bf16[64,2944]{1,0:T(8,128)(2,1)S(1)}, u32[]{:S(2)}, u32[]{:S(2)}) %collective-permute-start.5) | collective-permute-done | bytes 376864 | tf_op jit(solution)/shard_map/ppermute | solution.py:48
  77.2 4.0 %collective-permute-done.6.refs_3_ = bf16[64,2944]{1,0:T(8,128)(2,1)S(1)} collective-permute-done((bf16[64,2944]{1,0:T(8,128)(2,1)S(1)}, bf16[64,2944]{1,0:T(8,128)(2,1)S(1)}, u32[]{:S(2)}, u32[]{:S(2)}) %collective-permute-start.6) | collective-permute-done | bytes 376864 | tf_op jit(solution)/shard_map/ppermute | solution.py:48
  81.6 3.3 %collective-permute-done.7.refs_1_ = bf16[256,2944]{1,0:T(8,128)(2,1)} collective-permute-done((bf16[256,2944]{1,0:T(8,128)(2,1)S(1)}, bf16[256,2944]{1,0:T(8,128)(2,1)}, u32[]{:S(2)}, u32[]{:S(2)}) %collective-permute-start.7) | collective-permute-done | bytes 1507360 | tf_op jit(solution)/shard_map/ppermute | solution.py:48
  84.9 25.1 %shard_map.104 = (bf16[256,2944]{1,0:T(8,128)(2,1)S(1)}, bf16[256,2944]{1,0:T(8,128)(2,1)}, bf16[256,2944]{1,0:T(8,128)(2,1)}, bf16[256,2944]{1,0:T(8,128)(2,1)}) custom-call(s32[1]{0:T(128)} %bitcast.16.first_ref, bf16[256,2944]{1,0:T(8,128)(2,1)} %copy-done.1, bf16[256,2944]{1,0:T(8,128)(2,1)} %collective-permute-done.7.refs_1_, ...), custom_call_target="tpu_custom_call" | custom-call | flops 12740198400 | bytes 49766400 | tf_op jit(solution)/shard_map/pallas_call | solution.py:231
  110.6 3.0 %collective-permute-done.14.refs_1_ = bf16[256,2944]{1,0:T(8,128)(2,1)S(1)} collective-permute-done((bf16[256,2944]{1,0:T(8,128)(2,1)}, bf16[256,2944]{1,0:T(8,128)(2,1)S(1)}, u32[]{:S(2)}, u32[]{:S(2)}) %collective-permute-start.14) | collective-permute-done | bytes 1507360 | tf_op jit(solution)/shard_map/ppermute | solution.py:48
  116.8 8.9 %collective-permute-done.15.refs_1_ = bf16[128,2944]{1,0:T(8,128)(2,1)S(1)} collective-permute-done((bf16[128,2944]{1,0:T(8,128)(2,1)S(1)}, bf16[128,2944]{1,0:T(8,128)(2,1)S(1)}, u32[]{:S(2)}, u32[]{:S(2)}) %collective-permute-start.15) | collective-permute-done | bytes 753696 | tf_op jit(solution)/shard_map/ppermute | solution.py:48
  127.3 10.4 %collective-permute-done.19.refs_1_ = bf16[128,2944]{1,0:T(8,128)(2,1)S(1)} collective-permute-done((bf16[128,2944]{1,0:T(8,128)(2,1)S(1)}, bf16[128,2944]{1,0:T(8,128)(2,1)S(1)}, u32[]{:S(2)}, u32[]{:S(2)}) %collective-permute-start.19) | collective-permute-done | bytes 753696 | tf_op jit(solution)/shard_map/ppermute | solution.py:48
  139.6 5.9 %collective-permute-done.20.refs_1_ = bf16[64,2944]{1,0:T(8,128)(2,1)S(1)} collective-permute-done((bf16[64,2944]{1,0:T(8,128)(2,1)S(1)}, bf16[64,2944]{1,0:T(8,128)(2,1)S(1)}, u32[]{:S(2)}, u32[]{:S(2)}) %collective-permute-start.20) | collective-permute-done | bytes 376864 | tf_op jit(solution)/shard_map/ppermute | solution.py:48
  145.7 2.5 %collective-permute-start.22 = (bf16[32,2944]{1,0:T(8,128)(2,1)S(1)}, bf16[32,2944]{1,0:T(8,128)(2,1)S(1)}, u32[]{:S(2)}, u32[]{:S(2)}) collective-permute-start(bf16[32,2944]{1,0:T(8,128)(2,1)S(1)} %get-tuple-element.36), channel_id=1, source_target_pairs={{0,24},{1,25},{2,26},{3,27},{4,28},{5,29},{6,30},{7,31},{8,16},{9,... | collective-permute-start | bytes 565256 | tf_op jit(solution)/shard_map/ppermute | solution.py:48
  148.3 10.8 %collective-permute-done.21 = bf16[32,2944]{1,0:T(8,128)(2,1)S(1)} collective-permute-done((bf16[32,2944]{1,0:T(8,128)(2,1)S(1)}, bf16[32,2944]{1,0:T(8,128)(2,1)S(1)}, u32[]{:S(2)}, u32[]{:S(2)}) %collective-permute-start.21) | collective-permute-done | bytes 188448 | tf_op jit(solution)/shard_map/ppermute | solution.py:48
  (81 shorter events, 19.7 us)
Async XLA Ops:
  6.6 6.8 %collective-permute-start = (bf16[128,2,128]{0,2,1:T(8,128)(2,1)S(1)}, bf16[128,2,128]{0,2,1:T(8,128)(2,1)S(1)}, u32[]{:S(2)}, u32[]{:S(2)}) collective-permute-start(bf16[128,2,128]{0,2,1:T(8,128)(2,1)S(1)} %pad_maximum_fusion.1), channel_id=1, source_target_pairs={{0,4},{4,8},{8,12},{12,16},{16,20},{20,24},{24,28},{1,5},{5,9},{9,... | collective-permute-start | bytes 196616 | tf_op jit(solution)/shard_map/ppermute | solution.py:25
  23.8 1.9 %collective-permute-start.1 = (bf16[2,32,2880]{2,1,0:T(8,128)(2,1)}, bf16[2,32,2880]{2,1,0:T(8,128)(2,1)S(1)}, u32[]{:S(2)}, u32[]{:S(2)}) collective-permute-start(bf16[2,32,2880]{2,1,0:T(8,128)(2,1)} %fusion.20), channel_id=1, source_target_pairs={{0,1},{1,0},{2,3},{3,2},{4,5},{5,4},{6,7},{7,6},{8,9},{9,8},{10,11... | collective-permute-start | bytes 1105928 | tf_op jit(solution)/shard_map/ppermute | solution.py:48
  25.8 6.8 %collective-permute-start.2 = (bf16[32,2880]{1,0:T(8,128)(2,1)S(1)}, bf16[32,2880]{1,0:T(8,128)(2,1)S(1)}, u32[]{:S(2)}, u32[]{:S(2)}) collective-permute-start(bf16[32,2880]{1,0:T(8,128)(2,1)S(1)} %fusion.28), channel_id=1, source_target_pairs={{0,2},{1,3},{2,0},{3,1},{4,6},{5,7},{6,4},{7,5},{8,10},{9,11},{10,... | collective-permute-start | bytes 552968 | tf_op jit(solution)/shard_map/ppermute | solution.py:48
  33.0 11.0 %collective-permute-start.9 = (bf16[32,2944]{1,0:T(8,128)(2,1)S(1)}, bf16[32,2944]{1,0:T(8,128)(2,1)S(1)}, u32[]{:S(2)}, u32[]{:S(2)}) collective-permute-start(bf16[32,2944]{1,0:T(8,128)(2,1)S(1)} %pad_maximum_fusion.refs_0_), channel_id=1, source_target_pairs={{0,24},{1,25},{2,26},{3,27},{4,28},{5,29},{6,30},{7,31},{8,16},{9,... | collective-permute-start | bytes 565256 | tf_op jit(solution)/shard_map/ppermute | solution.py:48
  38.4 15.5 %collective-permute-start.8 = (bf16[32,2944]{1,0:T(8,128)(2,1)S(1)}, bf16[32,2944]{1,0:T(8,128)(2,1)S(1)}, u32[]{:S(2)}, u32[]{:S(2)}) collective-permute-start(bf16[32,2944]{1,0:T(8,128)(2,1)S(1)} %pad_maximum_fusion.refs_0_), channel_id=1, source_target_pairs={{0,16},{1,17},{2,18},{3,19},{4,20},{5,21},{6,22},{7,23},{8,24},{9,... | collective-permute-start | bytes 565256 | tf_op jit(solution)/shard_map/ppermute | solution.py:48
  38.4 17.0 %collective-permute-start.3 = (bf16[32,2944]{1,0:T(8,128)(2,1)S(1)}, bf16[32,2944]{1,0:T(8,128)(2,1)S(1)}, u32[]{:S(2)}, u32[]{:S(2)}) collective-permute-start(bf16[32,2944]{1,0:T(8,128)(2,1)S(1)} %pad_maximum_fusion.refs_0_), channel_id=1, source_target_pairs={{0,8},{1,9},{2,10},{3,11},{4,12},{5,13},{6,14},{7,15},{8,0},{9,1},... | collective-permute-start | bytes 565256 | tf_op jit(solution)/shard_map/ppermute | solution.py:48
  53.9 11.7 %collective-permute-start.10 = (bf16[64,2944]{1,0:T(8,128)(2,1)S(1)}, bf16[64,2944]{1,0:T(8,128)(2,1)S(1)}, u32[]{:S(2)}, u32[]{:S(2)}) collective-permute-start(bf16[64,2944]{1,0:T(8,128)(2,1)S(1)} %shard_map.102.refs_0_), channel_id=1, source_target_pairs={{0,2},{1,5},{2,0},{3,7},{4,6},{5,1},{6,4},{7,3},{8,10},{9,13},{10,... | collective-permute-start | bytes 1130504 | tf_op jit(solution)/shard_map/ppermute | solution.py:48
  55.5 18.2 %collective-permute-start.4 = (bf16[64,2944]{1,0:T(8,128)(2,1)S(1)}, bf16[64,2944]{1,0:T(8,128)(2,1)S(1)}, u32[]{:S(2)}, u32[]{:S(2)}) collective-permute-start(bf16[64,2944]{1,0:T(8,128)(2,1)S(1)} %shard_map.100.refs_0_), channel_id=1, source_target_pairs={{0,2},{1,5},{2,0},{3,7},{4,6},{5,1},{6,4},{7,3},{8,10},{9,13},{10,... | collective-permute-start | bytes 1130504 | tf_op jit(solution)/shard_map/ppermute | solution.py:48
  56.1 18.2 %collective-permute-start.11 = (bf16[64,2944]{1,0:T(8,128)(2,1)S(1)}, bf16[64,2944]{1,0:T(8,128)(2,1)S(1)}, u32[]{:S(2)}, u32[]{:S(2)}) collective-permute-start(bf16[64,2944]{1,0:T(8,128)(2,1)S(1)} %shard_map.102.refs_0_), channel_id=1, source_target_pairs={{0,4},{1,3},{2,6},{3,1},{4,0},{5,7},{6,2},{7,5},{8,12},{9,11},{10,... | collective-permute-start | bytes 1130504 | tf_op jit(solution)/shard_map/ppermute | solution.py:48
  65.6 8.7 %collective-permute-start.12 = (bf16[64,2944]{1,0:T(8,128)(2,1)S(1)}, bf16[64,2944]{1,0:T(8,128)(2,1)S(1)}, u32[]{:S(2)}, u32[]{:S(2)}) collective-permute-start(bf16[64,2944]{1,0:T(8,128)(2,1)S(1)} %collective-permute-done.10.refs_1_), channel_id=1, source_target_pairs={{0,4},{1,3},{2,6},{3,1},{4,0},{5,7},{6,2},{7,5},{8,12},{9,11},{10,... | collective-permute-start | bytes 1130504 | tf_op jit(solution)/shard_map/ppermute | solution.py:48
  66.2 11.0 %collective-permute-start.5 = (bf16[64,2944]{1,0:T(8,128)(2,1)S(1)}, bf16[64,2944]{1,0:T(8,128)(2,1)S(1)}, u32[]{:S(2)}, u32[]{:S(2)}) collective-permute-start(bf16[64,2944]{1,0:T(8,128)(2,1)S(1)} %shard_map.100.refs_0_), channel_id=1, source_target_pairs={{0,4},{1,3},{2,6},{3,1},{4,0},{5,7},{6,2},{7,5},{8,12},{9,11},{10,... | collective-permute-start | bytes 1130504 | tf_op jit(solution)/shard_map/ppermute | solution.py:48
  73.7 7.6 %collective-permute-start.6 = (bf16[64,2944]{1,0:T(8,128)(2,1)S(1)}, bf16[64,2944]{1,0:T(8,128)(2,1)S(1)}, u32[]{:S(2)}, u32[]{:S(2)}) collective-permute-start(bf16[64,2944]{1,0:T(8,128)(2,1)S(1)} %collective-permute-done.4.refs_1_), channel_id=1, source_target_pairs={{0,4},{1,3},{2,6},{3,1},{4,0},{5,7},{6,2},{7,5},{8,12},{9,11},{10,... | collective-permute-start | bytes 1130504 | tf_op jit(solution)/shard_map/ppermute | solution.py:48
  74.4 10.5 %copy-start = (bf16[256,2944]{1,0:T(8,128)(2,1)}, bf16[256,2944]{1,0:T(8,128)(2,1)S(1)}, u32[]{:S(2)}) copy-start(bf16[256,2944]{1,0:T(8,128)(2,1)S(1)} %shard_map.103.refs_2_) | copy-start | bytes 4521988
  74.4 7.2 %collective-permute-start.13 = (bf16[256,2944]{1,0:T(8,128)(2,1)S(1)}, bf16[256,2944]{1,0:T(8,128)(2,1)}, u32[]{:S(2)}, u32[]{:S(2)}) collective-permute-start(bf16[256,2944]{1,0:T(8,128)(2,1)S(1)} %shard_map.103.refs_2_), channel_id=1, source_target_pairs={{0,1},{1,0},{2,3},{3,2},{4,5},{5,4},{6,7},{7,6},{8,9},{9,8},{10,11... | collective-permute-start | bytes 4521992 | tf_op jit(solution)/shard_map/ppermute | solution.py:48
  81.4 3.5 %collective-permute-start.7 = (bf16[256,2944]{1,0:T(8,128)(2,1)S(1)}, bf16[256,2944]{1,0:T(8,128)(2,1)}, u32[]{:S(2)}, u32[]{:S(2)}) collective-permute-start(bf16[256,2944]{1,0:T(8,128)(2,1)S(1)} %shard_map.101.refs_0_), channel_id=1, source_target_pairs={{0,1},{1,0},{2,3},{3,2},{4,5},{5,4},{6,7},{7,6},{8,9},{9,8},{10,11... | collective-permute-start | bytes 4521992 | tf_op jit(solution)/shard_map/ppermute | solution.py:48
  110.0 3.6 %collective-permute-start.14 = (bf16[256,2944]{1,0:T(8,128)(2,1)}, bf16[256,2944]{1,0:T(8,128)(2,1)S(1)}, u32[]{:S(2)}, u32[]{:S(2)}) collective-permute-start(bf16[256,2944]{1,0:T(8,128)(2,1)} %get-tuple-element.22), channel_id=1, source_target_pairs={{0,1},{1,0},{2,3},{3,2},{4,5},{5,4},{6,7},{7,6},{8,9},{9,8},{10,11... | collective-permute-start | bytes 4521992 | tf_op jit(solution)/shard_map/ppermute | solution.py:48
  110.2 5.6 %collective-permute-start.18 = (bf16[256,2944]{1,0:T(8,128)(2,1)}, bf16[256,2944]{1,0:T(8,128)(2,1)S(1)}, u32[]{:S(2)}, u32[]{:S(2)}) collective-permute-start(bf16[256,2944]{1,0:T(8,128)(2,1)} %get-tuple-element.30), channel_id=1, source_target_pairs={{0,1},{1,0},{2,3},{3,2},{4,5},{5,4},{6,7},{7,6},{8,9},{9,8},{10,11... | collective-permute-start | bytes 4521992 | tf_op jit(solution)/shard_map/ppermute | solution.py:48
  114.0 11.7 %collective-permute-start.15 = (bf16[128,2944]{1,0:T(8,128)(2,1)S(1)}, bf16[128,2944]{1,0:T(8,128)(2,1)S(1)}, u32[]{:S(2)}, u32[]{:S(2)}) collective-permute-start(bf16[128,2944]{1,0:T(8,128)(2,1)S(1)} %get-tuple-element.24), channel_id=1, source_target_pairs={{0,4},{1,3},{2,6},{3,1},{4,0},{5,7},{6,2},{7,5},{8,12},{9,11},{10,... | collective-permute-start | bytes 2261000 | tf_op jit(solution)/shard_map/ppermute | solution.py:48
  116.1 21.7 %collective-permute-start.19 = (bf16[128,2944]{1,0:T(8,128)(2,1)S(1)}, bf16[128,2944]{1,0:T(8,128)(2,1)S(1)}, u32[]{:S(2)}, u32[]{:S(2)}) collective-permute-start(bf16[128,2944]{1,0:T(8,128)(2,1)S(1)} %get-tuple-element.32), channel_id=1, source_target_pairs={{0,4},{1,3},{2,6},{3,1},{4,0},{5,7},{6,2},{7,5},{8,12},{9,11},{10,... | collective-permute-start | bytes 2261000 | tf_op jit(solution)/shard_map/ppermute | solution.py:48
  125.8 13.7 %collective-permute-start.16 = (bf16[64,2944]{1,0:T(8,128)(2,1)S(1)}, bf16[64,2944]{1,0:T(8,128)(2,1)S(1)}, u32[]{:S(2)}, u32[]{:S(2)}) collective-permute-start(bf16[64,2944]{1,0:T(8,128)(2,1)S(1)} %get-tuple-element.26), channel_id=1, source_target_pairs={{0,2},{1,5},{2,0},{3,7},{4,6},{5,1},{6,4},{7,3},{8,10},{9,13},{10,... | collective-permute-start | bytes 1130504 | tf_op jit(solution)/shard_map/ppermute | solution.py:48
  137.9 7.7 %collective-permute-start.20 = (bf16[64,2944]{1,0:T(8,128)(2,1)S(1)}, bf16[64,2944]{1,0:T(8,128)(2,1)S(1)}, u32[]{:S(2)}, u32[]{:S(2)}) collective-permute-start(bf16[64,2944]{1,0:T(8,128)(2,1)S(1)} %get-tuple-element.34), channel_id=1, source_target_pairs={{0,2},{1,5},{2,0},{3,7},{4,6},{5,1},{6,4},{7,3},{8,10},{9,13},{10,... | collective-permute-start | bytes 1130504 | tf_op jit(solution)/shard_map/ppermute | solution.py:48
  139.6 8.7 %collective-permute-start.17 = (bf16[32,2944]{1,0:T(8,128)(2,1)S(1)}, bf16[32,2944]{1,0:T(8,128)(2,1)S(1)}, u32[]{:S(2)}, u32[]{:S(2)}) collective-permute-start(bf16[32,2944]{1,0:T(8,128)(2,1)S(1)} %get-tuple-element.28), channel_id=1, source_target_pairs={{0,8},{1,9},{2,10},{3,11},{4,12},{5,13},{6,14},{7,15},{8,0},{9,1},... | collective-permute-start | bytes 565256 | tf_op jit(solution)/shard_map/ppermute | solution.py:48
  145.6 13.4 %collective-permute-start.21 = (bf16[32,2944]{1,0:T(8,128)(2,1)S(1)}, bf16[32,2944]{1,0:T(8,128)(2,1)S(1)}, u32[]{:S(2)}, u32[]{:S(2)}) collective-permute-start(bf16[32,2944]{1,0:T(8,128)(2,1)S(1)} %get-tuple-element.35), channel_id=1, source_target_pairs={{0,16},{1,17},{2,18},{3,19},{4,20},{5,21},{6,22},{7,23},{8,24},{9,... | collective-permute-start | bytes 565256 | tf_op jit(solution)/shard_map/ppermute | solution.py:48
  145.7 13.3 %collective-permute-start.22 = (bf16[32,2944]{1,0:T(8,128)(2,1)S(1)}, bf16[32,2944]{1,0:T(8,128)(2,1)S(1)}, u32[]{:S(2)}, u32[]{:S(2)}) collective-permute-start(bf16[32,2944]{1,0:T(8,128)(2,1)S(1)} %get-tuple-element.36), channel_id=1, source_target_pairs={{0,24},{1,25},{2,26},{3,27},{4,28},{5,29},{6,30},{7,31},{8,16},{9,... | collective-permute-start | bytes 565256 | tf_op jit(solution)/shard_map/ppermute | solution.py:48
  (7 other events, 47.4 us)

commit v2 on v1

--- a/solution.py
+++ b/solution.py
@@ -59,29 +59,34 @@
 
 ROUTING = 64
 SMALL_KERNEL = 8 << 20
-
-
-def join_kernel(*refs):
-    parts, out_ref = refs[:-1], refs[-1]
-    rows = parts[0].shape[0]
-    for place, part in enumerate(parts):
-        out_ref[place * rows : (place + 1) * rows, :] = part[...]
-
-
-def join(parts):
+EXPERT_KERNEL = 6 << 20
+
+
+def join_kernel(count, pieces, *refs):
+    parts, out_ref = refs[:count], refs[-1]
+    rows = parts[0].shape[0] // pieces
+    for piece in range(pieces):
+        for place, part in enumerate(parts):
+            start = (piece * count + place) * rows
+            out_ref[start : start + rows, :] = part[piece * rows : (piece + 1) * rows, :]
+
+
+def join(parts, pieces=1, after=()):
     rows, width = parts[0].shape
     return pl.pallas_call(
-        join_kernel,
+        functools.partial(join_kernel, len(parts), pieces),
+        in_specs=[pl.BlockSpec(memory_space=pltpu.VMEM)] * len(parts)
+        + [pl.BlockSpec(memory_space=pl.ANY)] * len(after),
         out_shape=jax.ShapeDtypeStruct((len(parts) * rows, width), parts[0].dtype),
         compiler_params=pltpu.CompilerParams(vmem_limit_bytes=SMALL_KERNEL),
         cost_estimate=pl.CostEstimate(
             flops=0, bytes_accessed=4 * len(parts) * rows * width, transcendentals=0
         ),
-    )(*parts)
-
-
-def fold_kernel(count, *refs):
-    terms, outs = refs[:count], refs[count:]
+    )(*parts, *after)
+
+
+def fold_kernel(count, outs_n, *refs):
+    terms, outs = refs[:count], refs[len(refs) - outs_n :]
     rows = outs[0].shape[0]
     for place, out_ref in enumerate(outs):
         cut = slice(place * rows, (place + 1) * rows)
@@ -91,65 +96,82 @@
         out_ref[...] = total.astype(out_ref.dtype)
 
 
-def fold(terms, parts, first=jnp.float32):
+def fold(terms, kinds, after=()):
     rows, width = terms[0].shape
-    rows = rows // parts
-    kinds = [first] + [jnp.bfloat16] * (parts - 1)
+    rows = rows // len(kinds)
     return pl.pallas_call(
-        functools.partial(fold_kernel, len(terms)),
+        functools.partial(fold_kernel, len(terms), len(kinds)),
+        in_specs=[pl.BlockSpec(memory_space=pltpu.VMEM)] * len(terms)
+        + [pl.BlockSpec(memory_space=pl.ANY)] * len(after),
         out_shape=[jax.ShapeDtypeStruct((rows, width), kind) for kind in kinds],
         compiler_params=pltpu.CompilerParams(vmem_limit_bytes=SMALL_KERNEL),
         cost_estimate=pl.CostEstimate(
-            flops=len(terms) * rows * parts * width,
-            bytes_accessed=4 * len(terms) * rows * parts * width,
+            flops=len(terms) * rows * len(kinds) * width,
+            bytes_accessed=4 * len(terms) * rows * len(kinds) * width,
             transcendentals=0,
         ),
-    )(*terms)
-
-
-def collect(kept, arrived, steps, last, first):
-    terms = [kept, arrived]
-    for size, even, odd in reversed(steps):
-        parts = fold(terms, size)
-        terms = [parts[0]] + [
-            swap(parts[other], other * even, other * odd) for other in range(1, size)
-        ]
-    return fold(terms, last, first)
+    )(*terms, *after)
+
+
+def send_parts(parts, even, odd):
+    return [parts[0]] + [
+        swap(part, other * even, other * odd) for other, part in enumerate(parts[1:], 1)
+    ]
+
+
+PIECE_ROWS = 256
+PIECE_SLOTS = 6
+COLUMNS = 768
 
 
 def expert_kernel(sizes, first_ref, *refs):
-    groups, block_rows, capacity = sizes
+    groups, block_rows, capacity, step = sizes
     ins = refs[:groups]
     gate_up_ref, down_ref = refs[groups : groups + 2]
-    outs = refs[groups + 2 : 2 * groups + 2]
-    tokens_ref, gate_up_buf, down_buf, packed_ref, gate_ref, placer_ref = refs[2 * groups + 2 : -4]
-    token_sem, gate_up_sem, down_sem, out_sem = refs[-4:]
-    experts, _, units, width = gate_up_ref.shape
+    tokens_ref, ring_ref, packed_ref, sum_ref, gate_ref, placer_ref, sem, token_sem = refs[-8:]
+    outs = refs[-8 - groups : -8]
+    experts, units, width = down_ref.shape
     tokens_n = ins[0].shape[0]
     per_group = tokens_n // block_rows
     span = per_group * capacity
     slots_n = experts * span
 
+    columns = [slice(at, min(at + COLUMNS, width)) for at in range(0, width, COLUMNS)]
+
+    pieces = [
+        (expert, matrix, start, min(step, units - start))
+        for expert in range(experts)
+        for start in range(0, units, step)
+        for matrix in range(3)
+    ]
+
+    def piece_copy(number):
+        expert, matrix, start, rows = pieces[number]
+        if matrix == 2:
+            source = down_ref.at[expert, pl.ds(start, rows)]
+        else:
+            source = gate_up_ref.at[expert, matrix, pl.ds(start, rows)]
+        slot = number % PIECE_SLOTS
+        return pltpu.make_async_copy(source, ring_ref.at[slot, pl.ds(0, rows)], sem.at[slot])
+
+    def use(wanted, product):
+        number = pieces.index(wanted)
+        piece_copy(number).wait()
+        result = product(ring_ref.at[number % PIECE_SLOTS, pl.ds(0, wanted[3])])
+        if number + PIECE_SLOTS < len(pieces):
+            piece_copy(number + PIECE_SLOTS).start()
+        return result
+
     def token_copy(group):
         return pltpu.make_async_copy(ins[group], tokens_ref.at[group], token_sem.at[group])
 
     def out_copy(group):
-        return pltpu.make_async_copy(tokens_ref.at[group], outs[group], out_sem.at[group])
-
-    def gate_up_copy(expert):
-        return pltpu.make_async_copy(
-            gate_up_ref.at[expert], gate_up_buf.at[expert % 2], gate_up_sem.at[expert % 2]
-        )
-
-    def down_copy(expert):
-        return pltpu.make_async_copy(
-            down_ref.at[expert], down_buf.at[expert % 2], down_sem.at[expert % 2]
-        )
+        return pltpu.make_async_copy(tokens_ref.at[group], outs[group], token_sem.at[group])
 
     for group in range(groups):
         token_copy(group).start()
-    gate_up_copy(0).start()
-    down_copy(0).start()
+    for number in range(min(PIECE_SLOTS, len(pieces))):
+        piece_copy(number).start()
 
     slot = lax.broadcasted_iota(jnp.int32, (slots_n, tokens_n), 0)
     token = lax.broadcasted_iota(jnp.int32, (slots_n, tokens_n), 1)
@@ -181,41 +203,51 @@
         hot = jnp.where(chosen, 1.0, 0.0)
         gate = jnp.sum(jnp.where(chosen, gate, 0.0), axis=1, keepdims=True)
         placer_ref[group] = jnp.transpose(hot).astype(jnp.bfloat16)
-        rows = tokens_ref[group, :, :width]
-        packed = jnp.dot(hot.astype(jnp.bfloat16), rows, preferred_element_type=jnp.float32)
-        packed = packed.astype(jnp.bfloat16)
+        hot = hot.astype(jnp.bfloat16)
+        for cut in columns:
+            packed = jnp.dot(hot, tokens_ref[group, :, cut], preferred_element_type=jnp.float32)
+            packed = packed.astype(jnp.bfloat16)
+            for expert in range(experts):
+                packed_ref[expert, group * span : (group + 1) * span, cut] = packed[
+                    expert * span : (expert + 1) * span
+                ]
         for expert in range(experts):
             place = slice(group * span, (group + 1) * span)
-            packed_ref[expert, place] = packed[expert * span : (expert + 1) * span]
             gate_ref[expert, place] = jnp.broadcast_to(
                 gate[expert * span : (expert + 1) * span], (span, 128)
             )
 
-    contract = (((1,), (1,)), ((), ()))
     for expert in range(experts):
-        held = expert % 2
-        if expert + 1 < experts:
-            gate_up_copy(expert + 1).start()
-            down_copy(expert + 1).start()
-        gate_up_copy(expert).wait()
         rows = packed_ref[expert]
-        gate = lax.dot_general(
-            rows, gate_up_buf[held, 0], contract, preferred_element_type=jnp.float32
-        )
-        up = lax.dot_general(
-            rows, gate_up_buf[held, 1], contract, preferred_element_type=jnp.float32
-        )
-        act = gate / (1.0 + jnp.exp(-gate)) * up * gate_ref[expert][:, :1]
-        act = act.astype(jnp.bfloat16)
-        down_copy(expert).wait()
-        result = jnp.dot(act, down_buf[held], preferred_element_type=jnp.float32)
-        packed_ref[expert] = result.astype(jnp.bfloat16)
+
+        def project(weight):
+            return lax.dot_general(
+                rows, weight, (((1,), (1,)), ((), ())), preferred_element_type=jnp.float32
+            )
+
+        for start in range(0, units, step):
+            length = min(step, units - start)
+            gate = use((expert, 0, start, length), lambda ref: project(ref[...]))
+            up = use((expert, 1, start, length), lambda ref: project(ref[...]))
+            act = gate / (1.0 + jnp.exp(-gate)) * up * gate_ref[expert][:, :1]
+            act = act.astype(jnp.bfloat16)
+
+            def add(weight_ref):
+                for cut in columns:
+                    part = jnp.dot(act, weight_ref[:, cut], preferred_element_type=jnp.float32)
+                    sum_ref[:, cut] = sum_ref[:, cut] + part if start else part
+
+            use((expert, 2, start, length), add)
+        for cut in columns:
+            packed_ref[expert, :, cut] = sum_ref[:, cut].astype(jnp.bfloat16)
 
     for group in range(groups):
         place = slice(group * span, (group + 1) * span)
-        rows = jnp.concatenate([packed_ref[expert, place] for expert in range(experts)], axis=0)
-        summed = jnp.dot(placer_ref[group], rows, preferred_element_type=jnp.float32)
-        tokens_ref[group, :, :width] = summed.astype(jnp.bfloat16)
+        for cut in columns:
+            rows = [packed_ref[expert, place, cut] for expert in range(experts)]
+            rows = jnp.concatenate(rows, axis=0)
+            summed = jnp.dot(placer_ref[group], rows, preferred_element_type=jnp.float32)
+            tokens_ref[group, :, cut] = summed.astype(jnp.bfloat16)
         out_copy(group).start()
     for group in range(groups):
         out_copy(group).wait()
@@ -224,28 +256,32 @@
 def run_experts(first, tokens, gate_up, down, block_rows, capacity):
     groups = len(tokens)
     tokens_n, wide = tokens[0].shape
-    experts, _, units, width = gate_up.shape
+    experts, units, width = down.shape
     span = tokens_n // block_rows * capacity
     slots_n = experts * span
+    step = units if units % 16 else PIECE_ROWS
+    padded = -(-width // 128) * 128
+    scratch = 2 * padded * (groups * tokens_n + PIECE_SLOTS * min(step, units))
+    scratch += 2 * padded * (experts + 2) * groups * span + 512 * experts * groups * span
+    scratch += 2 * groups * tokens_n * slots_n
     anywhere = pl.BlockSpec(memory_space=pl.ANY)
     return pl.pallas_call(
-        functools.partial(expert_kernel, (groups, block_rows, capacity)),
-        in_specs=[pl.BlockSpec(memory_space=pltpu.SMEM)] + [anywhere] * (groups + 2),
+        functools.partial(expert_kernel, (groups, block_rows, capacity, step)),
+        in_specs=[pl.BlockSpec(memory_space=pltpu.SMEM)]
+        + [anywhere] * (groups + 2),
         out_specs=[anywhere] * groups,
         out_shape=[jax.ShapeDtypeStruct((tokens_n, wide), jnp.bfloat16)] * groups,
         scratch_shapes=[
             pltpu.VMEM((groups, tokens_n, wide), jnp.bfloat16),
-            pltpu.VMEM((2, 2, units, width), jnp.bfloat16),
-            pltpu.VMEM((2, units, width), jnp.bfloat16),
+            pltpu.VMEM((PIECE_SLOTS, min(step, units), width), jnp.bfloat16),
             pltpu.VMEM((experts, groups * span, width), jnp.bfloat16),
+            pltpu.VMEM((groups * span, width), jnp.float32),
             pltpu.VMEM((experts, groups * span, 128), jnp.float32),
             pltpu.VMEM((groups, tokens_n, slots_n), jnp.bfloat16),
-            pltpu.SemaphoreType.DMA((groups,)),
-            pltpu.SemaphoreType.DMA((2,)),
-            pltpu.SemaphoreType.DMA((2,)),
+            pltpu.SemaphoreType.DMA((PIECE_SLOTS,)),
             pltpu.SemaphoreType.DMA((groups,)),
         ],
-        compiler_params=pltpu.CompilerParams(vmem_limit_bytes=52 << 20),
+        compiler_params=pltpu.CompilerParams(vmem_limit_bytes=scratch + EXPERT_KERNEL),
         cost_estimate=pl.CostEstimate(
             flops=6 * slots_n * groups * width * units,
             bytes_accessed=6 * experts * width * units,
@@ -332,8 +368,8 @@
     place = lax.axis_index("tp") // 2
     attn_out = lax.dynamic_index_in_dim(kept, place, 0, False)
     for other in range(1, across):
-        part = lax.dynamic_index_in_dim(kept, place ^ other, 0, False).astype(jnp.bfloat16)
-        attn_out = attn_out + swap(part, 2 * other, 2 * other).astype(jnp.float32)
+        handed_on = lax.dynamic_index_in_dim(kept, place ^ other, 0, False).astype(jnp.bfloat16)
+        attn_out = attn_out + swap(handed_on, 2 * other, 2 * other).astype(jnp.float32)
     own_start = lax.axis_index("tp") * block_rows
     residual = (
         lax.dynamic_slice_in_dim(stream_in, own_start, block_rows, 0).astype(jnp.float32) + attn_out
@@ -347,25 +383,49 @@
     low = lax.reduce_precision(gate_weight - high - middle, 8, 7)
     routing = jnp.concatenate([expert_index.astype(jnp.float32), high, middle, low], axis=1)
     routing = jnp.pad(routing, ((0, 0), (0, ROUTING - 4 * TOPK))).astype(jnp.bfloat16)
+    gate_up = jnp.transpose(w_gateup, (0, 2, 3, 1))
+    gate_up = pltpu.with_memory_space_constraint(gate_up, pltpu.HBM)
+    down = pltpu.with_memory_space_constraint(w_down, pltpu.HBM)
     rows = jnp.concatenate([hidden_in, routing], axis=1)
 
     (slow, slow_step, _), inner = plan[0], plan[1:]
-    held = [rows] + [swap(rows, other * slow_step, other * slow_step) for other in range(1, slow)]
-    near, far = held[: slow // 2], held[slow // 2 :]
-    near, far = [join(spread(join(pieces), inner)) for pieces in (near, far)]
-    tokens = [near, swap(near, 1, 1), far, swap(far, 1, 1)]
+    (size, even, odd), (last_size, last_even, last_odd) = inner
+    half = slow // 2
+
+    def along(value, offset):
+        return swap(value, offset * slow_step, offset * slow_step)
+
+    even_pieces = [along(rows, offset) for offset in range(2, slow, 2)]
+    odd_pieces = [along(rows, 1)]
+    odd_pieces += [along(join([rows], 1, even_pieces), offset) for offset in range(3, slow, 2)]
+    spread_own = spread(rows, inner)
+    even_pieces = [join([piece], 1, [spread_own[1], spread_own[size]]) for piece in even_pieces]
+    pieces_a = spread_own + [piece for start in even_pieces for piece in spread(start, inner)]
+    pair = join(odd_pieces, 1, pieces_a[-size * last_size + 1 :][: size])
+    mine_a = join(pieces_a)
+    theirs_a = swap(mine_a, 1, 1)
+    pieces_b = spread(pair, inner)
+    mine_b = join(pieces_b, half)
+    tokens = [mine_a, theirs_a, mine_b, swap(mine_b, 1, 1)]
 
     first = (lax.axis_index("seq") * experts_dev).astype(jnp.int32).reshape(1)
-    weights = jnp.transpose(w_gateup, (0, 2, 3, 1))
-    near, near_handed, far, far_handed = run_experts(
-        first, tokens, weights, w_down, block_rows, capacity
-    )
-
-    far = collect(far, swap(far_handed, 1, 1), inner, slow // 2, jnp.bfloat16)
-    near = collect(near, swap(near_handed, 1, 1), inner, slow // 2, jnp.float32)
-    total = residual + near[0][:, :MODEL_WIDTH]
-    for other, part in enumerate(near[1:] + far, 1):
-        part = swap(part, other * slow_step, other * slow_step)
+    sums = run_experts(first, tokens, gate_up, down, block_rows, capacity)
+
+    kinds = ([jnp.float32] + [jnp.bfloat16] * (last_size - 1)) * half
+    inner_kinds = [jnp.float32] + [jnp.bfloat16] * (size - 1)
+    parts = [fold([kept, swap(handed, 1, 1)], kinds) for kept, handed in (sums[:2], sums[2:])]
+    arrived = []
+    after = []
+    for offset in list(range(slow - 1, 1, -1)) + [1, 0]:
+        place = offset // 2 * last_size
+        terms = send_parts(parts[offset % 2][place : place + last_size], last_even, last_odd)
+        terms = send_parts(fold(terms, inner_kinds, after + arrived[-2:-1]), even, odd)
+        if offset:
+            after = list(fold(terms, [jnp.bfloat16]))
+            arrived.append(along(after[0], offset))
+        else:
+            total = residual + fold(terms, [jnp.float32])[0][:, :MODEL_WIDTH]
+    for part in arrived:
         total = total + part[:, :MODEL_WIDTH].astype(jnp.float32)
     return total.astype(jnp.bfloat16)
 

time: 162 us -> 173 us (1.068); the launches traced: 160 us -> 173 us
  waiting for transfers between devices: 87.9 us -> 66.1 us
  starting transfers between devices: 25.9 us -> 45.6 us
  Pallas kernels: 26.4 us -> 41.8 us
    ppermute x22 -> x29, waiting for transfers between devices: 86.4 us -> 64.5 us  [swap(): return lax.ppermute(value, ('seq', 'tp'), pairs)]
    ppermute x22 -> x29, starting transfers between devices: 21 us -> 40.8 us  [swap(): return lax.ppermute(value, ('seq', 'tp'), pairs)]
    pallas_call x1, Pallas kernels: 25.1 us -> 40.4 us  [run_experts(): pl.pallas_call(functools.partial(expert_kernel, (groups, block_rows, capa...]
  transfers between devices with their start and end apart: 23 -> 30, of which waited for: 16 -> 19; matrix products, arithmetic and copies ran while one was open for 1% -> 1% of each run, Pallas kernels for 1% -> 1%
where the time goes in v2:
time: 173 us
  waiting for transfers between devices  66.1 us (38%)
  starting transfers between devices  45.6 us (26%)
  Pallas kernels  41.8 us (24%)
  matrix products  13.6 us (8%)
  other arithmetic  2.9 us (2%)
  local copies, waits for them, and re-layouts  2.77 us (2%)
    ppermute x29, waiting for transfers between devices, swap(): return lax.ppermute(value, ('seq', 'tp'), pairs)  64.5 us
    ppermute x29, starting transfers between devices, swap(): return lax.ppermute(value, ('seq', 'tp'), pairs)  40.8 us
    pallas_call x1, Pallas kernels, run_experts(): pl.pallas_call(functools.partial(expert_kernel, (groups, block_rows, capa...  40.4 us
    ppermute x1, starting transfers between devices, from_behind(): lax.ppermute(value, axis, [(source, source + steps) for source in range(f...  4.87 us
    dot_general x1, matrix products, local(): jnp.einsum('td,dhc->thc', normed, w_qkv, preferred_element_type=jnp.float32)  4.79 us
    dot_general x1, matrix products, local(): terms = jnp.dot(attended, w_out, preferred_element_type=jnp.float32)  4.79 us
  transfers between devices with their start and end apart: 30, of which 19 were waited for; matrix products, arithmetic and copies ran while one was open for 1% of the time, Pallas kernels for 1%

profile of v2, /device:TPU:0, one launch (start us, length us, event | category | flops | bytes accessed | tf_op | source)
XLA Modules:
  0.0 173.1 jit_solution(16454790407259332922)
XLA Ops:
  1.5 4.8 %fusion.9 = bf16[128,2,640]{2,0,1:T(8,128)(2,1)S(1)} fusion(bf16[2880,2,640]{2,1,0:T(2,128)(2,1)} %param.12, bf16[128,2880]{0,1:T(8,128)(2,1)} %param.10, f32[2880]{0:T(1024)} %param.11, f32[128]{0:T(128)S(1)} %add_rsqrt_fusion.1), kind=kOutput, calls=%fused_computation.14 | convolution fusion | flops 945356800 | bytes 8449792 | tf_op jit(solution)/shard_map/td,dhc->thc/dot_general | solution.py:332
  6.6 4.9 %collective-permute-start = (bf16[128,2,128]{0,2,1:T(8,128)(2,1)S(1)}, bf16[128,2,128]{0,2,1:T(8,128)(2,1)S(1)}, u32[]{:S(2)}, u32[]{:S(2)}) collective-permute-start(bf16[128,2,128]{0,2,1:T(8,128)(2,1)S(1)} %pad_maximum_fusion.1), channel_id=1, source_target_pairs={{0,4},{4,8},{8,12},{12,16},{16,20},{20,24},{24,28},{1,5},{5,9},{9,... | collective-permute-start | bytes 196616 | tf_op jit(solution)/shard_map/ppermute | solution.py:25
  13.4 2.1 %fusion.57 = (f32[2,8,128]{2,1,0:T(8,128)S(1)}, f32[2,8,128,256]{2,3,1,0:T(8,128)}) fusion(pred[128,256]{0,1:T(8,128)(4,1)S(1)} %fusion.35, bf16[128,2,10,64]{0,3,2,1:T(8,128)(2,1)S(1)} %bitcast.64, bf16[128,2,64]{0,2,1:T(8,128)(2,1)S(1)} %get-tuple-element.48, bf16[128,2,64]{0,2,1:T(8,128)(2,1)S(1)} %get-tuple-element.50), kind=kOutput, calls=%fused_computation.74 | convolution fusion | flops 69337344 | bytes 2465792 | tf_op jit(solution)/shard_map/sub | solution.py:306
  18.2 4.8 %fusion.3 = f32[2,2,32,2880]{3,2,1,0:T(8,128)S(1)} fusion(bf16[2,2,32,1024]{3,2,1,0:T(8,128)(2,1)S(1)} %dot_general.17, bf16[1024,2880]{0,1:T(8,128)(2,1)} %param.14), kind=kOutput, calls=%fused_computation.3 | convolution fusion | flops 754974720 | bytes 7634944 | tf_op jit(solution)/shard_map/dot_general | solution.py:362
  27.8 4.8 %collective-permute-done.2 = bf16[32,2880]{1,0:T(8,128)(2,1)S(1)} collective-permute-done((bf16[32,2880]{1,0:T(8,128)(2,1)S(1)}, bf16[32,2880]{1,0:T(8,128)(2,1)S(1)}, u32[]{:S(2)}, u32[]{:S(2)}) %collective-permute-start.2) | collective-permute-done | bytes 184352 | tf_op jit(solution)/shard_map/ppermute | solution.py:48
  33.0 4.3 %collective-permute-start.6 = (bf16[32,2944]{1,0:T(8,128)(2,1)S(1)}, bf16[32,2944]{1,0:T(8,128)(2,1)S(1)}, u32[]{:S(2)}, u32[]{:S(2)}) collective-permute-start(bf16[32,2944]{1,0:T(8,128)(2,1)S(1)} %pad_maximum_fusion.refs_0_), channel_id=1, source_target_pairs={{0,16},{1,17},{2,18},{3,19},{4,20},{5,21},{6,22},{7,23},{8,24},{9,... | collective-permute-start | bytes 565256 | tf_op jit(solution)/shard_map/ppermute | solution.py:48
  41.0 4.7 %collective-permute-done.6.refs_0_.refs_1_ = bf16[32,2944]{1,0:T(8,128)(2,1)S(1)} collective-permute-done((bf16[32,2944]{1,0:T(8,128)(2,1)S(1)}, bf16[32,2944]{1,0:T(8,128)(2,1)S(1)}, u32[]{:S(2)}, u32[]{:S(2)}) %collective-permute-start.6) | collective-permute-done | bytes 188448 | tf_op jit(solution)/shard_map/ppermute | solution.py:48
  45.7 3.6 %collective-permute-start.12 = (bf16[32,2944]{1,0:T(8,128)(2,1)S(1)}, bf16[32,2944]{1,0:T(8,128)(2,1)S(1)}, u32[]{:S(2)}, u32[]{:S(2)}) collective-permute-start(bf16[32,2944]{1,0:T(8,128)(2,1)S(1)} %shard_map.102), channel_id=1, source_target_pairs={{0,24},{1,25},{2,26},{3,27},{4,28},{5,29},{6,30},{7,31},{8,16},{9,... | collective-permute-start | bytes 565256 | tf_op jit(solution)/shard_map/ppermute | solution.py:48
  51.5 2.7 %collective-permute-done.12.refs_1_ = bf16[32,2944]{1,0:T(8,128)(2,1)S(1)} collective-permute-done((bf16[32,2944]{1,0:T(8,128)(2,1)S(1)}, bf16[32,2944]{1,0:T(8,128)(2,1)S(1)}, u32[]{:S(2)}, u32[]{:S(2)}) %collective-permute-start.12) | collective-permute-done | bytes 188448 | tf_op jit(solution)/shard_map/ppermute | solution.py:48
  54.3 2.7 %collective-permute-done.8.refs_6_.refs_3_ = bf16[32,2944]{1,0:T(8,128)(2,1)S(1)} collective-permute-done((bf16[32,2944]{1,0:T(8,128)(2,1)S(1)}, bf16[32,2944]{1,0:T(8,128)(2,1)S(1)}, u32[]{:S(2)}, u32[]{:S(2)}) %collective-permute-start.8) | collective-permute-done | bytes 188448 | tf_op jit(solution)/shard_map/ppermute | solution.py:48
  58.6 9.5 %collective-permute-done.13.refs_1_ = bf16[64,2944]{1,0:T(8,128)(2,1)S(1)} collective-permute-done((bf16[64,2944]{1,0:T(8,128)(2,1)S(1)}, bf16[64,2944]{1,0:T(8,128)(2,1)S(1)}, u32[]{:S(2)}, u32[]{:S(2)}) %collective-permute-start.13) | collective-permute-done | bytes 376864 | tf_op jit(solution)/shard_map/ppermute | solution.py:48
  71.1 6.5 %collective-permute-done.5.refs_3_ = bf16[32,2944]{1,0:T(8,128)(2,1)S(1)} collective-permute-done((bf16[32,2944]{1,0:T(8,128)(2,1)S(1)}, bf16[32,2944]{1,0:T(8,128)(2,1)S(1)}, u32[]{:S(2)}, u32[]{:S(2)}) %collective-permute-start.5) | collective-permute-done | bytes 188448 | tf_op jit(solution)/shard_map/ppermute | solution.py:48
  80.6 2.8 %collective-permute-done.10.refs_1_ = bf16[256,2944]{1,0:T(8,128)(2,1)} collective-permute-done((bf16[256,2944]{1,0:T(8,128)(2,1)S(1)}, bf16[256,2944]{1,0:T(8,128)(2,1)}, u32[]{:S(2)}, u32[]{:S(2)}) %collective-permute-start.10) | collective-permute-done | bytes 1507360 | tf_op jit(solution)/shard_map/ppermute | solution.py:48
  83.3 2.2 %collective-permute-done.16.refs_3_ = bf16[256,2944]{1,0:T(8,128)(2,1)} collective-permute-done((bf16[256,2944]{1,0:T(8,128)(2,1)S(1)}, bf16[256,2944]{1,0:T(8,128)(2,1)}, u32[]{:S(2)}, u32[]{:S(2)}) %collective-permute-start.16) | collective-permute-done | bytes 1507360 | tf_op jit(solution)/shard_map/ppermute | solution.py:48
  85.5 40.4 %shard_map.105 = (bf16[256,2944]{1,0:T(8,128)(2,1)S(1)}, bf16[256,2944]{1,0:T(8,128)(2,1)S(1)}, bf16[256,2944]{1,0:T(8,128)(2,1)S(1)}, bf16[256,2944]{1,0:T(8,128)(2,1)S(1)}) custom-call(s32[1]{0:T(128)} %bitcast.16.first_ref, bf16[256,2944]{1,0:T(8,128)(2,1)S(1)} %shard_map.101.refs_0_, bf16[256,2944]{1,0:T(8,128)(2,1)} %collective-permute-done.10.refs_1_, ...), custom_call_target="tpu_custom_call" | custom-call | flops 12740198400 | bytes 49766400 | tf_op jit(solution)/shard_map/pallas_call | solution.py:268
  126.5 2.8 %collective-permute-done.19.refs_1_ = bf16[256,2944]{1,0:T(8,128)(2,1)S(1)} collective-permute-done((bf16[256,2944]{1,0:T(8,128)(2,1)S(1)}, bf16[256,2944]{1,0:T(8,128)(2,1)S(1)}, u32[]{:S(2)}, u32[]{:S(2)}) %collective-permute-start.19) | collective-permute-done | bytes 1507360 | tf_op jit(solution)/shard_map/ppermute | solution.py:48
  132.9 4.4 %collective-permute-done.22.refs_1_ = bf16[64,2944]{1,0:T(8,128)(2,1)S(1)} collective-permute-done((bf16[64,2944]{1,0:T(8,128)(2,1)S(1)}, bf16[64,2944]{1,0:T(8,128)(2,1)S(1)}, u32[]{:S(2)}, u32[]{:S(2)}) %collective-permute-start.22) | collective-permute-done | bytes 376864 | tf_op jit(solution)/shard_map/ppermute | solution.py:48
  139.4 5.7 %collective-permute-done.23.refs_1_ = bf16[32,2944]{1,0:T(8,128)(2,1)S(1)} collective-permute-done((bf16[32,2944]{1,0:T(8,128)(2,1)S(1)}, bf16[32,2944]{1,0:T(8,128)(2,1)S(1)}, u32[]{:S(2)}, u32[]{:S(2)}) %collective-permute-start.23) | collective-permute-done | bytes 188448 | tf_op jit(solution)/shard_map/ppermute | solution.py:48
  146.7 2.1 %collective-permute-start.18 = (bf16[64,2944]{1,0:T(8,128)(2,1)S(1)}, bf16[64,2944]{1,0:T(8,128)(2,1)S(1)}, u32[]{:S(2)}, u32[]{:S(2)}) collective-permute-start(bf16[64,2944]{1,0:T(8,128)(2,1)S(1)} %get-tuple-element.28), channel_id=1, source_target_pairs={{0,4},{1,3},{2,6},{3,1},{4,0},{5,7},{6,2},{7,5},{8,12},{9,11},{10,... | collective-permute-start | bytes 1130504 | tf_op jit(solution)/shard_map/ppermute | solution.py:48
  148.8 4.1 %collective-permute-done.24.refs_1_ = bf16[32,2944]{1,0:T(8,128)(2,1)S(1)} collective-permute-done((bf16[32,2944]{1,0:T(8,128)(2,1)S(1)}, bf16[32,2944]{1,0:T(8,128)(2,1)S(1)}, u32[]{:S(2)}, u32[]{:S(2)}) %collective-permute-start.24) | collective-permute-done | bytes 188448 | tf_op jit(solution)/shard_map/ppermute | solution.py:48
  154.9 2.8 %collective-permute-start.27 = (bf16[32,2944]{1,0:T(8,128)(2,1)S(1)}, bf16[32,2944]{1,0:T(8,128)(2,1)S(1)}, u32[]{:S(2)}, u32[]{:S(2)}) collective-permute-start(bf16[32,2944]{1,0:T(8,128)(2,1)S(1)} %shard_map.111.refs_2_), channel_id=1, source_target_pairs={{0,16},{1,17},{2,18},{3,19},{4,20},{5,21},{6,22},{7,23},{8,24},{9,... | collective-permute-start | bytes 565256 | tf_op jit(solution)/shard_map/ppermute | solution.py:48
  158.8 2.9 %collective-permute-done.27.refs_3_ = bf16[32,2944]{1,0:T(8,128)(2,1)S(1)} collective-permute-done((bf16[32,2944]{1,0:T(8,128)(2,1)S(1)}, bf16[32,2944]{1,0:T(8,128)(2,1)S(1)}, u32[]{:S(2)}, u32[]{:S(2)}) %collective-permute-start.27) | collective-permute-done | bytes 188448 | tf_op jit(solution)/shard_map/ppermute | solution.py:48
  163.3 5.4 %collective-permute-start.29 = (bf16[32,2944]{1,0:T(8,128)(2,1)S(1)}, bf16[32,2944]{1,0:T(8,128)(2,1)S(1)}, u32[]{:S(2)}, u32[]{:S(2)}) collective-permute-start(bf16[32,2944]{1,0:T(8,128)(2,1)S(1)} %shard_map.113.refs_2_), channel_id=1, source_target_pairs={{0,8},{1,9},{2,10},{3,11},{4,12},{5,13},{6,14},{7,15},{8,0},{9,1},... | collective-permute-start | bytes 565256 | tf_op jit(solution)/shard_map/ppermute | solution.py:48
  168.8 3.5 %collective-permute-done.29 = bf16[32,2944]{1,0:T(8,128)(2,1)S(1)} collective-permute-done((bf16[32,2944]{1,0:T(8,128)(2,1)S(1)}, bf16[32,2944]{1,0:T(8,128)(2,1)S(1)}, u32[]{:S(2)}, u32[]{:S(2)}) %collective-permute-start.29) | collective-permute-done | bytes 188448 | tf_op jit(solution)/shard_map/ppermute | solution.py:48
  (94 shorter events, 38.3 us)
Async XLA Ops:
  6.6 6.8 %collective-permute-start = (bf16[128,2,128]{0,2,1:T(8,128)(2,1)S(1)}, bf16[128,2,128]{0,2,1:T(8,128)(2,1)S(1)}, u32[]{:S(2)}, u32[]{:S(2)}) collective-permute-start(bf16[128,2,128]{0,2,1:T(8,128)(2,1)S(1)} %pad_maximum_fusion.1), channel_id=1, source_target_pairs={{0,4},{4,8},{8,12},{12,16},{16,20},{20,24},{24,28},{1,5},{5,9},{9,... | collective-permute-start | bytes 196616 | tf_op jit(solution)/shard_map/ppermute | solution.py:25
  25.8 6.8 %collective-permute-start.2 = (bf16[32,2880]{1,0:T(8,128)(2,1)S(1)}, bf16[32,2880]{1,0:T(8,128)(2,1)S(1)}, u32[]{:S(2)}, u32[]{:S(2)}) collective-permute-start(bf16[32,2880]{1,0:T(8,128)(2,1)S(1)} %fusion.32), channel_id=1, source_target_pairs={{0,2},{1,3},{2,0},{3,1},{4,6},{5,7},{6,4},{7,5},{8,10},{9,11},{10,... | collective-permute-start | bytes 552968 | tf_op jit(solution)/shard_map/ppermute | solution.py:48
  33.0 12.7 %collective-permute-start.6 = (bf16[32,2944]{1,0:T(8,128)(2,1)S(1)}, bf16[32,2944]{1,0:T(8,128)(2,1)S(1)}, u32[]{:S(2)}, u32[]{:S(2)}) collective-permute-start(bf16[32,2944]{1,0:T(8,128)(2,1)S(1)} %pad_maximum_fusion.refs_0_), channel_id=1, source_target_pairs={{0,16},{1,17},{2,18},{3,19},{4,20},{5,21},{6,22},{7,23},{8,24},{9,... | collective-permute-start | bytes 565256 | tf_op jit(solution)/shard_map/ppermute | solution.py:48
  37.4 12.0 %collective-permute-start.4 = (bf16[32,2944]{1,0:T(8,128)(2,1)S(1)}, bf16[32,2944]{1,0:T(8,128)(2,1)S(1)}, u32[]{:S(2)}, u32[]{:S(2)}) collective-permute-start(bf16[32,2944]{1,0:T(8,128)(2,1)S(1)} %pad_maximum_fusion.refs_0_), channel_id=1, source_target_pairs={{0,4},{1,3},{2,6},{3,1},{4,0},{5,7},{6,2},{7,5},{8,12},{9,11},{10,... | collective-permute-start | bytes 565256 | tf_op jit(solution)/shard_map/ppermute | solution.py:48
  38.0 11.3 %collective-permute-start.3 = (bf16[32,2944]{1,0:T(8,128)(2,1)S(1)}, bf16[32,2944]{1,0:T(8,128)(2,1)S(1)}, u32[]{:S(2)}, u32[]{:S(2)}) collective-permute-start(bf16[32,2944]{1,0:T(8,128)(2,1)S(1)} %pad_maximum_fusion.refs_0_), channel_id=1, source_target_pairs={{0,2},{1,5},{2,0},{3,7},{4,6},{5,1},{6,4},{7,3},{8,10},{9,13},{10,... | collective-permute-start | bytes 565256 | tf_op jit(solution)/shard_map/ppermute | solution.py:48
  39.5 12.1 %collective-permute-start.11 = (bf16[32,2944]{1,0:T(8,128)(2,1)S(1)}, bf16[32,2944]{1,0:T(8,128)(2,1)S(1)}, u32[]{:S(2)}, u32[]{:S(2)}) collective-permute-start(bf16[32,2944]{1,0:T(8,128)(2,1)S(1)} %pad_maximum_fusion.refs_0_), channel_id=1, source_target_pairs={{0,8},{1,9},{2,10},{3,11},{4,12},{5,13},{6,14},{7,15},{8,0},{9,1},... | collective-permute-start | bytes 565256 | tf_op jit(solution)/shard_map/ppermute | solution.py:48
  45.7 8.6 %collective-permute-start.12 = (bf16[32,2944]{1,0:T(8,128)(2,1)S(1)}, bf16[32,2944]{1,0:T(8,128)(2,1)S(1)}, u32[]{:S(2)}, u32[]{:S(2)}) collective-permute-start(bf16[32,2944]{1,0:T(8,128)(2,1)S(1)} %shard_map.102), channel_id=1, source_target_pairs={{0,24},{1,25},{2,26},{3,27},{4,28},{5,29},{6,30},{7,31},{8,16},{9,... | collective-permute-start | bytes 565256 | tf_op jit(solution)/shard_map/ppermute | solution.py:48
  49.3 7.6 %collective-permute-start.8 = (bf16[32,2944]{1,0:T(8,128)(2,1)S(1)}, bf16[32,2944]{1,0:T(8,128)(2,1)S(1)}, u32[]{:S(2)}, u32[]{:S(2)}) collective-permute-start(bf16[32,2944]{1,0:T(8,128)(2,1)S(1)} %shard_map.100.refs_4_), channel_id=1, source_target_pairs={{0,4},{1,3},{2,6},{3,1},{4,0},{5,7},{6,2},{7,5},{8,12},{9,11},{10,... | collective-permute-start | bytes 565256 | tf_op jit(solution)/shard_map/ppermute | solution.py:48
  50.0 6.9 %collective-permute-start.7 = (bf16[32,2944]{1,0:T(8,128)(2,1)S(1)}, bf16[32,2944]{1,0:T(8,128)(2,1)S(1)}, u32[]{:S(2)}, u32[]{:S(2)}) collective-permute-start(bf16[32,2944]{1,0:T(8,128)(2,1)S(1)} %shard_map.100.refs_4_), channel_id=1, source_target_pairs={{0,2},{1,5},{2,0},{3,7},{4,6},{5,1},{6,4},{7,3},{8,10},{9,13},{10,... | collective-permute-start | bytes 565256 | tf_op jit(solution)/shard_map/ppermute | solution.py:48
  57.0 11.1 %collective-permute-start.13 = (bf16[64,2944]{1,0:T(8,128)(2,1)S(1)}, bf16[64,2944]{1,0:T(8,128)(2,1)S(1)}, u32[]{:S(2)}, u32[]{:S(2)}) collective-permute-start(bf16[64,2944]{1,0:T(8,128)(2,1)S(1)} %shard_map.103.refs_0_), channel_id=1, source_target_pairs={{0,2},{1,5},{2,0},{3,7},{4,6},{5,1},{6,4},{7,3},{8,10},{9,13},{10,... | collective-permute-start | bytes 1130504 | tf_op jit(solution)/shard_map/ppermute | solution.py:48
  57.6 22.3 %collective-permute-start.14 = (bf16[64,2944]{1,0:T(8,128)(2,1)S(1)}, bf16[64,2944]{1,0:T(8,128)(2,1)S(1)}, u32[]{:S(2)}, u32[]{:S(2)}) collective-permute-start(bf16[64,2944]{1,0:T(8,128)(2,1)S(1)} %shard_map.103.refs_0_), channel_id=1, source_target_pairs={{0,4},{1,3},{2,6},{3,1},{4,0},{5,7},{6,2},{7,5},{8,12},{9,11},{10,... | collective-permute-start | bytes 1130504 | tf_op jit(solution)/shard_map/ppermute | solution.py:48
  68.1 11.8 %collective-permute-start.15 = (bf16[64,2944]{1,0:T(8,128)(2,1)S(1)}, bf16[64,2944]{1,0:T(8,128)(2,1)S(1)}, u32[]{:S(2)}, u32[]{:S(2)}) collective-permute-start(bf16[64,2944]{1,0:T(8,128)(2,1)S(1)} %collective-permute-done.13.refs_1_), channel_id=1, source_target_pairs={{0,4},{1,3},{2,6},{3,1},{4,0},{5,7},{6,2},{7,5},{8,12},{9,11},{10,... | collective-permute-start | bytes 1130504 | tf_op jit(solution)/shard_map/ppermute | solution.py:48
  69.1 8.6 %collective-permute-start.5 = (bf16[32,2944]{1,0:T(8,128)(2,1)S(1)}, bf16[32,2944]{1,0:T(8,128)(2,1)S(1)}, u32[]{:S(2)}, u32[]{:S(2)}) collective-permute-start(bf16[32,2944]{1,0:T(8,128)(2,1)S(1)} %collective-permute-done.3.refs_1_), channel_id=1, source_target_pairs={{0,4},{1,3},{2,6},{3,1},{4,0},{5,7},{6,2},{7,5},{8,12},{9,11},{10,... | collective-permute-start | bytes 565256 | tf_op jit(solution)/shard_map/ppermute | solution.py:48
  70.1 9.6 %collective-permute-start.9 = (bf16[32,2944]{1,0:T(8,128)(2,1)S(1)}, bf16[32,2944]{1,0:T(8,128)(2,1)S(1)}, u32[]{:S(2)}, u32[]{:S(2)}) collective-permute-start(bf16[32,2944]{1,0:T(8,128)(2,1)S(1)} %collective-permute-done.7.refs_5_.refs_2_), channel_id=1, source_target_pairs={{0,4},{1,3},{2,6},{3,1},{4,0},{5,7},{6,2},{7,5},{8,12},{9,11},{10,... | collective-permute-start | bytes 565256 | tf_op jit(solution)/shard_map/ppermute | solution.py:48
  129.6 7.7 %collective-permute-start.22 = (bf16[64,2944]{1,0:T(8,128)(2,1)S(1)}, bf16[64,2944]{1,0:T(8,128)(2,1)S(1)}, u32[]{:S(2)}, u32[]{:S(2)}) collective-permute-start(bf16[64,2944]{1,0:T(8,128)(2,1)S(1)} %get-tuple-element.36), channel_id=1, source_target_pairs={{0,4},{1,3},{2,6},{3,1},{4,0},{5,7},{6,2},{7,5},{8,12},{9,11},{10,... | collective-permute-start | bytes 1130504 | tf_op jit(solution)/shard_map/ppermute | solution.py:48
  131.8 13.4 %collective-permute-start.21 = (bf16[64,2944]{1,0:T(8,128)(2,1)S(1)}, bf16[64,2944]{1,0:T(8,128)(2,1)S(1)}, u32[]{:S(2)}, u32[]{:S(2)}) collective-permute-start(bf16[64,2944]{1,0:T(8,128)(2,1)S(1)} %get-tuple-element.34), channel_id=1, source_target_pairs={{0,4},{1,3},{2,6},{3,1},{4,0},{5,7},{6,2},{7,5},{8,12},{9,11},{10,... | collective-permute-start | bytes 1130504 | tf_op jit(solution)/shard_map/ppermute | solution.py:48
  137.4 7.7 %collective-permute-start.23 = (bf16[32,2944]{1,0:T(8,128)(2,1)S(1)}, bf16[32,2944]{1,0:T(8,128)(2,1)S(1)}, u32[]{:S(2)}, u32[]{:S(2)}) collective-permute-start(bf16[32,2944]{1,0:T(8,128)(2,1)S(1)} %get-tuple-element.38), channel_id=1, source_target_pairs={{0,2},{1,5},{2,0},{3,7},{4,6},{5,1},{6,4},{7,3},{8,10},{9,13},{10,... | collective-permute-start | bytes 565256 | tf_op jit(solution)/shard_map/ppermute | solution.py:48
  137.7 15.3 %collective-permute-start.20 = (bf16[64,2944]{1,0:T(8,128)(2,1)S(1)}, bf16[64,2944]{1,0:T(8,128)(2,1)S(1)}, u32[]{:S(2)}, u32[]{:S(2)}) collective-permute-start(bf16[64,2944]{1,0:T(8,128)(2,1)S(1)} %get-tuple-element.32), channel_id=1, source_target_pairs={{0,4},{1,3},{2,6},{3,1},{4,0},{5,7},{6,2},{7,5},{8,12},{9,11},{10,... | collective-permute-start | bytes 1130504 | tf_op jit(solution)/shard_map/ppermute | solution.py:48
  145.2 7.7 %collective-permute-start.24 = (bf16[32,2944]{1,0:T(8,128)(2,1)S(1)}, bf16[32,2944]{1,0:T(8,128)(2,1)S(1)}, u32[]{:S(2)}, u32[]{:S(2)}) collective-permute-start(bf16[32,2944]{1,0:T(8,128)(2,1)S(1)} %get-tuple-element.40), channel_id=1, source_target_pairs={{0,2},{1,5},{2,0},{3,7},{4,6},{5,1},{6,4},{7,3},{8,10},{9,13},{10,... | collective-permute-start | bytes 565256 | tf_op jit(solution)/shard_map/ppermute | solution.py:48
  145.5 7.5 %collective-permute-start.25 = (bf16[32,2944]{1,0:T(8,128)(2,1)S(1)}, bf16[32,2944]{1,0:T(8,128)(2,1)S(1)}, u32[]{:S(2)}, u32[]{:S(2)}) collective-permute-start(bf16[32,2944]{1,0:T(8,128)(2,1)S(1)} %shard_map.109.refs_2_), channel_id=1, source_target_pairs={{0,24},{1,25},{2,26},{3,27},{4,28},{5,29},{6,30},{7,31},{8,16},{9,... | collective-permute-start | bytes 565256 | tf_op jit(solution)/shard_map/ppermute | solution.py:48
  146.7 12.1 %collective-permute-start.18 = (bf16[64,2944]{1,0:T(8,128)(2,1)S(1)}, bf16[64,2944]{1,0:T(8,128)(2,1)S(1)}, u32[]{:S(2)}, u32[]{:S(2)}) collective-permute-start(bf16[64,2944]{1,0:T(8,128)(2,1)S(1)} %get-tuple-element.28), channel_id=1, source_target_pairs={{0,4},{1,3},{2,6},{3,1},{4,0},{5,7},{6,2},{7,5},{8,12},{9,11},{10,... | collective-permute-start | bytes 1130504 | tf_op jit(solution)/shard_map/ppermute | solution.py:48
  154.9 6.7 %collective-permute-start.27 = (bf16[32,2944]{1,0:T(8,128)(2,1)S(1)}, bf16[32,2944]{1,0:T(8,128)(2,1)S(1)}, u32[]{:S(2)}, u32[]{:S(2)}) collective-permute-start(bf16[32,2944]{1,0:T(8,128)(2,1)S(1)} %shard_map.111.refs_2_), channel_id=1, source_target_pairs={{0,16},{1,17},{2,18},{3,19},{4,20},{5,21},{6,22},{7,23},{8,24},{9,... | collective-permute-start | bytes 565256 | tf_op jit(solution)/shard_map/ppermute | solution.py:48
  161.7 7.0 %collective-permute-start.28 = (bf16[32,2944]{1,0:T(8,128)(2,1)S(1)}, bf16[32,2944]{1,0:T(8,128)(2,1)S(1)}, u32[]{:S(2)}, u32[]{:S(2)}) collective-permute-start(bf16[32,2944]{1,0:T(8,128)(2,1)S(1)} %get-tuple-element.44), channel_id=1, source_target_pairs={{0,2},{1,5},{2,0},{3,7},{4,6},{5,1},{6,4},{7,3},{8,10},{9,13},{10,... | collective-permute-start | bytes 565256 | tf_op jit(solution)/shard_map/ppermute | solution.py:48
  163.3 8.9 %collective-permute-start.29 = (bf16[32,2944]{1,0:T(8,128)(2,1)S(1)}, bf16[32,2944]{1,0:T(8,128)(2,1)S(1)}, u32[]{:S(2)}, u32[]{:S(2)}) collective-permute-start(bf16[32,2944]{1,0:T(8,128)(2,1)S(1)} %shard_map.113.refs_2_), channel_id=1, source_target_pairs={{0,8},{1,9},{2,10},{3,11},{4,12},{5,13},{6,14},{7,15},{8,0},{9,1},... | collective-permute-start | bytes 565256 | tf_op jit(solution)/shard_map/ppermute | solution.py:48
  (11 other events, 63.3 us)

commit v3 on v1

--- a/solution.py
+++ b/solution.py
@@ -61,27 +61,31 @@
 SMALL_KERNEL = 8 << 20
 
 
-def join_kernel(*refs):
-    parts, out_ref = refs[:-1], refs[-1]
-    rows = parts[0].shape[0]
-    for place, part in enumerate(parts):
-        out_ref[place * rows : (place + 1) * rows, :] = part[...]
-
-
-def join(parts):
+def join_kernel(count, pieces, *refs):
+    parts, out_ref = refs[:count], refs[-1]
+    rows = parts[0].shape[0] // pieces
+    for piece in range(pieces):
+        for place, part in enumerate(parts):
+            start = (piece * count + place) * rows
+            out_ref[start : start + rows, :] = part[piece * rows : (piece + 1) * rows, :]
+
+
+def join(parts, pieces=1, after=()):
     rows, width = parts[0].shape
     return pl.pallas_call(
-        join_kernel,
+        functools.partial(join_kernel, len(parts), pieces),
+        in_specs=[pl.BlockSpec(memory_space=pltpu.VMEM)] * len(parts)
+        + [pl.BlockSpec(memory_space=pl.ANY)] * len(after),
         out_shape=jax.ShapeDtypeStruct((len(parts) * rows, width), parts[0].dtype),
         compiler_params=pltpu.CompilerParams(vmem_limit_bytes=SMALL_KERNEL),
         cost_estimate=pl.CostEstimate(
             flops=0, bytes_accessed=4 * len(parts) * rows * width, transcendentals=0
         ),
-    )(*parts)
-
-
-def fold_kernel(count, *refs):
-    terms, outs = refs[:count], refs[count:]
+    )(*parts, *after)
+
+
+def fold_kernel(count, outs_n, *refs):
+    terms, outs = refs[:count], refs[len(refs) - outs_n :]
     rows = outs[0].shape[0]
     for place, out_ref in enumerate(outs):
         cut = slice(place * rows, (place + 1) * rows)
@@ -91,30 +95,27 @@
         out_ref[...] = total.astype(out_ref.dtype)
 
 
-def fold(terms, parts, first=jnp.float32):
+def fold(terms, kinds, after=()):
     rows, width = terms[0].shape
-    rows = rows // parts
-    kinds = [first] + [jnp.bfloat16] * (parts - 1)
+    rows = rows // len(kinds)
     return pl.pallas_call(
-        functools.partial(fold_kernel, len(terms)),
+        functools.partial(fold_kernel, len(terms), len(kinds)),
+        in_specs=[pl.BlockSpec(memory_space=pltpu.VMEM)] * len(terms)
+        + [pl.BlockSpec(memory_space=pl.ANY)] * len(after),
         out_shape=[jax.ShapeDtypeStruct((rows, width), kind) for kind in kinds],
         compiler_params=pltpu.CompilerParams(vmem_limit_bytes=SMALL_KERNEL),
         cost_estimate=pl.CostEstimate(
-            flops=len(terms) * rows * parts * width,
-            bytes_accessed=4 * len(terms) * rows * parts * width,
+            flops=len(terms) * rows * len(kinds) * width,
+            bytes_accessed=4 * len(terms) * rows * len(kinds) * width,
             transcendentals=0,
         ),
-    )(*terms)
-
-
-def collect(kept, arrived, steps, last, first):
-    terms = [kept, arrived]
-    for size, even, odd in reversed(steps):
-        parts = fold(terms, size)
-        terms = [parts[0]] + [
-            swap(parts[other], other * even, other * odd) for other in range(1, size)
-        ]
-    return fold(terms, last, first)
+    )(*terms, *after)
+
+
+def send_parts(parts, even, odd):
+    return [parts[0]] + [
+        swap(part, other * even, other * odd) for other, part in enumerate(parts[1:], 1)
+    ]
 
 
 def expert_kernel(sizes, first_ref, *refs):
@@ -199,12 +200,13 @@
             down_copy(expert + 1).start()
         gate_up_copy(expert).wait()
         rows = packed_ref[expert]
-        gate = lax.dot_general(
-            rows, gate_up_buf[held, 0], contract, preferred_element_type=jnp.float32
+        both = lax.dot_general(
+            rows,
+            gate_up_buf[held].reshape(2 * units, width),
+            contract,
+            preferred_element_type=jnp.float32,
         )
-        up = lax.dot_general(
-            rows, gate_up_buf[held, 1], contract, preferred_element_type=jnp.float32
-        )
+        gate, up = both[:, :units], both[:, units:]
         act = gate / (1.0 + jnp.exp(-gate)) * up * gate_ref[expert][:, :1]
         act = act.astype(jnp.bfloat16)
         down_copy(expert).wait()
@@ -332,8 +334,8 @@
     place = lax.axis_index("tp") // 2
     attn_out = lax.dynamic_index_in_dim(kept, place, 0, False)
     for other in range(1, across):
-        part = lax.dynamic_index_in_dim(kept, place ^ other, 0, False).astype(jnp.bfloat16)
-        attn_out = attn_out + swap(part, 2 * other, 2 * other).astype(jnp.float32)
+        handed_on = lax.dynamic_index_in_dim(kept, place ^ other, 0, False).astype(jnp.bfloat16)
+        attn_out = attn_out + swap(handed_on, 2 * other, 2 * other).astype(jnp.float32)
     own_start = lax.axis_index("tp") * block_rows
     residual = (
         lax.dynamic_slice_in_dim(stream_in, own_start, block_rows, 0).astype(jnp.float32) + attn_out
@@ -347,25 +349,47 @@
     low = lax.reduce_precision(gate_weight - high - middle, 8, 7)
     routing = jnp.concatenate([expert_index.astype(jnp.float32), high, middle, low], axis=1)
     routing = jnp.pad(routing, ((0, 0), (0, ROUTING - 4 * TOPK))).astype(jnp.bfloat16)
+    gate_up = jnp.transpose(w_gateup, (0, 2, 3, 1))
+    gate_up = pltpu.with_memory_space_constraint(gate_up, pltpu.HBM)
+    down = pltpu.with_memory_space_constraint(w_down, pltpu.HBM)
     rows = jnp.concatenate([hidden_in, routing], axis=1)
 
     (slow, slow_step, _), inner = plan[0], plan[1:]
-    held = [rows] + [swap(rows, other * slow_step, other * slow_step) for other in range(1, slow)]
-    near, far = held[: slow // 2], held[slow // 2 :]
-    near, far = [join(spread(join(pieces), inner)) for pieces in (near, far)]
-    tokens = [near, swap(near, 1, 1), far, swap(far, 1, 1)]
+    (size, even, odd), (last_size, last_even, last_odd) = inner
+    half = slow // 2
+
+    def along(value, offset):
+        return swap(value, offset * slow_step, offset * slow_step)
+
+    others = [along(rows, offset) for offset in range(1, slow)]
+    first_pieces, second_pieces = [rows] + others[: half - 1], others[half - 1 :]
+    spread_a = [spread(rows, inner)]
+    for piece in first_pieces[1:]:
+        spread_a.append(spread(join([piece], 1, spread_a[0][1:2]), inner))
+    forwards = [piece for pieces in spread_a for piece in pieces[1 : size + 1]]
+    pieces_b = spread(join(second_pieces, 1, forwards + spread_a[0][size + 1 :]), inner)
+    mine_a = join([piece for pieces in spread_a for piece in pieces])
+    mine_b = join(pieces_b, half)
+    tokens = [mine_a, swap(mine_a, 1, 1), mine_b, swap(mine_b, 1, 1)]
 
     first = (lax.axis_index("seq") * experts_dev).astype(jnp.int32).reshape(1)
-    weights = jnp.transpose(w_gateup, (0, 2, 3, 1))
-    near, near_handed, far, far_handed = run_experts(
-        first, tokens, weights, w_down, block_rows, capacity
-    )
-
-    far = collect(far, swap(far_handed, 1, 1), inner, slow // 2, jnp.bfloat16)
-    near = collect(near, swap(near_handed, 1, 1), inner, slow // 2, jnp.float32)
-    total = residual + near[0][:, :MODEL_WIDTH]
-    for other, part in enumerate(near[1:] + far, 1):
-        part = swap(part, other * slow_step, other * slow_step)
+    sums = run_experts(first, tokens, gate_up, down, block_rows, capacity)
+
+    kinds = ([jnp.float32] + [jnp.bfloat16] * (last_size - 1)) * half
+    inner_kinds = [jnp.float32] + [jnp.bfloat16] * (size - 1)
+    parts = [fold([kept, swap(handed, 1, 1)], kinds) for kept, handed in (sums[:2], sums[2:])]
+    arrived = []
+    after = []
+    for offset in list(range(slow - 1, 1, -1)) + [1, 0]:
+        place = offset % half * last_size
+        terms = send_parts(parts[offset // half][place : place + last_size], last_even, last_odd)
+        terms = send_parts(fold(terms, inner_kinds, after + arrived[-2:-1]), even, odd)
+        if offset:
+            after = list(fold(terms, [jnp.bfloat16]))
+            arrived.append(along(after[0], offset))
+        else:
+            total = residual + fold(terms, [jnp.float32], arrived[-1:])[0][:, :MODEL_WIDTH]
+    for part in arrived:
         total = total + part[:, :MODEL_WIDTH].astype(jnp.float32)
     return total.astype(jnp.bfloat16)
 

time: 162 us -> 161 us (level); the launches traced: 160 us -> 161 us
  waiting for transfers between devices: 87.9 us -> 74.7 us
  starting transfers between devices: 25.9 us -> 37.6 us
    ppermute x22 -> x29, waiting for transfers between devices: 86.4 us -> 73.2 us  [swap(): return lax.ppermute(value, ('seq', 'tp'), pairs)]
    ppermute x22 -> x29, starting transfers between devices: 21 us -> 32.7 us  [swap(): return lax.ppermute(value, ('seq', 'tp'), pairs)]
  transfers between devices with their start and end apart: 23 -> 30, of which waited for: 16 -> 20; matrix products, arithmetic and copies ran while one was open for 1% -> 1% of each run, Pallas kernels for 1% -> 1%
where the time goes in v3:
time: 161 us
  waiting for transfers between devices  74.7 us (46%)
  starting transfers between devices  37.6 us (23%)
  Pallas kernels  27.2 us (17%)
  matrix products  13.6 us (8%)
  local copies, waits for them, and re-layouts  4.18 us (3%)
  other arithmetic  2.91 us (2%)
    ppermute x29, waiting for transfers between devices, swap(): return lax.ppermute(value, ('seq', 'tp'), pairs)  73.2 us
    ppermute x29, starting transfers between devices, swap(): return lax.ppermute(value, ('seq', 'tp'), pairs)  32.7 us
    pallas_call x1, Pallas kernels, run_experts(): pl.pallas_call(functools.partial(expert_kernel, (groups, block_rows, capa...  25.9 us
    ppermute x1, starting transfers between devices, from_behind(): lax.ppermute(value, axis, [(source, source + steps) for source in range(f...  4.87 us
    dot_general x1, matrix products, local(): jnp.einsum('td,dhc->thc', normed, w_qkv, preferred_element_type=jnp.float32)  4.79 us
    dot_general x1, matrix products, local(): terms = jnp.dot(attended, w_out, preferred_element_type=jnp.float32)  4.78 us
  transfers between devices with their start and end apart: 30, of which 20 were waited for; matrix products, arithmetic and copies ran while one was open for 1% of the time, Pallas kernels for 1%

profile of v3, /device:TPU:0, one launch (start us, length us, event | category | flops | bytes accessed | tf_op | source)
XLA Modules:
  0.0 160.6 jit_solution(9354624600130323134)
XLA Ops:
  1.5 4.8 %fusion.9 = bf16[128,2,640]{2,0,1:T(8,128)(2,1)S(1)} fusion(bf16[2880,2,640]{2,1,0:T(2,128)(2,1)} %param.12, bf16[128,2880]{0,1:T(8,128)(2,1)} %param.10, f32[2880]{0:T(1024)} %param.11, f32[128]{0:T(128)S(1)} %add_rsqrt_fusion.1), kind=kOutput, calls=%fused_computation.14 | convolution fusion | flops 945356800 | bytes 8449792 | tf_op jit(solution)/shard_map/td,dhc->thc/dot_general | solution.py:298
  6.6 4.9 %collective-permute-start = (bf16[128,2,128]{0,2,1:T(8,128)(2,1)S(1)}, bf16[128,2,128]{0,2,1:T(8,128)(2,1)S(1)}, u32[]{:S(2)}, u32[]{:S(2)}) collective-permute-start(bf16[128,2,128]{0,2,1:T(8,128)(2,1)S(1)} %pad_maximum_fusion.1), channel_id=1, source_target_pairs={{0,4},{4,8},{8,12},{12,16},{16,20},{20,24},{24,28},{1,5},{5,9},{9,... | collective-permute-start | bytes 196616 | tf_op jit(solution)/shard_map/ppermute | solution.py:25
  13.4 2.1 %fusion.57 = (f32[2,8,128]{2,1,0:T(8,128)S(1)}, f32[2,8,128,256]{2,3,1,0:T(8,128)}) fusion(pred[128,256]{0,1:T(8,128)(4,1)S(1)} %fusion.35, bf16[128,2,10,64]{0,3,2,1:T(8,128)(2,1)S(1)} %bitcast.64, bf16[128,2,64]{0,2,1:T(8,128)(2,1)S(1)} %get-tuple-element.48, bf16[128,2,64]{0,2,1:T(8,128)(2,1)S(1)} %get-tuple-element.50), kind=kOutput, calls=%fused_computation.74 | convolution fusion | flops 69337344 | bytes 2465792 | tf_op jit(solution)/shard_map/sub | solution.py:272
  18.2 4.8 %fusion.3 = f32[2,2,32,2880]{3,2,1,0:T(8,128)S(1)} fusion(bf16[2,2,32,1024]{3,2,1,0:T(8,128)(2,1)S(1)} %dot_general.17, bf16[1024,2880]{0,1:T(8,128)(2,1)} %param.14), kind=kOutput, calls=%fused_computation.3 | convolution fusion | flops 754974720 | bytes 7634944 | tf_op jit(solution)/shard_map/dot_general | solution.py:328
  27.8 4.8 %collective-permute-done.2 = bf16[32,2880]{1,0:T(8,128)(2,1)S(1)} collective-permute-done((bf16[32,2880]{1,0:T(8,128)(2,1)S(1)}, bf16[32,2880]{1,0:T(8,128)(2,1)S(1)}, u32[]{:S(2)}, u32[]{:S(2)}) %collective-permute-start.2) | collective-permute-done | bytes 184352 | tf_op jit(solution)/shard_map/ppermute | solution.py:48
  33.0 3.3 %collective-permute-start.6 = (bf16[32,2944]{1,0:T(8,128)(2,1)S(1)}, bf16[32,2944]{1,0:T(8,128)(2,1)S(1)}, u32[]{:S(2)}, u32[]{:S(2)}) collective-permute-start(bf16[32,2944]{1,0:T(8,128)(2,1)S(1)} %pad_maximum_fusion.refs_0_), channel_id=1, source_target_pairs={{0,8},{1,9},{2,10},{3,11},{4,12},{5,13},{6,14},{7,15},{8,0},{9,1},... | collective-permute-start | bytes 565256 | tf_op jit(solution)/shard_map/ppermute | solution.py:48
  37.9 2.5 %collective-permute-start.12 = (bf16[32,2944]{1,0:T(8,128)(2,1)S(1)}, bf16[32,2944]{1,0:T(8,128)(2,1)S(1)}, u32[]{:S(2)}, u32[]{:S(2)}) collective-permute-start(bf16[32,2944]{1,0:T(8,128)(2,1)S(1)} %pad_maximum_fusion.refs_0_), channel_id=1, source_target_pairs={{0,24},{1,25},{2,26},{3,27},{4,28},{5,29},{6,30},{7,31},{8,16},{9,... | collective-permute-start | bytes 565256 | tf_op jit(solution)/shard_map/ppermute | solution.py:48
  45.0 3.7 %collective-permute-done.12.refs_1_ = bf16[32,2944]{1,0:T(8,128)(2,1)S(1)} collective-permute-done((bf16[32,2944]{1,0:T(8,128)(2,1)S(1)}, bf16[32,2944]{1,0:T(8,128)(2,1)S(1)}, u32[]{:S(2)}, u32[]{:S(2)}) %collective-permute-start.12) | collective-permute-done | bytes 188448 | tf_op jit(solution)/shard_map/ppermute | solution.py:48
  49.2 6.1 %collective-permute-done.11.refs_0_ = bf16[32,2944]{1,0:T(8,128)(2,1)S(1)} collective-permute-done((bf16[32,2944]{1,0:T(8,128)(2,1)S(1)}, bf16[32,2944]{1,0:T(8,128)(2,1)S(1)}, u32[]{:S(2)}, u32[]{:S(2)}) %collective-permute-start.11) | collective-permute-done | bytes 188448 | tf_op jit(solution)/shard_map/ppermute | solution.py:48
  58.3 8.8 %collective-permute-done.13.refs_1_ = bf16[64,2944]{1,0:T(8,128)(2,1)S(1)} collective-permute-done((bf16[64,2944]{1,0:T(8,128)(2,1)S(1)}, bf16[64,2944]{1,0:T(8,128)(2,1)S(1)}, u32[]{:S(2)}, u32[]{:S(2)}) %collective-permute-start.13) | collective-permute-done | bytes 376864 | tf_op jit(solution)/shard_map/ppermute | solution.py:48
  67.1 2.0 %collective-permute-start.9 = (bf16[32,2944]{1,0:T(8,128)(2,1)S(1)}, bf16[32,2944]{1,0:T(8,128)(2,1)S(1)}, u32[]{:S(2)}, u32[]{:S(2)}) collective-permute-start(bf16[32,2944]{1,0:T(8,128)(2,1)S(1)} %collective-permute-done.7.refs_5_.refs_4_), channel_id=1, source_target_pairs={{0,4},{1,3},{2,6},{3,1},{4,0},{5,7},{6,2},{7,5},{8,12},{9,11},{10,... | collective-permute-start | bytes 565256 | tf_op jit(solution)/shard_map/ppermute | solution.py:48
  69.2 7.6 %collective-permute-done.9.refs_7_ = bf16[32,2944]{1,0:T(8,128)(2,1)S(1)} collective-permute-done((bf16[32,2944]{1,0:T(8,128)(2,1)S(1)}, bf16[32,2944]{1,0:T(8,128)(2,1)S(1)}, u32[]{:S(2)}, u32[]{:S(2)}) %collective-permute-start.9) | collective-permute-done | bytes 188448 | tf_op jit(solution)/shard_map/ppermute | solution.py:48
  77.6 2.7 %collective-permute-done.10.refs_1_ = bf16[256,2944]{1,0:T(8,128)(2,1)} collective-permute-done((bf16[256,2944]{1,0:T(8,128)(2,1)S(1)}, bf16[256,2944]{1,0:T(8,128)(2,1)}, u32[]{:S(2)}, u32[]{:S(2)}) %collective-permute-start.10) | collective-permute-done | bytes 1507360 | tf_op jit(solution)/shard_map/ppermute | solution.py:48
  80.4 2.2 %collective-permute-done.16.refs_3_ = bf16[256,2944]{1,0:T(8,128)(2,1)} collective-permute-done((bf16[256,2944]{1,0:T(8,128)(2,1)S(1)}, bf16[256,2944]{1,0:T(8,128)(2,1)}, u32[]{:S(2)}, u32[]{:S(2)}) %collective-permute-start.16) | collective-permute-done | bytes 1507360 | tf_op jit(solution)/shard_map/ppermute | solution.py:48
  82.5 25.9 %shard_map.104 = (bf16[256,2944]{1,0:T(8,128)(2,1)S(1)}, bf16[256,2944]{1,0:T(8,128)(2,1)}, bf16[256,2944]{1,0:T(8,128)(2,1)}, bf16[256,2944]{1,0:T(8,128)(2,1)}) custom-call(s32[1]{0:T(128)} %bitcast.16.first_ref, bf16[256,2944]{1,0:T(8,128)(2,1)} %copy-done, bf16[256,2944]{1,0:T(8,128)(2,1)} %collective-permute-done.10.refs_1_, ...), custom_call_target="tpu_custom_call" | custom-call | flops 12740198400 | bytes 49766400 | tf_op jit(solution)/shard_map/pallas_call | solution.py:233
  109.0 3.0 %collective-permute-done.20.refs_1_ = bf16[256,2944]{1,0:T(8,128)(2,1)S(1)} collective-permute-done((bf16[256,2944]{1,0:T(8,128)(2,1)}, bf16[256,2944]{1,0:T(8,128)(2,1)S(1)}, u32[]{:S(2)}, u32[]{:S(2)}) %collective-permute-start.20) | collective-permute-done | bytes 1507360 | tf_op jit(solution)/shard_map/ppermute | solution.py:48
  113.8 2.0 %collective-permute-start.21 = (bf16[64,2944]{1,0:T(8,128)(2,1)S(1)}, bf16[64,2944]{1,0:T(8,128)(2,1)S(1)}, u32[]{:S(2)}, u32[]{:S(2)}) collective-permute-start(bf16[64,2944]{1,0:T(8,128)(2,1)S(1)} %get-tuple-element.34), channel_id=1, source_target_pairs={{0,4},{1,3},{2,6},{3,1},{4,0},{5,7},{6,2},{7,5},{8,12},{9,11},{10,... | collective-permute-start | bytes 1130504 | tf_op jit(solution)/shard_map/ppermute | solution.py:48
  115.9 5.6 %collective-permute-done.22.refs_1_ = bf16[64,2944]{1,0:T(8,128)(2,1)S(1)} collective-permute-done((bf16[64,2944]{1,0:T(8,128)(2,1)S(1)}, bf16[64,2944]{1,0:T(8,128)(2,1)S(1)}, u32[]{:S(2)}, u32[]{:S(2)}) %collective-permute-start.22) | collective-permute-done | bytes 376864 | tf_op jit(solution)/shard_map/ppermute | solution.py:48
  123.4 5.9 %collective-permute-done.23.refs_1_ = bf16[32,2944]{1,0:T(8,128)(2,1)S(1)} collective-permute-done((bf16[32,2944]{1,0:T(8,128)(2,1)S(1)}, bf16[32,2944]{1,0:T(8,128)(2,1)S(1)}, u32[]{:S(2)}, u32[]{:S(2)}) %collective-permute-start.23) | collective-permute-done | bytes 188448 | tf_op jit(solution)/shard_map/ppermute | solution.py:48
  130.8 2.7 %collective-permute-start.25 = (bf16[32,2944]{1,0:T(8,128)(2,1)S(1)}, bf16[32,2944]{1,0:T(8,128)(2,1)S(1)}, u32[]{:S(2)}, u32[]{:S(2)}) collective-permute-start(bf16[32,2944]{1,0:T(8,128)(2,1)S(1)} %shard_map.108.refs_2_), channel_id=1, source_target_pairs={{0,24},{1,25},{2,26},{3,27},{4,28},{5,29},{6,30},{7,31},{8,16},{9,... | collective-permute-start | bytes 565256 | tf_op jit(solution)/shard_map/ppermute | solution.py:48
  133.5 3.5 %collective-permute-done.24.refs_1_ = bf16[32,2944]{1,0:T(8,128)(2,1)S(1)} collective-permute-done((bf16[32,2944]{1,0:T(8,128)(2,1)S(1)}, bf16[32,2944]{1,0:T(8,128)(2,1)S(1)}, u32[]{:S(2)}, u32[]{:S(2)}) %collective-permute-start.24) | collective-permute-done | bytes 188448 | tf_op jit(solution)/shard_map/ppermute | solution.py:48
  139.1 4.8 %collective-permute-start.27 = (bf16[32,2944]{1,0:T(8,128)(2,1)S(1)}, bf16[32,2944]{1,0:T(8,128)(2,1)S(1)}, u32[]{:S(2)}, u32[]{:S(2)}) collective-permute-start(bf16[32,2944]{1,0:T(8,128)(2,1)S(1)} %shard_map.110.refs_2_), channel_id=1, source_target_pairs={{0,16},{1,17},{2,18},{3,19},{4,20},{5,21},{6,22},{7,23},{8,24},{9,... | collective-permute-start | bytes 565256 | tf_op jit(solution)/shard_map/ppermute | solution.py:48
  144.1 8.5 %collective-permute-done.27.refs_3_ = bf16[32,2944]{1,0:T(8,128)(2,1)S(1)} collective-permute-done((bf16[32,2944]{1,0:T(8,128)(2,1)S(1)}, bf16[32,2944]{1,0:T(8,128)(2,1)S(1)}, u32[]{:S(2)}, u32[]{:S(2)}) %collective-permute-start.27) | collective-permute-done | bytes 188448 | tf_op jit(solution)/shard_map/ppermute | solution.py:48
  154.2 4.2 %collective-permute-done.28.refs_1_ = bf16[32,2944]{1,0:T(8,128)(2,1)S(1)} collective-permute-done((bf16[32,2944]{1,0:T(8,128)(2,1)S(1)}, bf16[32,2944]{1,0:T(8,128)(2,1)S(1)}, u32[]{:S(2)}, u32[]{:S(2)}) %collective-permute-start.28) | collective-permute-done | bytes 188448 | tf_op jit(solution)/shard_map/ppermute | solution.py:48
  (99 shorter events, 33.8 us)
Async XLA Ops:
  6.6 6.8 %collective-permute-start = (bf16[128,2,128]{0,2,1:T(8,128)(2,1)S(1)}, bf16[128,2,128]{0,2,1:T(8,128)(2,1)S(1)}, u32[]{:S(2)}, u32[]{:S(2)}) collective-permute-start(bf16[128,2,128]{0,2,1:T(8,128)(2,1)S(1)} %pad_maximum_fusion.1), channel_id=1, source_target_pairs={{0,4},{4,8},{8,12},{12,16},{16,20},{20,24},{24,28},{1,5},{5,9},{9,... | collective-permute-start | bytes 196616 | tf_op jit(solution)/shard_map/ppermute | solution.py:25
  25.8 6.8 %collective-permute-start.2 = (bf16[32,2880]{1,0:T(8,128)(2,1)S(1)}, bf16[32,2880]{1,0:T(8,128)(2,1)S(1)}, u32[]{:S(2)}, u32[]{:S(2)}) collective-permute-start(bf16[32,2880]{1,0:T(8,128)(2,1)S(1)} %fusion.32), channel_id=1, source_target_pairs={{0,2},{1,3},{2,0},{3,1},{4,6},{5,7},{6,4},{7,5},{8,10},{9,11},{10,... | collective-permute-start | bytes 552968 | tf_op jit(solution)/shard_map/ppermute | solution.py:48
  33.0 8.3 %collective-permute-start.6 = (bf16[32,2944]{1,0:T(8,128)(2,1)S(1)}, bf16[32,2944]{1,0:T(8,128)(2,1)S(1)}, u32[]{:S(2)}, u32[]{:S(2)}) collective-permute-start(bf16[32,2944]{1,0:T(8,128)(2,1)S(1)} %pad_maximum_fusion.refs_0_), channel_id=1, source_target_pairs={{0,8},{1,9},{2,10},{3,11},{4,12},{5,13},{6,14},{7,15},{8,0},{9,1},... | collective-permute-start | bytes 565256 | tf_op jit(solution)/shard_map/ppermute | solution.py:48
  36.4 6.9 %collective-permute-start.3 = (bf16[32,2944]{1,0:T(8,128)(2,1)S(1)}, bf16[32,2944]{1,0:T(8,128)(2,1)S(1)}, u32[]{:S(2)}, u32[]{:S(2)}) collective-permute-start(bf16[32,2944]{1,0:T(8,128)(2,1)S(1)} %pad_maximum_fusion.refs_0_), channel_id=1, source_target_pairs={{0,2},{1,5},{2,0},{3,7},{4,6},{5,1},{6,4},{7,3},{8,10},{9,13},{10,... | collective-permute-start | bytes 565256 | tf_op jit(solution)/shard_map/ppermute | solution.py:48
  37.9 10.8 %collective-permute-start.12 = (bf16[32,2944]{1,0:T(8,128)(2,1)S(1)}, bf16[32,2944]{1,0:T(8,128)(2,1)S(1)}, u32[]{:S(2)}, u32[]{:S(2)}) collective-permute-start(bf16[32,2944]{1,0:T(8,128)(2,1)S(1)} %pad_maximum_fusion.refs_0_), channel_id=1, source_target_pairs={{0,24},{1,25},{2,26},{3,27},{4,28},{5,29},{6,30},{7,31},{8,16},{9,... | collective-permute-start | bytes 565256 | tf_op jit(solution)/shard_map/ppermute | solution.py:48
  40.3 15.0 %collective-permute-start.11 = (bf16[32,2944]{1,0:T(8,128)(2,1)S(1)}, bf16[32,2944]{1,0:T(8,128)(2,1)S(1)}, u32[]{:S(2)}, u32[]{:S(2)}) collective-permute-start(bf16[32,2944]{1,0:T(8,128)(2,1)S(1)} %pad_maximum_fusion.refs_0_), channel_id=1, source_target_pairs={{0,16},{1,17},{2,18},{3,19},{4,20},{5,21},{6,22},{7,23},{8,24},{9,... | collective-permute-start | bytes 565256 | tf_op jit(solution)/shard_map/ppermute | solution.py:48
  40.4 14.9 %collective-permute-start.4 = (bf16[32,2944]{1,0:T(8,128)(2,1)S(1)}, bf16[32,2944]{1,0:T(8,128)(2,1)S(1)}, u32[]{:S(2)}, u32[]{:S(2)}) collective-permute-start(bf16[32,2944]{1,0:T(8,128)(2,1)S(1)} %pad_maximum_fusion.refs_0_), channel_id=1, source_target_pairs={{0,4},{1,3},{2,6},{3,1},{4,0},{5,7},{6,2},{7,5},{8,12},{9,11},{10,... | collective-permute-start | bytes 565256 | tf_op jit(solution)/shard_map/ppermute | solution.py:48
  43.3 12.1 %collective-permute-start.8 = (bf16[32,2944]{1,0:T(8,128)(2,1)S(1)}, bf16[32,2944]{1,0:T(8,128)(2,1)S(1)}, u32[]{:S(2)}, u32[]{:S(2)}) collective-permute-start(bf16[32,2944]{1,0:T(8,128)(2,1)S(1)} %shard_map.100.refs_4_), channel_id=1, source_target_pairs={{0,4},{1,3},{2,6},{3,1},{4,0},{5,7},{6,2},{7,5},{8,12},{9,11},{10,... | collective-permute-start | bytes 565256 | tf_op jit(solution)/shard_map/ppermute | solution.py:48
  43.4 12.0 %collective-permute-start.7 = (bf16[32,2944]{1,0:T(8,128)(2,1)S(1)}, bf16[32,2944]{1,0:T(8,128)(2,1)S(1)}, u32[]{:S(2)}, u32[]{:S(2)}) collective-permute-start(bf16[32,2944]{1,0:T(8,128)(2,1)S(1)} %shard_map.100.refs_4_), channel_id=1, source_target_pairs={{0,2},{1,5},{2,0},{3,7},{4,6},{5,1},{6,4},{7,3},{8,10},{9,13},{10,... | collective-permute-start | bytes 565256 | tf_op jit(solution)/shard_map/ppermute | solution.py:48
  48.6 6.8 %collective-permute-start.5 = (bf16[32,2944]{1,0:T(8,128)(2,1)S(1)}, bf16[32,2944]{1,0:T(8,128)(2,1)S(1)}, u32[]{:S(2)}, u32[]{:S(2)}) collective-permute-start(bf16[32,2944]{1,0:T(8,128)(2,1)S(1)} %collective-permute-done.3.refs_1_.refs_2_), channel_id=1, source_target_pairs={{0,4},{1,3},{2,6},{3,1},{4,0},{5,7},{6,2},{7,5},{8,12},{9,11},{10,... | collective-permute-start | bytes 565256 | tf_op jit(solution)/shard_map/ppermute | solution.py:48
  55.4 11.7 %collective-permute-start.13 = (bf16[64,2944]{1,0:T(8,128)(2,1)S(1)}, bf16[64,2944]{1,0:T(8,128)(2,1)S(1)}, u32[]{:S(2)}, u32[]{:S(2)}) collective-permute-start(bf16[64,2944]{1,0:T(8,128)(2,1)S(1)} %shard_map.102.refs_0_), channel_id=1, source_target_pairs={{0,2},{1,5},{2,0},{3,7},{4,6},{5,1},{6,4},{7,3},{8,10},{9,13},{10,... | collective-permute-start | bytes 1130504 | tf_op jit(solution)/shard_map/ppermute | solution.py:48
  56.9 20.0 %collective-permute-start.14 = (bf16[64,2944]{1,0:T(8,128)(2,1)S(1)}, bf16[64,2944]{1,0:T(8,128)(2,1)S(1)}, u32[]{:S(2)}, u32[]{:S(2)}) collective-permute-start(bf16[64,2944]{1,0:T(8,128)(2,1)S(1)} %shard_map.102.refs_0_), channel_id=1, source_target_pairs={{0,4},{1,3},{2,6},{3,1},{4,0},{5,7},{6,2},{7,5},{8,12},{9,11},{10,... | collective-permute-start | bytes 1130504 | tf_op jit(solution)/shard_map/ppermute | solution.py:48
  67.1 9.8 %collective-permute-start.15 = (bf16[64,2944]{1,0:T(8,128)(2,1)S(1)}, bf16[64,2944]{1,0:T(8,128)(2,1)S(1)}, u32[]{:S(2)}, u32[]{:S(2)}) collective-permute-start(bf16[64,2944]{1,0:T(8,128)(2,1)S(1)} %collective-permute-done.13.refs_1_), channel_id=1, source_target_pairs={{0,4},{1,3},{2,6},{3,1},{4,0},{5,7},{6,2},{7,5},{8,12},{9,11},{10,... | collective-permute-start | bytes 1130504 | tf_op jit(solution)/shard_map/ppermute | solution.py:48
  67.1 9.6 %collective-permute-start.9 = (bf16[32,2944]{1,0:T(8,128)(2,1)S(1)}, bf16[32,2944]{1,0:T(8,128)(2,1)S(1)}, u32[]{:S(2)}, u32[]{:S(2)}) collective-permute-start(bf16[32,2944]{1,0:T(8,128)(2,1)S(1)} %collective-permute-done.7.refs_5_.refs_4_), channel_id=1, source_target_pairs={{0,4},{1,3},{2,6},{3,1},{4,0},{5,7},{6,2},{7,5},{8,12},{9,11},{10,... | collective-permute-start | bytes 565256 | tf_op jit(solution)/shard_map/ppermute | solution.py:48
  108.7 14.3 %collective-permute-start.17 = (bf16[256,2944]{1,0:T(8,128)(2,1)}, bf16[256,2944]{1,0:T(8,128)(2,1)S(1)}, u32[]{:S(2)}, u32[]{:S(2)}) collective-permute-start(bf16[256,2944]{1,0:T(8,128)(2,1)} %get-tuple-element.26), channel_id=1, source_target_pairs={{0,1},{1,0},{2,3},{3,2},{4,5},{5,4},{6,7},{7,6},{8,9},{9,8},{10,11... | collective-permute-start | bytes 4521992 | tf_op jit(solution)/shard_map/ppermute | solution.py:48
  113.8 7.7 %collective-permute-start.22 = (bf16[64,2944]{1,0:T(8,128)(2,1)S(1)}, bf16[64,2944]{1,0:T(8,128)(2,1)S(1)}, u32[]{:S(2)}, u32[]{:S(2)}) collective-permute-start(bf16[64,2944]{1,0:T(8,128)(2,1)S(1)} %get-tuple-element.36), channel_id=1, source_target_pairs={{0,4},{1,3},{2,6},{3,1},{4,0},{5,7},{6,2},{7,5},{8,12},{9,11},{10,... | collective-permute-start | bytes 1130504 | tf_op jit(solution)/shard_map/ppermute | solution.py:48
  113.8 15.4 %collective-permute-start.21 = (bf16[64,2944]{1,0:T(8,128)(2,1)S(1)}, bf16[64,2944]{1,0:T(8,128)(2,1)S(1)}, u32[]{:S(2)}, u32[]{:S(2)}) collective-permute-start(bf16[64,2944]{1,0:T(8,128)(2,1)S(1)} %get-tuple-element.34), channel_id=1, source_target_pairs={{0,4},{1,3},{2,6},{3,1},{4,0},{5,7},{6,2},{7,5},{8,12},{9,11},{10,... | collective-permute-start | bytes 1130504 | tf_op jit(solution)/shard_map/ppermute | solution.py:48
  121.5 7.7 %collective-permute-start.23 = (bf16[32,2944]{1,0:T(8,128)(2,1)S(1)}, bf16[32,2944]{1,0:T(8,128)(2,1)S(1)}, u32[]{:S(2)}, u32[]{:S(2)}) collective-permute-start(bf16[32,2944]{1,0:T(8,128)(2,1)S(1)} %get-tuple-element.38), channel_id=1, source_target_pairs={{0,2},{1,5},{2,0},{3,7},{4,6},{5,1},{6,4},{7,3},{8,10},{9,13},{10,... | collective-permute-start | bytes 565256 | tf_op jit(solution)/shard_map/ppermute | solution.py:48
  123.3 13.8 %collective-permute-start.19 = (bf16[64,2944]{1,0:T(8,128)(2,1)S(1)}, bf16[64,2944]{1,0:T(8,128)(2,1)S(1)}, u32[]{:S(2)}, u32[]{:S(2)}) collective-permute-start(bf16[64,2944]{1,0:T(8,128)(2,1)S(1)} %get-tuple-element.30), channel_id=1, source_target_pairs={{0,4},{1,3},{2,6},{3,1},{4,0},{5,7},{6,2},{7,5},{8,12},{9,11},{10,... | collective-permute-start | bytes 1130504 | tf_op jit(solution)/shard_map/ppermute | solution.py:48
  129.4 7.7 %collective-permute-start.24 = (bf16[32,2944]{1,0:T(8,128)(2,1)S(1)}, bf16[32,2944]{1,0:T(8,128)(2,1)S(1)}, u32[]{:S(2)}, u32[]{:S(2)}) collective-permute-start(bf16[32,2944]{1,0:T(8,128)(2,1)S(1)} %get-tuple-element.40), channel_id=1, source_target_pairs={{0,2},{1,5},{2,0},{3,7},{4,6},{5,1},{6,4},{7,3},{8,10},{9,13},{10,... | collective-permute-start | bytes 565256 | tf_op jit(solution)/shard_map/ppermute | solution.py:48
  130.8 7.5 %collective-permute-start.25 = (bf16[32,2944]{1,0:T(8,128)(2,1)S(1)}, bf16[32,2944]{1,0:T(8,128)(2,1)S(1)}, u32[]{:S(2)}, u32[]{:S(2)}) collective-permute-start(bf16[32,2944]{1,0:T(8,128)(2,1)S(1)} %shard_map.108.refs_2_), channel_id=1, source_target_pairs={{0,24},{1,25},{2,26},{3,27},{4,28},{5,29},{6,30},{7,31},{8,16},{9,... | collective-permute-start | bytes 565256 | tf_op jit(solution)/shard_map/ppermute | solution.py:48
  133.5 10.6 %collective-permute-start.18 = (bf16[64,2944]{1,0:T(8,128)(2,1)S(1)}, bf16[64,2944]{1,0:T(8,128)(2,1)S(1)}, u32[]{:S(2)}, u32[]{:S(2)}) collective-permute-start(bf16[64,2944]{1,0:T(8,128)(2,1)S(1)} %get-tuple-element.28), channel_id=1, source_target_pairs={{0,4},{1,3},{2,6},{3,1},{4,0},{5,7},{6,2},{7,5},{8,12},{9,11},{10,... | collective-permute-start | bytes 1130504 | tf_op jit(solution)/shard_map/ppermute | solution.py:48
  138.4 5.6 %collective-permute-start.26 = (bf16[32,2944]{1,0:T(8,128)(2,1)S(1)}, bf16[32,2944]{1,0:T(8,128)(2,1)S(1)}, u32[]{:S(2)}, u32[]{:S(2)}) collective-permute-start(bf16[32,2944]{1,0:T(8,128)(2,1)S(1)} %get-tuple-element.42), channel_id=1, source_target_pairs={{0,2},{1,5},{2,0},{3,7},{4,6},{5,1},{6,4},{7,3},{8,10},{9,13},{10,... | collective-permute-start | bytes 565256 | tf_op jit(solution)/shard_map/ppermute | solution.py:48
  139.1 13.6 %collective-permute-start.27 = (bf16[32,2944]{1,0:T(8,128)(2,1)S(1)}, bf16[32,2944]{1,0:T(8,128)(2,1)S(1)}, u32[]{:S(2)}, u32[]{:S(2)}) collective-permute-start(bf16[32,2944]{1,0:T(8,128)(2,1)S(1)} %shard_map.110.refs_2_), channel_id=1, source_target_pairs={{0,16},{1,17},{2,18},{3,19},{4,20},{5,21},{6,22},{7,23},{8,24},{9,... | collective-permute-start | bytes 565256 | tf_op jit(solution)/shard_map/ppermute | solution.py:48
  (14 other events, 76.3 us)

commit v4 on v3

--- a/solution.py
+++ b/solution.py
@@ -84,22 +84,22 @@
     )(*parts, *after)
 
 
-def fold_kernel(count, outs_n, *refs):
+def fold_kernel(count, outs_n, first_row, *refs):
     terms, outs = refs[:count], refs[len(refs) - outs_n :]
     rows = outs[0].shape[0]
     for place, out_ref in enumerate(outs):
-        cut = slice(place * rows, (place + 1) * rows)
+        cut = slice(first_row + place * rows, first_row + (place + 1) * rows)
         total = terms[0][cut, :].astype(jnp.float32)
         for term in terms[1:]:
             total = total + term[cut, :].astype(jnp.float32)
         out_ref[...] = total.astype(out_ref.dtype)
 
 
-def fold(terms, kinds, after=()):
+def fold(terms, kinds, after=(), piece=0, pieces=1):
     rows, width = terms[0].shape
-    rows = rows // len(kinds)
+    rows = rows // (pieces * len(kinds))
     return pl.pallas_call(
-        functools.partial(fold_kernel, len(terms), len(kinds)),
+        functools.partial(fold_kernel, len(terms), len(kinds), piece * len(kinds) * rows),
         in_specs=[pl.BlockSpec(memory_space=pltpu.VMEM)] * len(terms)
         + [pl.BlockSpec(memory_space=pl.ANY)] * len(after),
         out_shape=[jax.ShapeDtypeStruct((rows, width), kind) for kind in kinds],
@@ -247,7 +247,7 @@
             pltpu.SemaphoreType.DMA((2,)),
             pltpu.SemaphoreType.DMA((groups,)),
         ],
-        compiler_params=pltpu.CompilerParams(vmem_limit_bytes=52 << 20),
+        compiler_params=pltpu.CompilerParams(vmem_limit_bytes=46 << 20),
         cost_estimate=pl.CostEstimate(
             flops=6 * slots_n * groups * width * units,
             bytes_accessed=6 * experts * width * units,
@@ -367,26 +367,35 @@
     for piece in first_pieces[1:]:
         spread_a.append(spread(join([piece], 1, spread_a[0][1:2]), inner))
     forwards = [piece for pieces in spread_a for piece in pieces[1 : size + 1]]
-    pieces_b = spread(join(second_pieces, 1, forwards + spread_a[0][size + 1 :]), inner)
+    pair = join(second_pieces, 1, forwards + spread_a[0][size + 1 :])
     mine_a = join([piece for pieces in spread_a for piece in pieces])
+    near = [swap(pair, other * even, other * odd) for other in range(1, size)]
+    passed = [join([piece], 1, [mine_a]) for piece in near]
+    pieces_b = [pair] + near
+    for other in range(1, last_size):
+        pieces_b += [
+            swap(piece, other * last_even, other * last_odd) for piece in [pair] + passed
+        ]
     mine_b = join(pieces_b, half)
     tokens = [mine_a, swap(mine_a, 1, 1), mine_b, swap(mine_b, 1, 1)]
 
     first = (lax.axis_index("seq") * experts_dev).astype(jnp.int32).reshape(1)
     sums = run_experts(first, tokens, gate_up, down, block_rows, capacity)
 
-    kinds = ([jnp.float32] + [jnp.bfloat16] * (last_size - 1)) * half
+    last_kinds = [jnp.float32] + [jnp.bfloat16] * (last_size - 1)
     inner_kinds = [jnp.float32] + [jnp.bfloat16] * (size - 1)
-    parts = [fold([kept, swap(handed, 1, 1)], kinds) for kept, handed in (sums[:2], sums[2:])]
+    whole = [[kept, swap(handed, 1, 1)] for kept, handed in (sums[:2], sums[2:])]
     arrived = []
     after = []
-    for offset in list(range(slow - 1, 1, -1)) + [1, 0]:
-        place = offset % half * last_size
-        terms = send_parts(parts[offset // half][place : place + last_size], last_even, last_odd)
-        terms = send_parts(fold(terms, inner_kinds, after + arrived[-2:-1]), even, odd)
+    for offset in list(range(slow - 1, 0, -1)) + [0]:
+        after = after + ([] if offset else arrived[:1])
+        terms = fold(whole[offset // half], last_kinds, after, offset % half, half)
+        terms = send_parts(terms, last_even, last_odd)
+        after = terms[1:]
+        behind = [] if offset else arrived[1:2]
+        terms = send_parts(fold(terms, inner_kinds, behind), even, odd)
         if offset:
-            after = list(fold(terms, [jnp.bfloat16]))
-            arrived.append(along(after[0], offset))
+            arrived.append(along(fold(terms, [jnp.bfloat16])[0], offset))
         else:
             total = residual + fold(terms, [jnp.float32], arrived[-1:])[0][:, :MODEL_WIDTH]
     for part in arrived:

time: 161 us -> 156 us (0.969)
  waiting for transfers between devices: 74.7 us -> 64.3 us
  starting transfers between devices: 37.6 us -> 45.1 us
    ppermute x29, waiting for transfers between devices: 73.2 us -> 62.8 us  [swap(): return lax.ppermute(value, ('seq', 'tp'), pairs)]
    ppermute x29, starting transfers between devices: 32.7 us -> 40.2 us  [swap(): return lax.ppermute(value, ('seq', 'tp'), pairs)]
where the time goes in v4:
time: 156 us
  waiting for transfers between devices  64.3 us (41%)
  starting transfers between devices  45.1 us (29%)
  Pallas kernels  27.2 us (17%)
  matrix products  13.6 us (9%)
  other arithmetic  2.91 us (2%)
  local copies, waits for them, and re-layouts  2.79 us (2%)
    ppermute x29, waiting for transfers between devices, swap(): return lax.ppermute(value, ('seq', 'tp'), pairs)  62.8 us
    ppermute x29, starting transfers between devices, swap(): return lax.ppermute(value, ('seq', 'tp'), pairs)  40.2 us
    pallas_call x1, Pallas kernels, run_experts(): pl.pallas_call(functools.partial(expert_kernel, (groups, block_rows, capa...  25.8 us
    ppermute x1, starting transfers between devices, from_behind(): lax.ppermute(value, axis, [(source, source + steps) for source in range(f...  4.87 us
    dot_general x1, matrix products, local(): jnp.einsum('td,dhc->thc', normed, w_qkv, preferred_element_type=jnp.float32)  4.79 us
    dot_general x1, matrix products, local(): terms = jnp.dot(attended, w_out, preferred_element_type=jnp.float32)  4.78 us
  transfers between devices with their start and end apart: 30, of which 20 were waited for; matrix products, arithmetic and copies ran while one was open for 1% of the time, Pallas kernels for 1%

profile of v4, /device:TPU:0, one launch (start us, length us, event | category | flops | bytes accessed | tf_op | source)
XLA Modules:
  0.0 156.3 jit_solution(12502652264258931536)
XLA Ops:
  1.5 4.8 %fusion.9 = bf16[128,2,640]{2,0,1:T(8,128)(2,1)S(1)} fusion(bf16[2880,2,640]{2,1,0:T(2,128)(2,1)} %param.12, bf16[128,2880]{0,1:T(8,128)(2,1)} %param.10, f32[2880]{0:T(1024)} %param.11, f32[128]{0:T(128)S(1)} %add_rsqrt_fusion.1), kind=kOutput, calls=%fused_computation.14 | convolution fusion | flops 945356800 | bytes 8449792 | tf_op jit(solution)/shard_map/td,dhc->thc/dot_general | solution.py:298
  6.6 4.9 %collective-permute-start = (bf16[128,2,128]{0,2,1:T(8,128)(2,1)S(1)}, bf16[128,2,128]{0,2,1:T(8,128)(2,1)S(1)}, u32[]{:S(2)}, u32[]{:S(2)}) collective-permute-start(bf16[128,2,128]{0,2,1:T(8,128)(2,1)S(1)} %pad_maximum_fusion.1), channel_id=1, source_target_pairs={{0,4},{4,8},{8,12},{12,16},{16,20},{20,24},{24,28},{1,5},{5,9},{9,... | collective-permute-start | bytes 196616 | tf_op jit(solution)/shard_map/ppermute | solution.py:25
  13.4 2.1 %fusion.57 = (f32[2,8,128]{2,1,0:T(8,128)S(1)}, f32[2,8,128,256]{2,3,1,0:T(8,128)}) fusion(pred[128,256]{0,1:T(8,128)(4,1)S(1)} %fusion.35, bf16[128,2,10,64]{0,3,2,1:T(8,128)(2,1)S(1)} %bitcast.64, bf16[128,2,64]{0,2,1:T(8,128)(2,1)S(1)} %get-tuple-element.48, bf16[128,2,64]{0,2,1:T(8,128)(2,1)S(1)} %get-tuple-element.50), kind=kOutput, calls=%fused_computation.74 | convolution fusion | flops 69337344 | bytes 2465792 | tf_op jit(solution)/shard_map/sub | solution.py:272
  18.2 4.8 %fusion.3 = f32[2,2,32,2880]{3,2,1,0:T(8,128)S(1)} fusion(bf16[2,2,32,1024]{3,2,1,0:T(8,128)(2,1)S(1)} %dot_general.17, bf16[1024,2880]{0,1:T(8,128)(2,1)} %param.14), kind=kOutput, calls=%fused_computation.3 | convolution fusion | flops 754974720 | bytes 7634944 | tf_op jit(solution)/shard_map/dot_general | solution.py:328
  27.8 4.8 %collective-permute-done.2 = bf16[32,2880]{1,0:T(8,128)(2,1)S(1)} collective-permute-done((bf16[32,2880]{1,0:T(8,128)(2,1)S(1)}, bf16[32,2880]{1,0:T(8,128)(2,1)S(1)}, u32[]{:S(2)}, u32[]{:S(2)}) %collective-permute-start.2) | collective-permute-done | bytes 184352 | tf_op jit(solution)/shard_map/ppermute | solution.py:48
  33.0 3.3 %collective-permute-start.6 = (bf16[32,2944]{1,0:T(8,128)(2,1)S(1)}, bf16[32,2944]{1,0:T(8,128)(2,1)S(1)}, u32[]{:S(2)}, u32[]{:S(2)}) collective-permute-start(bf16[32,2944]{1,0:T(8,128)(2,1)S(1)} %pad_maximum_fusion.refs_0_), channel_id=1, source_target_pairs={{0,8},{1,9},{2,10},{3,11},{4,12},{5,13},{6,14},{7,15},{8,0},{9,1},... | collective-permute-start | bytes 565256 | tf_op jit(solution)/shard_map/ppermute | solution.py:48
  37.9 2.5 %collective-permute-start.12 = (bf16[32,2944]{1,0:T(8,128)(2,1)S(1)}, bf16[32,2944]{1,0:T(8,128)(2,1)S(1)}, u32[]{:S(2)}, u32[]{:S(2)}) collective-permute-start(bf16[32,2944]{1,0:T(8,128)(2,1)S(1)} %pad_maximum_fusion.refs_0_), channel_id=1, source_target_pairs={{0,24},{1,25},{2,26},{3,27},{4,28},{5,29},{6,30},{7,31},{8,16},{9,... | collective-permute-start | bytes 565256 | tf_op jit(solution)/shard_map/ppermute | solution.py:48
  41.3 2.0 %collective-permute-done.3.refs_1_.refs_2_ = bf16[32,2944]{1,0:T(8,128)(2,1)S(1)} collective-permute-done((bf16[32,2944]{1,0:T(8,128)(2,1)S(1)}, bf16[32,2944]{1,0:T(8,128)(2,1)S(1)}, u32[]{:S(2)}, u32[]{:S(2)}) %collective-permute-start.3) | collective-permute-done | bytes 188448 | tf_op jit(solution)/shard_map/ppermute | solution.py:48
  45.0 3.7 %collective-permute-done.12.refs_1_ = bf16[32,2944]{1,0:T(8,128)(2,1)S(1)} collective-permute-done((bf16[32,2944]{1,0:T(8,128)(2,1)S(1)}, bf16[32,2944]{1,0:T(8,128)(2,1)S(1)}, u32[]{:S(2)}, u32[]{:S(2)}) %collective-permute-start.12) | collective-permute-done | bytes 188448 | tf_op jit(solution)/shard_map/ppermute | solution.py:48
  49.2 6.1 %collective-permute-done.11.refs_0_ = bf16[32,2944]{1,0:T(8,128)(2,1)S(1)} collective-permute-done((bf16[32,2944]{1,0:T(8,128)(2,1)S(1)}, bf16[32,2944]{1,0:T(8,128)(2,1)S(1)}, u32[]{:S(2)}, u32[]{:S(2)}) %collective-permute-start.11) | collective-permute-done | bytes 188448 | tf_op jit(solution)/shard_map/ppermute | solution.py:48
  59.0 3.6 %collective-permute-done.9.refs_7_ = bf16[32,2944]{1,0:T(8,128)(2,1)S(1)} collective-permute-done((bf16[32,2944]{1,0:T(8,128)(2,1)S(1)}, bf16[32,2944]{1,0:T(8,128)(2,1)S(1)}, u32[]{:S(2)}, u32[]{:S(2)}) %collective-permute-start.9) | collective-permute-done | bytes 188448 | tf_op jit(solution)/shard_map/ppermute | solution.py:48
  62.6 4.5 %collective-permute-done.13.refs_0_.refs_1_ = bf16[64,2944]{1,0:T(8,128)(2,1)S(1)} collective-permute-done((bf16[64,2944]{1,0:T(8,128)(2,1)S(1)}, bf16[64,2944]{1,0:T(8,128)(2,1)S(1)}, u32[]{:S(2)}, u32[]{:S(2)}) %collective-permute-start.13) | collective-permute-done | bytes 376864 | tf_op jit(solution)/shard_map/ppermute | solution.py:48
  68.7 6.2 %collective-permute-done.15.refs_3_ = bf16[64,2944]{1,0:T(8,128)(2,1)S(1)} collective-permute-done((bf16[64,2944]{1,0:T(8,128)(2,1)S(1)}, bf16[64,2944]{1,0:T(8,128)(2,1)S(1)}, u32[]{:S(2)}, u32[]{:S(2)}) %collective-permute-start.15) | collective-permute-done | bytes 376864 | tf_op jit(solution)/shard_map/ppermute | solution.py:48
  75.0 3.4 %collective-permute-done.16.refs_3_ = bf16[256,2944]{1,0:T(8,128)(2,1)} collective-permute-done((bf16[256,2944]{1,0:T(8,128)(2,1)S(1)}, bf16[256,2944]{1,0:T(8,128)(2,1)}, u32[]{:S(2)}, u32[]{:S(2)}) %collective-permute-start.16) | collective-permute-done | bytes 1507360 | tf_op jit(solution)/shard_map/ppermute | solution.py:48
  78.5 25.8 %shard_map.105 = (bf16[256,2944]{1,0:T(8,128)(2,1)S(1)}, bf16[256,2944]{1,0:T(8,128)(2,1)S(1)}, bf16[256,2944]{1,0:T(8,128)(2,1)S(1)}, bf16[256,2944]{1,0:T(8,128)(2,1)S(1)}) custom-call(s32[1]{0:T(128)} %bitcast.16.first_ref, bf16[256,2944]{1,0:T(8,128)(2,1)S(1)} %shard_map.101.refs_1_.refs_0_, bf16[256,2944]{1,0:T(8,128)(2,1)} %collective-permute-done.10.refs_1_, ...), custom_call_target="tpu_custom_call" | custom-call | flops 12740198400 | bytes 49766400 | tf_op jit(solution)/shard_map/pallas_call | solution.py:233
  104.9 2.8 %collective-permute-done.18.refs_1_ = bf16[256,2944]{1,0:T(8,128)(2,1)S(1)} collective-permute-done((bf16[256,2944]{1,0:T(8,128)(2,1)S(1)}, bf16[256,2944]{1,0:T(8,128)(2,1)S(1)}, u32[]{:S(2)}, u32[]{:S(2)}) %collective-permute-start.18) | collective-permute-done | bytes 1507360 | tf_op jit(solution)/shard_map/ppermute | solution.py:48
  109.4 6.2 %collective-permute-done.19.refs_2_.refs_1_ = bf16[64,2944]{1,0:T(8,128)(2,1)S(1)} collective-permute-done((bf16[64,2944]{1,0:T(8,128)(2,1)S(1)}, bf16[64,2944]{1,0:T(8,128)(2,1)S(1)}, u32[]{:S(2)}, u32[]{:S(2)}) %collective-permute-start.19) | collective-permute-done | bytes 376864 | tf_op jit(solution)/shard_map/ppermute | solution.py:48
  118.8 6.1 %collective-permute-done.20.refs_2_.refs_1_ = bf16[64,2944]{1,0:T(8,128)(2,1)S(1)} collective-permute-done((bf16[64,2944]{1,0:T(8,128)(2,1)S(1)}, bf16[64,2944]{1,0:T(8,128)(2,1)S(1)}, u32[]{:S(2)}, u32[]{:S(2)}) %collective-permute-start.20) | collective-permute-done | bytes 376864 | tf_op jit(solution)/shard_map/ppermute | solution.py:48
  126.7 2.7 %collective-permute-start.23 = (bf16[32,2944]{1,0:T(8,128)(2,1)S(1)}, bf16[32,2944]{1,0:T(8,128)(2,1)S(1)}, u32[]{:S(2)}, u32[]{:S(2)}) collective-permute-start(bf16[32,2944]{1,0:T(8,128)(2,1)S(1)} %shard_map.110), channel_id=1, source_target_pairs={{0,24},{1,25},{2,26},{3,27},{4,28},{5,29},{6,30},{7,31},{8,16},{9,... | collective-permute-start | bytes 565256 | tf_op jit(solution)/shard_map/ppermute | solution.py:48
  130.1 4.2 %collective-permute-done.23.refs_3_ = bf16[32,2944]{1,0:T(8,128)(2,1)S(1)} collective-permute-done((bf16[32,2944]{1,0:T(8,128)(2,1)S(1)}, bf16[32,2944]{1,0:T(8,128)(2,1)S(1)}, u32[]{:S(2)}, u32[]{:S(2)}) %collective-permute-start.23) | collective-permute-done | bytes 188448 | tf_op jit(solution)/shard_map/ppermute | solution.py:48
  137.3 4.7 %collective-permute-start.26 = (bf16[32,2944]{1,0:T(8,128)(2,1)S(1)}, bf16[32,2944]{1,0:T(8,128)(2,1)S(1)}, u32[]{:S(2)}, u32[]{:S(2)}) collective-permute-start(bf16[32,2944]{1,0:T(8,128)(2,1)S(1)} %shard_map.113), channel_id=1, source_target_pairs={{0,16},{1,17},{2,18},{3,19},{4,20},{5,21},{6,22},{7,23},{8,24},{9,... | collective-permute-start | bytes 565256 | tf_op jit(solution)/shard_map/ppermute | solution.py:48
  142.5 5.2 %collective-permute-start.29 = (bf16[32,2944]{1,0:T(8,128)(2,1)S(1)}, bf16[32,2944]{1,0:T(8,128)(2,1)S(1)}, u32[]{:S(2)}, u32[]{:S(2)}) collective-permute-start(bf16[32,2944]{1,0:T(8,128)(2,1)S(1)} %shard_map.116), channel_id=1, source_target_pairs={{0,8},{1,9},{2,10},{3,11},{4,12},{5,13},{6,14},{7,15},{8,0},{9,1},... | collective-permute-start | bytes 565256 | tf_op jit(solution)/shard_map/ppermute | solution.py:48
  147.8 1.9 %collective-permute-done.26.refs_2_ = bf16[32,2944]{1,0:T(8,128)(2,1)S(1)} collective-permute-done((bf16[32,2944]{1,0:T(8,128)(2,1)S(1)}, bf16[32,2944]{1,0:T(8,128)(2,1)S(1)}, u32[]{:S(2)}, u32[]{:S(2)}) %collective-permute-start.26) | collective-permute-done | bytes 188448 | tf_op jit(solution)/shard_map/ppermute | solution.py:48
  151.7 3.7 %collective-permute-done.27.refs_1_ = bf16[32,2944]{1,0:T(8,128)(2,1)S(1)} collective-permute-done((bf16[32,2944]{1,0:T(8,128)(2,1)S(1)}, bf16[32,2944]{1,0:T(8,128)(2,1)S(1)}, u32[]{:S(2)}, u32[]{:S(2)}) %collective-permute-start.27) | collective-permute-done | bytes 188448 | tf_op jit(solution)/shard_map/ppermute | solution.py:48
  (98 shorter events, 35.9 us)
Async XLA Ops:
  6.6 6.8 %collective-permute-start = (bf16[128,2,128]{0,2,1:T(8,128)(2,1)S(1)}, bf16[128,2,128]{0,2,1:T(8,128)(2,1)S(1)}, u32[]{:S(2)}, u32[]{:S(2)}) collective-permute-start(bf16[128,2,128]{0,2,1:T(8,128)(2,1)S(1)} %pad_maximum_fusion.1), channel_id=1, source_target_pairs={{0,4},{4,8},{8,12},{12,16},{16,20},{20,24},{24,28},{1,5},{5,9},{9,... | collective-permute-start | bytes 196616 | tf_op jit(solution)/shard_map/ppermute | solution.py:25
  25.8 6.8 %collective-permute-start.2 = (bf16[32,2880]{1,0:T(8,128)(2,1)S(1)}, bf16[32,2880]{1,0:T(8,128)(2,1)S(1)}, u32[]{:S(2)}, u32[]{:S(2)}) collective-permute-start(bf16[32,2880]{1,0:T(8,128)(2,1)S(1)} %fusion.32), channel_id=1, source_target_pairs={{0,2},{1,3},{2,0},{3,1},{4,6},{5,7},{6,4},{7,5},{8,10},{9,11},{10,... | collective-permute-start | bytes 552968 | tf_op jit(solution)/shard_map/ppermute | solution.py:48
  33.0 8.3 %collective-permute-start.6 = (bf16[32,2944]{1,0:T(8,128)(2,1)S(1)}, bf16[32,2944]{1,0:T(8,128)(2,1)S(1)}, u32[]{:S(2)}, u32[]{:S(2)}) collective-permute-start(bf16[32,2944]{1,0:T(8,128)(2,1)S(1)} %pad_maximum_fusion.refs_0_), channel_id=1, source_target_pairs={{0,8},{1,9},{2,10},{3,11},{4,12},{5,13},{6,14},{7,15},{8,0},{9,1},... | collective-permute-start | bytes 565256 | tf_op jit(solution)/shard_map/ppermute | solution.py:48
  36.4 6.9 %collective-permute-start.3 = (bf16[32,2944]{1,0:T(8,128)(2,1)S(1)}, bf16[32,2944]{1,0:T(8,128)(2,1)S(1)}, u32[]{:S(2)}, u32[]{:S(2)}) collective-permute-start(bf16[32,2944]{1,0:T(8,128)(2,1)S(1)} %pad_maximum_fusion.refs_0_), channel_id=1, source_target_pairs={{0,2},{1,5},{2,0},{3,7},{4,6},{5,1},{6,4},{7,3},{8,10},{9,13},{10,... | collective-permute-start | bytes 565256 | tf_op jit(solution)/shard_map/ppermute | solution.py:48
  37.9 10.8 %collective-permute-start.12 = (bf16[32,2944]{1,0:T(8,128)(2,1)S(1)}, bf16[32,2944]{1,0:T(8,128)(2,1)S(1)}, u32[]{:S(2)}, u32[]{:S(2)}) collective-permute-start(bf16[32,2944]{1,0:T(8,128)(2,1)S(1)} %pad_maximum_fusion.refs_0_), channel_id=1, source_target_pairs={{0,24},{1,25},{2,26},{3,27},{4,28},{5,29},{6,30},{7,31},{8,16},{9,... | collective-permute-start | bytes 565256 | tf_op jit(solution)/shard_map/ppermute | solution.py:48
  40.3 15.0 %collective-permute-start.11 = (bf16[32,2944]{1,0:T(8,128)(2,1)S(1)}, bf16[32,2944]{1,0:T(8,128)(2,1)S(1)}, u32[]{:S(2)}, u32[]{:S(2)}) collective-permute-start(bf16[32,2944]{1,0:T(8,128)(2,1)S(1)} %pad_maximum_fusion.refs_0_), channel_id=1, source_target_pairs={{0,16},{1,17},{2,18},{3,19},{4,20},{5,21},{6,22},{7,23},{8,24},{9,... | collective-permute-start | bytes 565256 | tf_op jit(solution)/shard_map/ppermute | solution.py:48
  40.4 14.9 %collective-permute-start.4 = (bf16[32,2944]{1,0:T(8,128)(2,1)S(1)}, bf16[32,2944]{1,0:T(8,128)(2,1)S(1)}, u32[]{:S(2)}, u32[]{:S(2)}) collective-permute-start(bf16[32,2944]{1,0:T(8,128)(2,1)S(1)} %pad_maximum_fusion.refs_0_), channel_id=1, source_target_pairs={{0,4},{1,3},{2,6},{3,1},{4,0},{5,7},{6,2},{7,5},{8,12},{9,11},{10,... | collective-permute-start | bytes 565256 | tf_op jit(solution)/shard_map/ppermute | solution.py:48
  43.3 12.1 %collective-permute-start.8 = (bf16[32,2944]{1,0:T(8,128)(2,1)S(1)}, bf16[32,2944]{1,0:T(8,128)(2,1)S(1)}, u32[]{:S(2)}, u32[]{:S(2)}) collective-permute-start(bf16[32,2944]{1,0:T(8,128)(2,1)S(1)} %shard_map.100.refs_4_), channel_id=1, source_target_pairs={{0,4},{1,3},{2,6},{3,1},{4,0},{5,7},{6,2},{7,5},{8,12},{9,11},{10,... | collective-permute-start | bytes 565256 | tf_op jit(solution)/shard_map/ppermute | solution.py:48
  43.4 12.0 %collective-permute-start.7 = (bf16[32,2944]{1,0:T(8,128)(2,1)S(1)}, bf16[32,2944]{1,0:T(8,128)(2,1)S(1)}, u32[]{:S(2)}, u32[]{:S(2)}) collective-permute-start(bf16[32,2944]{1,0:T(8,128)(2,1)S(1)} %shard_map.100.refs_4_), channel_id=1, source_target_pairs={{0,2},{1,5},{2,0},{3,7},{4,6},{5,1},{6,4},{7,3},{8,10},{9,13},{10,... | collective-permute-start | bytes 565256 | tf_op jit(solution)/shard_map/ppermute | solution.py:48
  48.6 6.8 %collective-permute-start.5 = (bf16[32,2944]{1,0:T(8,128)(2,1)S(1)}, bf16[32,2944]{1,0:T(8,128)(2,1)S(1)}, u32[]{:S(2)}, u32[]{:S(2)}) collective-permute-start(bf16[32,2944]{1,0:T(8,128)(2,1)S(1)} %collective-permute-done.3.refs_1_.refs_2_), channel_id=1, source_target_pairs={{0,4},{1,3},{2,6},{3,1},{4,0},{5,7},{6,2},{7,5},{8,12},{9,11},{10,... | collective-permute-start | bytes 565256 | tf_op jit(solution)/shard_map/ppermute | solution.py:48
  55.4 11.7 %collective-permute-start.13 = (bf16[64,2944]{1,0:T(8,128)(2,1)S(1)}, bf16[64,2944]{1,0:T(8,128)(2,1)S(1)}, u32[]{:S(2)}, u32[]{:S(2)}) collective-permute-start(bf16[64,2944]{1,0:T(8,128)(2,1)S(1)} %shard_map.102.refs_0_), channel_id=1, source_target_pairs={{0,2},{1,5},{2,0},{3,7},{4,6},{5,1},{6,4},{7,3},{8,10},{9,13},{10,... | collective-permute-start | bytes 1130504 | tf_op jit(solution)/shard_map/ppermute | solution.py:48
  58.3 10.3 %collective-permute-start.14 = (bf16[64,2944]{1,0:T(8,128)(2,1)S(1)}, bf16[64,2944]{1,0:T(8,128)(2,1)S(1)}, u32[]{:S(2)}, u32[]{:S(2)}) collective-permute-start(bf16[64,2944]{1,0:T(8,128)(2,1)S(1)} %shard_map.102.refs_0_), channel_id=1, source_target_pairs={{0,4},{1,3},{2,6},{3,1},{4,0},{5,7},{6,2},{7,5},{8,12},{9,11},{10,... | collective-permute-start | bytes 1130504 | tf_op jit(solution)/shard_map/ppermute | solution.py:48
  67.2 7.7 %collective-permute-start.15 = (bf16[64,2944]{1,0:T(8,128)(2,1)S(1)}, bf16[64,2944]{1,0:T(8,128)(2,1)S(1)}, u32[]{:S(2)}, u32[]{:S(2)}) collective-permute-start(bf16[64,2944]{1,0:T(8,128)(2,1)S(1)} %shard_map.103), channel_id=1, source_target_pairs={{0,4},{1,3},{2,6},{3,1},{4,0},{5,7},{6,2},{7,5},{8,12},{9,11},{10,... | collective-permute-start | bytes 1130504 | tf_op jit(solution)/shard_map/ppermute | solution.py:48
  68.7 6.4 %collective-permute-start.10 = (bf16[256,2944]{1,0:T(8,128)(2,1)S(1)}, bf16[256,2944]{1,0:T(8,128)(2,1)}, u32[]{:S(2)}, u32[]{:S(2)}) collective-permute-start(bf16[256,2944]{1,0:T(8,128)(2,1)S(1)} %shard_map.101.refs_1_.refs_0_), channel_id=1, source_target_pairs={{0,1},{1,0},{2,3},{3,2},{4,5},{5,4},{6,7},{7,6},{8,9},{9,8},{10,11... | collective-permute-start | bytes 4521992 | tf_op jit(solution)/shard_map/ppermute | solution.py:48
  104.5 14.3 %collective-permute-start.17 = (bf16[256,2944]{1,0:T(8,128)(2,1)S(1)}, bf16[256,2944]{1,0:T(8,128)(2,1)S(1)}, u32[]{:S(2)}, u32[]{:S(2)}) collective-permute-start(bf16[256,2944]{1,0:T(8,128)(2,1)S(1)} %get-tuple-element.26), channel_id=1, source_target_pairs={{0,1},{1,0},{2,3},{3,2},{4,5},{5,4},{6,7},{7,6},{8,9},{9,8},{10,11... | collective-permute-start | bytes 4521992 | tf_op jit(solution)/shard_map/ppermute | solution.py:48
  107.9 7.7 %collective-permute-start.19 = (bf16[64,2944]{1,0:T(8,128)(2,1)S(1)}, bf16[64,2944]{1,0:T(8,128)(2,1)S(1)}, u32[]{:S(2)}, u32[]{:S(2)}) collective-permute-start(bf16[64,2944]{1,0:T(8,128)(2,1)S(1)} %get-tuple-element.29), channel_id=1, source_target_pairs={{0,4},{1,3},{2,6},{3,1},{4,0},{5,7},{6,2},{7,5},{8,12},{9,11},{10,... | collective-permute-start | bytes 1130504 | tf_op jit(solution)/shard_map/ppermute | solution.py:48
  115.7 9.3 %collective-permute-start.20 = (bf16[64,2944]{1,0:T(8,128)(2,1)S(1)}, bf16[64,2944]{1,0:T(8,128)(2,1)S(1)}, u32[]{:S(2)}, u32[]{:S(2)}) collective-permute-start(bf16[64,2944]{1,0:T(8,128)(2,1)S(1)} %get-tuple-element.30), channel_id=1, source_target_pairs={{0,4},{1,3},{2,6},{3,1},{4,0},{5,7},{6,2},{7,5},{8,12},{9,11},{10,... | collective-permute-start | bytes 1130504 | tf_op jit(solution)/shard_map/ppermute | solution.py:48
  117.3 9.4 %collective-permute-start.22 = (bf16[32,2944]{1,0:T(8,128)(2,1)S(1)}, bf16[32,2944]{1,0:T(8,128)(2,1)S(1)}, u32[]{:S(2)}, u32[]{:S(2)}) collective-permute-start(bf16[32,2944]{1,0:T(8,128)(2,1)S(1)} %get-tuple-element.34), channel_id=1, source_target_pairs={{0,2},{1,5},{2,0},{3,7},{4,6},{5,1},{6,4},{7,3},{8,10},{9,13},{10,... | collective-permute-start | bytes 565256 | tf_op jit(solution)/shard_map/ppermute | solution.py:48
  125.1 10.2 %collective-permute-start.21 = (bf16[64,2944]{1,0:T(8,128)(2,1)S(1)}, bf16[64,2944]{1,0:T(8,128)(2,1)S(1)}, u32[]{:S(2)}, u32[]{:S(2)}) collective-permute-start(bf16[64,2944]{1,0:T(8,128)(2,1)S(1)} %get-tuple-element.31), channel_id=1, source_target_pairs={{0,4},{1,3},{2,6},{3,1},{4,0},{5,7},{6,2},{7,5},{8,12},{9,11},{10,... | collective-permute-start | bytes 1130504 | tf_op jit(solution)/shard_map/ppermute | solution.py:48
  126.7 7.5 %collective-permute-start.23 = (bf16[32,2944]{1,0:T(8,128)(2,1)S(1)}, bf16[32,2944]{1,0:T(8,128)(2,1)S(1)}, u32[]{:S(2)}, u32[]{:S(2)}) collective-permute-start(bf16[32,2944]{1,0:T(8,128)(2,1)S(1)} %shard_map.110), channel_id=1, source_target_pairs={{0,24},{1,25},{2,26},{3,27},{4,28},{5,29},{6,30},{7,31},{8,16},{9,... | collective-permute-start | bytes 565256 | tf_op jit(solution)/shard_map/ppermute | solution.py:48
  129.5 7.7 %collective-permute-start.25 = (bf16[32,2944]{1,0:T(8,128)(2,1)S(1)}, bf16[32,2944]{1,0:T(8,128)(2,1)S(1)}, u32[]{:S(2)}, u32[]{:S(2)}) collective-permute-start(bf16[32,2944]{1,0:T(8,128)(2,1)S(1)} %get-tuple-element.39), channel_id=1, source_target_pairs={{0,2},{1,5},{2,0},{3,7},{4,6},{5,1},{6,4},{7,3},{8,10},{9,13},{10,... | collective-permute-start | bytes 565256 | tf_op jit(solution)/shard_map/ppermute | solution.py:48
  135.5 14.3 %collective-permute-start.24 = (bf16[64,2944]{1,0:T(8,128)(2,1)S(1)}, bf16[64,2944]{1,0:T(8,128)(2,1)S(1)}, u32[]{:S(2)}, u32[]{:S(2)}) collective-permute-start(bf16[64,2944]{1,0:T(8,128)(2,1)S(1)} %get-tuple-element.36), channel_id=1, source_target_pairs={{0,4},{1,3},{2,6},{3,1},{4,0},{5,7},{6,2},{7,5},{8,12},{9,11},{10,... | collective-permute-start | bytes 1130504 | tf_op jit(solution)/shard_map/ppermute | solution.py:48
  137.3 12.4 %collective-permute-start.26 = (bf16[32,2944]{1,0:T(8,128)(2,1)S(1)}, bf16[32,2944]{1,0:T(8,128)(2,1)S(1)}, u32[]{:S(2)}, u32[]{:S(2)}) collective-permute-start(bf16[32,2944]{1,0:T(8,128)(2,1)S(1)} %shard_map.113), channel_id=1, source_target_pairs={{0,16},{1,17},{2,18},{3,19},{4,20},{5,21},{6,22},{7,23},{8,24},{9,... | collective-permute-start | bytes 565256 | tf_op jit(solution)/shard_map/ppermute | solution.py:48
  142.5 9.2 %collective-permute-start.29 = (bf16[32,2944]{1,0:T(8,128)(2,1)S(1)}, bf16[32,2944]{1,0:T(8,128)(2,1)S(1)}, u32[]{:S(2)}, u32[]{:S(2)}) collective-permute-start(bf16[32,2944]{1,0:T(8,128)(2,1)S(1)} %shard_map.116), channel_id=1, source_target_pairs={{0,8},{1,9},{2,10},{3,11},{4,12},{5,13},{6,14},{7,15},{8,0},{9,1},... | collective-permute-start | bytes 565256 | tf_op jit(solution)/shard_map/ppermute | solution.py:48
  (12 other events, 67.3 us)

commit v5 on v4

--- a/solution.py
+++ b/solution.py
@@ -392,12 +392,11 @@
         terms = fold(whole[offset // half], last_kinds, after, offset % half, half)
         terms = send_parts(terms, last_even, last_odd)
         after = terms[1:]
-        behind = [] if offset else arrived[1:2]
-        terms = send_parts(fold(terms, inner_kinds, behind), even, odd)
+        terms = send_parts(fold(terms, inner_kinds), even, odd)
         if offset:
             arrived.append(along(fold(terms, [jnp.bfloat16])[0], offset))
         else:
-            total = residual + fold(terms, [jnp.float32], arrived[-1:])[0][:, :MODEL_WIDTH]
+            total = residual + fold(terms, [jnp.float32], arrived[1:])[0][:, :MODEL_WIDTH]
     for part in arrived:
         total = total + part[:, :MODEL_WIDTH].astype(jnp.float32)
     return total.astype(jnp.bfloat16)

time: 156 us -> 159 us (1.019)
  waiting for transfers between devices: 64.3 us -> 68.2 us
    ppermute x29, waiting for transfers between devices: 62.8 us -> 66.7 us  [swap(): return lax.ppermute(value, ('seq', 'tp'), pairs)]
  transfers between devices with their start and end apart: 30 -> 30, of which waited for: 20 -> 18; matrix products, arithmetic and copies ran while one was open for 1% -> 1% of each run, Pallas kernels for 1% -> 1%
where the time goes in v5:
time: 159 us
  waiting for transfers between devices  68.2 us (43%)
  starting transfers between devices  43.6 us (27%)
  Pallas kernels  27.2 us (17%)
  matrix products  13.6 us (9%)
  other arithmetic  2.91 us (2%)
  local copies, waits for them, and re-layouts  2.79 us (2%)
    ppermute x29, waiting for transfers between devices, swap(): return lax.ppermute(value, ('seq', 'tp'), pairs)  66.7 us
    ppermute x29, starting transfers between devices, swap(): return lax.ppermute(value, ('seq', 'tp'), pairs)  38.7 us
    pallas_call x1, Pallas kernels, run_experts(): pl.pallas_call(functools.partial(expert_kernel, (groups, block_rows, capa...  25.8 us
    ppermute x1, starting transfers between devices, from_behind(): lax.ppermute(value, axis, [(source, source + steps) for source in range(f...  4.87 us
    dot_general x1, matrix products, local(): jnp.einsum('td,dhc->thc', normed, w_qkv, preferred_element_type=jnp.float32)  4.79 us
    dot_general x1, matrix products, local(): terms = jnp.dot(attended, w_out, preferred_element_type=jnp.float32)  4.78 us
  transfers between devices with their start and end apart: 30, of which 18 were waited for; matrix products, arithmetic and copies ran while one was open for 1% of the time, Pallas kernels for 1%

profile of v5, /device:TPU:0, one launch (start us, length us, event | category | flops | bytes accessed | tf_op | source)
XLA Modules:
  0.0 158.6 jit_solution(8894815005225969116)
XLA Ops:
  1.5 4.8 %fusion.9 = bf16[128,2,640]{2,0,1:T(8,128)(2,1)S(1)} fusion(bf16[2880,2,640]{2,1,0:T(2,128)(2,1)} %param.12, bf16[128,2880]{0,1:T(8,128)(2,1)} %param.10, f32[2880]{0:T(1024)} %param.11, f32[128]{0:T(128)S(1)} %add_rsqrt_fusion.1), kind=kOutput, calls=%fused_computation.14 | convolution fusion | flops 945356800 | bytes 8449792 | tf_op jit(solution)/shard_map/td,dhc->thc/dot_general | solution.py:298
  6.6 4.9 %collective-permute-start = (bf16[128,2,128]{0,2,1:T(8,128)(2,1)S(1)}, bf16[128,2,128]{0,2,1:T(8,128)(2,1)S(1)}, u32[]{:S(2)}, u32[]{:S(2)}) collective-permute-start(bf16[128,2,128]{0,2,1:T(8,128)(2,1)S(1)} %pad_maximum_fusion.1), channel_id=1, source_target_pairs={{0,4},{4,8},{8,12},{12,16},{16,20},{20,24},{24,28},{1,5},{5,9},{9,... | collective-permute-start | bytes 196616 | tf_op jit(solution)/shard_map/ppermute | solution.py:25
  13.4 2.1 %fusion.57 = (f32[2,8,128]{2,1,0:T(8,128)S(1)}, f32[2,8,128,256]{2,3,1,0:T(8,128)}) fusion(pred[128,256]{0,1:T(8,128)(4,1)S(1)} %fusion.35, bf16[128,2,10,64]{0,3,2,1:T(8,128)(2,1)S(1)} %bitcast.64, bf16[128,2,64]{0,2,1:T(8,128)(2,1)S(1)} %get-tuple-element.48, bf16[128,2,64]{0,2,1:T(8,128)(2,1)S(1)} %get-tuple-element.50), kind=kOutput, calls=%fused_computation.74 | convolution fusion | flops 69337344 | bytes 2465792 | tf_op jit(solution)/shard_map/sub | solution.py:272
  15.5 1.9 %fusion.12 = bf16[128,2,8,64]{0,3,2,1:T(8,128)(2,1)S(1)} fusion(f32[2,8,128,256]{2,3,1,0:T(8,128)} %get-tuple-element.55, f32[2,8,128]{2,1,0:T(8,128)S(1)} %get-tuple-element.54, bf16[128,2,64]{0,2,1:T(8,128)(2,1)S(1)} %get-tuple-element.47, bf16[128,2,64]{0,2,1:T(8,128)(2,1)S(1)} %get-tuple-element.49), kind=kOutput, calls=%fused_computation.16 | convolution fusion | flops 68419584 | bytes 2433024 | tf_op jit(solution)/shard_map/hgqk,khc->qhgc/dot_general | solution.py:274
  18.2 4.8 %fusion.3 = f32[2,2,32,2880]{3,2,1,0:T(8,128)S(1)} fusion(bf16[2,2,32,1024]{3,2,1,0:T(8,128)(2,1)S(1)} %dot_general.17, bf16[1024,2880]{0,1:T(8,128)(2,1)} %param.14), kind=kOutput, calls=%fused_computation.3 | convolution fusion | flops 754974720 | bytes 7634944 | tf_op jit(solution)/shard_map/dot_general | solution.py:328
  27.8 4.8 %collective-permute-done.2 = bf16[32,2880]{1,0:T(8,128)(2,1)S(1)} collective-permute-done((bf16[32,2880]{1,0:T(8,128)(2,1)S(1)}, bf16[32,2880]{1,0:T(8,128)(2,1)S(1)}, u32[]{:S(2)}, u32[]{:S(2)}) %collective-permute-start.2) | collective-permute-done | bytes 184352 | tf_op jit(solution)/shard_map/ppermute | solution.py:48
  33.0 3.3 %collective-permute-start.6 = (bf16[32,2944]{1,0:T(8,128)(2,1)S(1)}, bf16[32,2944]{1,0:T(8,128)(2,1)S(1)}, u32[]{:S(2)}, u32[]{:S(2)}) collective-permute-start(bf16[32,2944]{1,0:T(8,128)(2,1)S(1)} %pad_maximum_fusion.refs_0_), channel_id=1, source_target_pairs={{0,8},{1,9},{2,10},{3,11},{4,12},{5,13},{6,14},{7,15},{8,0},{9,1},... | collective-permute-start | bytes 565256 | tf_op jit(solution)/shard_map/ppermute | solution.py:48
  37.9 2.5 %collective-permute-start.12 = (bf16[32,2944]{1,0:T(8,128)(2,1)S(1)}, bf16[32,2944]{1,0:T(8,128)(2,1)S(1)}, u32[]{:S(2)}, u32[]{:S(2)}) collective-permute-start(bf16[32,2944]{1,0:T(8,128)(2,1)S(1)} %pad_maximum_fusion.refs_0_), channel_id=1, source_target_pairs={{0,24},{1,25},{2,26},{3,27},{4,28},{5,29},{6,30},{7,31},{8,16},{9,... | collective-permute-start | bytes 565256 | tf_op jit(solution)/shard_map/ppermute | solution.py:48
  41.3 2.0 %collective-permute-done.3.refs_1_.refs_2_ = bf16[32,2944]{1,0:T(8,128)(2,1)S(1)} collective-permute-done((bf16[32,2944]{1,0:T(8,128)(2,1)S(1)}, bf16[32,2944]{1,0:T(8,128)(2,1)S(1)}, u32[]{:S(2)}, u32[]{:S(2)}) %collective-permute-start.3) | collective-permute-done | bytes 188448 | tf_op jit(solution)/shard_map/ppermute | solution.py:48
  45.0 3.7 %collective-permute-done.12.refs_1_ = bf16[32,2944]{1,0:T(8,128)(2,1)S(1)} collective-permute-done((bf16[32,2944]{1,0:T(8,128)(2,1)S(1)}, bf16[32,2944]{1,0:T(8,128)(2,1)S(1)}, u32[]{:S(2)}, u32[]{:S(2)}) %collective-permute-start.12) | collective-permute-done | bytes 188448 | tf_op jit(solution)/shard_map/ppermute | solution.py:48
  49.2 6.1 %collective-permute-done.11.refs_0_ = bf16[32,2944]{1,0:T(8,128)(2,1)S(1)} collective-permute-done((bf16[32,2944]{1,0:T(8,128)(2,1)S(1)}, bf16[32,2944]{1,0:T(8,128)(2,1)S(1)}, u32[]{:S(2)}, u32[]{:S(2)}) %collective-permute-start.11) | collective-permute-done | bytes 188448 | tf_op jit(solution)/shard_map/ppermute | solution.py:48
  59.0 3.6 %collective-permute-done.9.refs_7_ = bf16[32,2944]{1,0:T(8,128)(2,1)S(1)} collective-permute-done((bf16[32,2944]{1,0:T(8,128)(2,1)S(1)}, bf16[32,2944]{1,0:T(8,128)(2,1)S(1)}, u32[]{:S(2)}, u32[]{:S(2)}) %collective-permute-start.9) | collective-permute-done | bytes 188448 | tf_op jit(solution)/shard_map/ppermute | solution.py:48
  62.6 4.5 %collective-permute-done.13.refs_0_.refs_1_ = bf16[64,2944]{1,0:T(8,128)(2,1)S(1)} collective-permute-done((bf16[64,2944]{1,0:T(8,128)(2,1)S(1)}, bf16[64,2944]{1,0:T(8,128)(2,1)S(1)}, u32[]{:S(2)}, u32[]{:S(2)}) %collective-permute-start.13) | collective-permute-done | bytes 376864 | tf_op jit(solution)/shard_map/ppermute | solution.py:48
  68.7 6.2 %collective-permute-done.15.refs_3_ = bf16[64,2944]{1,0:T(8,128)(2,1)S(1)} collective-permute-done((bf16[64,2944]{1,0:T(8,128)(2,1)S(1)}, bf16[64,2944]{1,0:T(8,128)(2,1)S(1)}, u32[]{:S(2)}, u32[]{:S(2)}) %collective-permute-start.15) | collective-permute-done | bytes 376864 | tf_op jit(solution)/shard_map/ppermute | solution.py:48
  75.0 3.4 %collective-permute-done.16.refs_3_ = bf16[256,2944]{1,0:T(8,128)(2,1)} collective-permute-done((bf16[256,2944]{1,0:T(8,128)(2,1)S(1)}, bf16[256,2944]{1,0:T(8,128)(2,1)}, u32[]{:S(2)}, u32[]{:S(2)}) %collective-permute-start.16) | collective-permute-done | bytes 1507360 | tf_op jit(solution)/shard_map/ppermute | solution.py:48
  78.5 25.8 %shard_map.105 = (bf16[256,2944]{1,0:T(8,128)(2,1)S(1)}, bf16[256,2944]{1,0:T(8,128)(2,1)S(1)}, bf16[256,2944]{1,0:T(8,128)(2,1)S(1)}, bf16[256,2944]{1,0:T(8,128)(2,1)S(1)}) custom-call(s32[1]{0:T(128)} %bitcast.16.first_ref, bf16[256,2944]{1,0:T(8,128)(2,1)S(1)} %shard_map.101.refs_1_.refs_0_, bf16[256,2944]{1,0:T(8,128)(2,1)} %collective-permute-done.10.refs_1_, ...), custom_call_target="tpu_custom_call" | custom-call | flops 12740198400 | bytes 49766400 | tf_op jit(solution)/shard_map/pallas_call | solution.py:233
  104.9 2.8 %collective-permute-done.18.refs_1_ = bf16[256,2944]{1,0:T(8,128)(2,1)S(1)} collective-permute-done((bf16[256,2944]{1,0:T(8,128)(2,1)S(1)}, bf16[256,2944]{1,0:T(8,128)(2,1)S(1)}, u32[]{:S(2)}, u32[]{:S(2)}) %collective-permute-start.18) | collective-permute-done | bytes 1507360 | tf_op jit(solution)/shard_map/ppermute | solution.py:48
  109.4 6.2 %collective-permute-done.19.refs_2_.refs_1_ = bf16[64,2944]{1,0:T(8,128)(2,1)S(1)} collective-permute-done((bf16[64,2944]{1,0:T(8,128)(2,1)S(1)}, bf16[64,2944]{1,0:T(8,128)(2,1)S(1)}, u32[]{:S(2)}, u32[]{:S(2)}) %collective-permute-start.19) | collective-permute-done | bytes 376864 | tf_op jit(solution)/shard_map/ppermute | solution.py:48
  118.8 6.1 %collective-permute-done.20.refs_2_.refs_1_ = bf16[64,2944]{1,0:T(8,128)(2,1)S(1)} collective-permute-done((bf16[64,2944]{1,0:T(8,128)(2,1)S(1)}, bf16[64,2944]{1,0:T(8,128)(2,1)S(1)}, u32[]{:S(2)}, u32[]{:S(2)}) %collective-permute-start.20) | collective-permute-done | bytes 376864 | tf_op jit(solution)/shard_map/ppermute | solution.py:48
  126.7 2.7 %collective-permute-start.23 = (bf16[32,2944]{1,0:T(8,128)(2,1)S(1)}, bf16[32,2944]{1,0:T(8,128)(2,1)S(1)}, u32[]{:S(2)}, u32[]{:S(2)}) collective-permute-start(bf16[32,2944]{1,0:T(8,128)(2,1)S(1)} %shard_map.110), channel_id=1, source_target_pairs={{0,24},{1,25},{2,26},{3,27},{4,28},{5,29},{6,30},{7,31},{8,16},{9,... | collective-permute-start | bytes 565256 | tf_op jit(solution)/shard_map/ppermute | solution.py:48
  129.4 4.8 %collective-permute-done.23.refs_3_ = bf16[32,2944]{1,0:T(8,128)(2,1)S(1)} collective-permute-done((bf16[32,2944]{1,0:T(8,128)(2,1)S(1)}, bf16[32,2944]{1,0:T(8,128)(2,1)S(1)}, u32[]{:S(2)}, u32[]{:S(2)}) %collective-permute-start.23) | collective-permute-done | bytes 188448 | tf_op jit(solution)/shard_map/ppermute | solution.py:48
  137.5 3.4 %collective-permute-done.26.refs_1_ = bf16[32,2944]{1,0:T(8,128)(2,1)S(1)} collective-permute-done((bf16[32,2944]{1,0:T(8,128)(2,1)S(1)}, bf16[32,2944]{1,0:T(8,128)(2,1)S(1)}, u32[]{:S(2)}, u32[]{:S(2)}) %collective-permute-start.26) | collective-permute-done | bytes 188448 | tf_op jit(solution)/shard_map/ppermute | solution.py:48
  140.9 7.8 %collective-permute-start.27 = (bf16[32,2944]{1,0:T(8,128)(2,1)S(1)}, bf16[32,2944]{1,0:T(8,128)(2,1)S(1)}, u32[]{:S(2)}, u32[]{:S(2)}) collective-permute-start(bf16[32,2944]{1,0:T(8,128)(2,1)S(1)} %shard_map.114), channel_id=1, source_target_pairs={{0,16},{1,17},{2,18},{3,19},{4,20},{5,21},{6,22},{7,23},{8,24},{9,... | collective-permute-start | bytes 565256 | tf_op jit(solution)/shard_map/ppermute | solution.py:48
  150.5 5.6 %collective-permute-done.27.refs_2_ = bf16[32,2944]{1,0:T(8,128)(2,1)S(1)} collective-permute-done((bf16[32,2944]{1,0:T(8,128)(2,1)S(1)}, bf16[32,2944]{1,0:T(8,128)(2,1)S(1)}, u32[]{:S(2)}, u32[]{:S(2)}) %collective-permute-start.27) | collective-permute-done | bytes 188448 | tf_op jit(solution)/shard_map/ppermute | solution.py:48
  (98 shorter events, 34.5 us)
Async XLA Ops:
  6.6 6.8 %collective-permute-start = (bf16[128,2,128]{0,2,1:T(8,128)(2,1)S(1)}, bf16[128,2,128]{0,2,1:T(8,128)(2,1)S(1)}, u32[]{:S(2)}, u32[]{:S(2)}) collective-permute-start(bf16[128,2,128]{0,2,1:T(8,128)(2,1)S(1)} %pad_maximum_fusion.1), channel_id=1, source_target_pairs={{0,4},{4,8},{8,12},{12,16},{16,20},{20,24},{24,28},{1,5},{5,9},{9,... | collective-permute-start | bytes 196616 | tf_op jit(solution)/shard_map/ppermute | solution.py:25
  25.8 6.8 %collective-permute-start.2 = (bf16[32,2880]{1,0:T(8,128)(2,1)S(1)}, bf16[32,2880]{1,0:T(8,128)(2,1)S(1)}, u32[]{:S(2)}, u32[]{:S(2)}) collective-permute-start(bf16[32,2880]{1,0:T(8,128)(2,1)S(1)} %fusion.32), channel_id=1, source_target_pairs={{0,2},{1,3},{2,0},{3,1},{4,6},{5,7},{6,4},{7,5},{8,10},{9,11},{10,... | collective-permute-start | bytes 552968 | tf_op jit(solution)/shard_map/ppermute | solution.py:48
  33.0 8.3 %collective-permute-start.6 = (bf16[32,2944]{1,0:T(8,128)(2,1)S(1)}, bf16[32,2944]{1,0:T(8,128)(2,1)S(1)}, u32[]{:S(2)}, u32[]{:S(2)}) collective-permute-start(bf16[32,2944]{1,0:T(8,128)(2,1)S(1)} %pad_maximum_fusion.refs_0_), channel_id=1, source_target_pairs={{0,8},{1,9},{2,10},{3,11},{4,12},{5,13},{6,14},{7,15},{8,0},{9,1},... | collective-permute-start | bytes 565256 | tf_op jit(solution)/shard_map/ppermute | solution.py:48
  36.4 6.9 %collective-permute-start.3 = (bf16[32,2944]{1,0:T(8,128)(2,1)S(1)}, bf16[32,2944]{1,0:T(8,128)(2,1)S(1)}, u32[]{:S(2)}, u32[]{:S(2)}) collective-permute-start(bf16[32,2944]{1,0:T(8,128)(2,1)S(1)} %pad_maximum_fusion.refs_0_), channel_id=1, source_target_pairs={{0,2},{1,5},{2,0},{3,7},{4,6},{5,1},{6,4},{7,3},{8,10},{9,13},{10,... | collective-permute-start | bytes 565256 | tf_op jit(solution)/shard_map/ppermute | solution.py:48
  37.9 10.8 %collective-permute-start.12 = (bf16[32,2944]{1,0:T(8,128)(2,1)S(1)}, bf16[32,2944]{1,0:T(8,128)(2,1)S(1)}, u32[]{:S(2)}, u32[]{:S(2)}) collective-permute-start(bf16[32,2944]{1,0:T(8,128)(2,1)S(1)} %pad_maximum_fusion.refs_0_), channel_id=1, source_target_pairs={{0,24},{1,25},{2,26},{3,27},{4,28},{5,29},{6,30},{7,31},{8,16},{9,... | collective-permute-start | bytes 565256 | tf_op jit(solution)/shard_map/ppermute | solution.py:48
  40.3 15.0 %collective-permute-start.11 = (bf16[32,2944]{1,0:T(8,128)(2,1)S(1)}, bf16[32,2944]{1,0:T(8,128)(2,1)S(1)}, u32[]{:S(2)}, u32[]{:S(2)}) collective-permute-start(bf16[32,2944]{1,0:T(8,128)(2,1)S(1)} %pad_maximum_fusion.refs_0_), channel_id=1, source_target_pairs={{0,16},{1,17},{2,18},{3,19},{4,20},{5,21},{6,22},{7,23},{8,24},{9,... | collective-permute-start | bytes 565256 | tf_op jit(solution)/shard_map/ppermute | solution.py:48
  40.4 14.9 %collective-permute-start.4 = (bf16[32,2944]{1,0:T(8,128)(2,1)S(1)}, bf16[32,2944]{1,0:T(8,128)(2,1)S(1)}, u32[]{:S(2)}, u32[]{:S(2)}) collective-permute-start(bf16[32,2944]{1,0:T(8,128)(2,1)S(1)} %pad_maximum_fusion.refs_0_), channel_id=1, source_target_pairs={{0,4},{1,3},{2,6},{3,1},{4,0},{5,7},{6,2},{7,5},{8,12},{9,11},{10,... | collective-permute-start | bytes 565256 | tf_op jit(solution)/shard_map/ppermute | solution.py:48
  43.3 12.1 %collective-permute-start.8 = (bf16[32,2944]{1,0:T(8,128)(2,1)S(1)}, bf16[32,2944]{1,0:T(8,128)(2,1)S(1)}, u32[]{:S(2)}, u32[]{:S(2)}) collective-permute-start(bf16[32,2944]{1,0:T(8,128)(2,1)S(1)} %shard_map.100.refs_4_), channel_id=1, source_target_pairs={{0,4},{1,3},{2,6},{3,1},{4,0},{5,7},{6,2},{7,5},{8,12},{9,11},{10,... | collective-permute-start | bytes 565256 | tf_op jit(solution)/shard_map/ppermute | solution.py:48
  43.4 12.0 %collective-permute-start.7 = (bf16[32,2944]{1,0:T(8,128)(2,1)S(1)}, bf16[32,2944]{1,0:T(8,128)(2,1)S(1)}, u32[]{:S(2)}, u32[]{:S(2)}) collective-permute-start(bf16[32,2944]{1,0:T(8,128)(2,1)S(1)} %shard_map.100.refs_4_), channel_id=1, source_target_pairs={{0,2},{1,5},{2,0},{3,7},{4,6},{5,1},{6,4},{7,3},{8,10},{9,13},{10,... | collective-permute-start | bytes 565256 | tf_op jit(solution)/shard_map/ppermute | solution.py:48
  48.6 6.8 %collective-permute-start.5 = (bf16[32,2944]{1,0:T(8,128)(2,1)S(1)}, bf16[32,2944]{1,0:T(8,128)(2,1)S(1)}, u32[]{:S(2)}, u32[]{:S(2)}) collective-permute-start(bf16[32,2944]{1,0:T(8,128)(2,1)S(1)} %collective-permute-done.3.refs_1_.refs_2_), channel_id=1, source_target_pairs={{0,4},{1,3},{2,6},{3,1},{4,0},{5,7},{6,2},{7,5},{8,12},{9,11},{10,... | collective-permute-start | bytes 565256 | tf_op jit(solution)/shard_map/ppermute | solution.py:48
  55.4 11.7 %collective-permute-start.13 = (bf16[64,2944]{1,0:T(8,128)(2,1)S(1)}, bf16[64,2944]{1,0:T(8,128)(2,1)S(1)}, u32[]{:S(2)}, u32[]{:S(2)}) collective-permute-start(bf16[64,2944]{1,0:T(8,128)(2,1)S(1)} %shard_map.102.refs_0_), channel_id=1, source_target_pairs={{0,2},{1,5},{2,0},{3,7},{4,6},{5,1},{6,4},{7,3},{8,10},{9,13},{10,... | collective-permute-start | bytes 1130504 | tf_op jit(solution)/shard_map/ppermute | solution.py:48
  58.3 10.3 %collective-permute-start.14 = (bf16[64,2944]{1,0:T(8,128)(2,1)S(1)}, bf16[64,2944]{1,0:T(8,128)(2,1)S(1)}, u32[]{:S(2)}, u32[]{:S(2)}) collective-permute-start(bf16[64,2944]{1,0:T(8,128)(2,1)S(1)} %shard_map.102.refs_0_), channel_id=1, source_target_pairs={{0,4},{1,3},{2,6},{3,1},{4,0},{5,7},{6,2},{7,5},{8,12},{9,11},{10,... | collective-permute-start | bytes 1130504 | tf_op jit(solution)/shard_map/ppermute | solution.py:48
  67.2 7.7 %collective-permute-start.15 = (bf16[64,2944]{1,0:T(8,128)(2,1)S(1)}, bf16[64,2944]{1,0:T(8,128)(2,1)S(1)}, u32[]{:S(2)}, u32[]{:S(2)}) collective-permute-start(bf16[64,2944]{1,0:T(8,128)(2,1)S(1)} %shard_map.103), channel_id=1, source_target_pairs={{0,4},{1,3},{2,6},{3,1},{4,0},{5,7},{6,2},{7,5},{8,12},{9,11},{10,... | collective-permute-start | bytes 1130504 | tf_op jit(solution)/shard_map/ppermute | solution.py:48
  104.5 14.3 %collective-permute-start.17 = (bf16[256,2944]{1,0:T(8,128)(2,1)S(1)}, bf16[256,2944]{1,0:T(8,128)(2,1)S(1)}, u32[]{:S(2)}, u32[]{:S(2)}) collective-permute-start(bf16[256,2944]{1,0:T(8,128)(2,1)S(1)} %get-tuple-element.26), channel_id=1, source_target_pairs={{0,1},{1,0},{2,3},{3,2},{4,5},{5,4},{6,7},{7,6},{8,9},{9,8},{10,11... | collective-permute-start | bytes 4521992 | tf_op jit(solution)/shard_map/ppermute | solution.py:48
  107.9 7.7 %collective-permute-start.19 = (bf16[64,2944]{1,0:T(8,128)(2,1)S(1)}, bf16[64,2944]{1,0:T(8,128)(2,1)S(1)}, u32[]{:S(2)}, u32[]{:S(2)}) collective-permute-start(bf16[64,2944]{1,0:T(8,128)(2,1)S(1)} %get-tuple-element.29), channel_id=1, source_target_pairs={{0,4},{1,3},{2,6},{3,1},{4,0},{5,7},{6,2},{7,5},{8,12},{9,11},{10,... | collective-permute-start | bytes 1130504 | tf_op jit(solution)/shard_map/ppermute | solution.py:48
  115.7 9.3 %collective-permute-start.20 = (bf16[64,2944]{1,0:T(8,128)(2,1)S(1)}, bf16[64,2944]{1,0:T(8,128)(2,1)S(1)}, u32[]{:S(2)}, u32[]{:S(2)}) collective-permute-start(bf16[64,2944]{1,0:T(8,128)(2,1)S(1)} %get-tuple-element.30), channel_id=1, source_target_pairs={{0,4},{1,3},{2,6},{3,1},{4,0},{5,7},{6,2},{7,5},{8,12},{9,11},{10,... | collective-permute-start | bytes 1130504 | tf_op jit(solution)/shard_map/ppermute | solution.py:48
  117.3 9.4 %collective-permute-start.22 = (bf16[32,2944]{1,0:T(8,128)(2,1)S(1)}, bf16[32,2944]{1,0:T(8,128)(2,1)S(1)}, u32[]{:S(2)}, u32[]{:S(2)}) collective-permute-start(bf16[32,2944]{1,0:T(8,128)(2,1)S(1)} %get-tuple-element.34), channel_id=1, source_target_pairs={{0,2},{1,5},{2,0},{3,7},{4,6},{5,1},{6,4},{7,3},{8,10},{9,13},{10,... | collective-permute-start | bytes 565256 | tf_op jit(solution)/shard_map/ppermute | solution.py:48
  125.1 9.2 %collective-permute-start.21 = (bf16[64,2944]{1,0:T(8,128)(2,1)S(1)}, bf16[64,2944]{1,0:T(8,128)(2,1)S(1)}, u32[]{:S(2)}, u32[]{:S(2)}) collective-permute-start(bf16[64,2944]{1,0:T(8,128)(2,1)S(1)} %get-tuple-element.31), channel_id=1, source_target_pairs={{0,4},{1,3},{2,6},{3,1},{4,0},{5,7},{6,2},{7,5},{8,12},{9,11},{10,... | collective-permute-start | bytes 1130504 | tf_op jit(solution)/shard_map/ppermute | solution.py:48
  126.7 7.5 %collective-permute-start.23 = (bf16[32,2944]{1,0:T(8,128)(2,1)S(1)}, bf16[32,2944]{1,0:T(8,128)(2,1)S(1)}, u32[]{:S(2)}, u32[]{:S(2)}) collective-permute-start(bf16[32,2944]{1,0:T(8,128)(2,1)S(1)} %shard_map.110), channel_id=1, source_target_pairs={{0,24},{1,25},{2,26},{3,27},{4,28},{5,29},{6,30},{7,31},{8,16},{9,... | collective-permute-start | bytes 565256 | tf_op jit(solution)/shard_map/ppermute | solution.py:48
  134.5 15.4 %collective-permute-start.24 = (bf16[64,2944]{1,0:T(8,128)(2,1)S(1)}, bf16[64,2944]{1,0:T(8,128)(2,1)S(1)}, u32[]{:S(2)}, u32[]{:S(2)}) collective-permute-start(bf16[64,2944]{1,0:T(8,128)(2,1)S(1)} %get-tuple-element.36), channel_id=1, source_target_pairs={{0,4},{1,3},{2,6},{3,1},{4,0},{5,7},{6,2},{7,5},{8,12},{9,11},{10,... | collective-permute-start | bytes 1130504 | tf_op jit(solution)/shard_map/ppermute | solution.py:48
  135.8 12.9 %collective-permute-start.28 = (bf16[32,2944]{1,0:T(8,128)(2,1)S(1)}, bf16[32,2944]{1,0:T(8,128)(2,1)S(1)}, u32[]{:S(2)}, u32[]{:S(2)}) collective-permute-start(bf16[32,2944]{1,0:T(8,128)(2,1)S(1)} %get-tuple-element.44), channel_id=1, source_target_pairs={{0,2},{1,5},{2,0},{3,7},{4,6},{5,1},{6,4},{7,3},{8,10},{9,13},{10,... | collective-permute-start | bytes 565256 | tf_op jit(solution)/shard_map/ppermute | solution.py:48
  140.9 15.1 %collective-permute-start.27 = (bf16[32,2944]{1,0:T(8,128)(2,1)S(1)}, bf16[32,2944]{1,0:T(8,128)(2,1)S(1)}, u32[]{:S(2)}, u32[]{:S(2)}) collective-permute-start(bf16[32,2944]{1,0:T(8,128)(2,1)S(1)} %shard_map.114), channel_id=1, source_target_pairs={{0,16},{1,17},{2,18},{3,19},{4,20},{5,21},{6,22},{7,23},{8,24},{9,... | collective-permute-start | bytes 565256 | tf_op jit(solution)/shard_map/ppermute | solution.py:48
  148.8 9.0 %collective-permute-start.29 = (bf16[32,2944]{1,0:T(8,128)(2,1)S(1)}, bf16[32,2944]{1,0:T(8,128)(2,1)S(1)}, u32[]{:S(2)}, u32[]{:S(2)}) collective-permute-start(bf16[32,2944]{1,0:T(8,128)(2,1)S(1)} %shard_map.116), channel_id=1, source_target_pairs={{0,8},{1,9},{2,10},{3,11},{4,12},{5,13},{6,14},{7,15},{8,0},{9,1},... | collective-permute-start | bytes 565256 | tf_op jit(solution)/shard_map/ppermute | solution.py:48
  149.9 7.9 %collective-permute-start.25 = (bf16[32,2944]{1,0:T(8,128)(2,1)S(1)}, bf16[32,2944]{1,0:T(8,128)(2,1)S(1)}, u32[]{:S(2)}, u32[]{:S(2)}) collective-permute-start(bf16[32,2944]{1,0:T(8,128)(2,1)S(1)} %get-tuple-element.38), channel_id=1, source_target_pairs={{0,2},{1,5},{2,0},{3,7},{4,6},{5,1},{6,4},{7,3},{8,10},{9,13},{10,... | collective-permute-start | bytes 565256 | tf_op jit(solution)/shard_map/ppermute | solution.py:48
  (12 other events, 68.0 us)
